TPU v7x, 32 devices: a whole 2x2x4 slice. The times are simulated.
32 devices in a mesh: dp: 8 (over z, y), tensor: 4 (over x, core).
Axes of the slice: x: 2, y: 2, z: 4, core: 2. Of those that a mesh axis runs over, the one named last changes fastest.
Arguments:
- tokens: bfloat16 [4096, 1536], P('dp'), may hold values from -6 to 6
- lengths: int32 [2], replicated, may hold values from 1537 to 2048, as said below
- norm_conv: float32 [1536], replicated, may hold values from 0.5 to 1.5
- conv_in: bfloat16 [1536, 3, 1536], P(None, None, 'tensor'), may hold values from -0.15625 to 0.15625
- conv_kernel: bfloat16 [3, 1536], P(None, 'tensor'), may hold values from -3.5 to 3.5
- conv_out: bfloat16 [1536, 1536], P('tensor'), may hold values from -0.15625 to 0.15625
- norm_mlp_one: float32 [1536], replicated, may hold values from 0.5 to 1.5
- gate_up_one: bfloat16 [1536, 2, 6912], P(None, None, 'tensor'), may hold values from -0.15625 to 0.15625
- down_one: bfloat16 [6912, 1536], P('tensor'), may hold values from -0.078125 to 0.078125
- norm_attn: float32 [1536], replicated, may hold values from 0.5 to 1.5
- query_weight: bfloat16 [1536, 1536], P(None, 'tensor'), may hold values from -0.15625 to 0.15625
- kv_weight: bfloat16 [1536, 2, 512], P(None, None, 'tensor'), may hold values from -0.15625 to 0.15625
- query_gain: float32 [64], replicated, may hold values from 0.5 to 1.5
- key_gain: float32 [64], replicated, may hold values from 0.5 to 1.5
- attn_out: bfloat16 [1536, 1536], P('tensor'), may hold values from -0.625 to 0.625
- norm_mlp_two: float32 [1536], replicated, may hold values from 0.5 to 1.5
- gate_up_two: bfloat16 [1536, 2, 6912], P(None, None, 'tensor'), may hold values from -0.15625 to 0.15625
- down_two: bfloat16 [6912, 1536], P('tensor'), may hold values from -0.078125 to 0.078125
- cotangent: bfloat16 [4096, 1536], P('dp'), may hold values from -6 to 6
Outputs:
- output: bfloat16 [4096, 1536], P('dp')
- grad_tokens: float32 [4096, 1536], P('dp')
- grad_norm_conv: float32 [1536], replicated
- grad_conv_in: float32 [1536, 3, 1536], P('dp', None, 'tensor')
- grad_conv_kernel: float32 [3, 1536], P(None, 'tensor')
- grad_conv_out: float32 [1536, 1536], P('tensor', 'dp')
- grad_norm_mlp_one: float32 [1536], replicated
- grad_gate_up_one: float32 [1536, 2, 6912], P('dp', None, 'tensor')
- grad_down_one: float32 [6912, 1536], P('tensor', 'dp')
- grad_norm_attn: float32 [1536], replicated
- grad_query_weight: float32 [1536, 1536], P('dp', 'tensor')
- grad_kv_weight: float32 [1536, 2, 512], P('dp', None, 'tensor')
- grad_query_gain: float32 [64], replicated
- grad_key_gain: float32 [64], replicated
- grad_attn_out: float32 [1536, 1536], P('tensor', 'dp')
- grad_norm_mlp_two: float32 [1536], replicated
- grad_gate_up_two: float32 [1536, 2, 6912], P('dp', None, 'tensor')
- grad_down_two: float32 [6912, 1536], P('tensor', 'dp')
Inputs may be any that keep to these rules, and one draw needn't show every extreme that they name: `lengths`: some sequence has exactly 2048 live tokens.
All inputs are finite; a program needn't handle non-finite values.
Results may differ from a plain program's by a relative error of at most 0.025.
Values may be sent and summed in bfloat16 or wider, within the bound.
A program may use at most 320 MiB of HBM per device.

v0:
```python
import jax
import jax.numpy as jnp
from jax import lax
from jax.sharding import PartitionSpec as P

HEAD = 64
KW = 3
SPAN = 4
GROUP = 3


EPSILON = 1e-05
THETA = 1000000.0


def shifted(block, axis, distance):
    devices = range(lax.axis_size(axis))
    route = [(i - distance, i) for i in devices if i - distance in devices]
    return lax.ppermute(block, axis, route)


def matmul(left, right):
    return jnp.dot(left, right, preferred_element_type=jnp.float32)


def outer_sum(left, right):
    return lax.dot_general(
        left, right, (((0,), (0,)), ((), ())), preferred_element_type=jnp.float32
    )


def inner_back(left, right):
    return lax.dot_general(
        left, right, (((1,), (1,)), ((), ())), preferred_element_type=jnp.float32
    )


def normalize(values, gain):
    inverse = lax.rsqrt(jnp.mean(values * values, axis=-1, keepdims=True) + EPSILON)
    return (values * inverse * gain, inverse)


def normalize_back(values, inverse, gain, grad_result):
    weighted = grad_result * gain
    grad_gain = jnp.sum(grad_result * values * inverse, axis=tuple(range(values.ndim - 1)))
    inner = jnp.mean(weighted * values, axis=-1, keepdims=True)
    grad_values = inverse * (weighted - values * inverse * inverse * inner)
    return (grad_values, grad_gain)


def rotate(values, cosine, sine_table):
    middle = values.shape[-1] // 2
    turned = jnp.concatenate([-values[..., middle:], values[..., :middle]], axis=-1)
    return values * cosine + turned * sine_table


def rotate_back(grads, cosine, sine_table):
    middle = grads.shape[-1] // 2
    scaled = grads * sine_table
    turned = jnp.concatenate([scaled[..., middle:], -scaled[..., :middle]], axis=-1)
    return grads * cosine + turned


def tensor_total(partial_value):
    return lax.psum(partial_value, "tensor")


def mlp_forward(hidden, gain, gate_up, down):
    normed, inverse = normalize(hidden, gain)
    normed_b = normed.astype(jnp.bfloat16)
    units = gate_up.shape[2]
    joined = matmul(normed_b, gate_up.reshape(gate_up.shape[0], 2 * units))
    gate = joined[:, :units]
    upward = joined[:, units:]
    active_b = (jax.nn.silu(gate) * upward).astype(jnp.bfloat16)
    return (tensor_total(matmul(active_b, down)), (normed_b, inverse, gate, upward, active_b))


def mlp_backward(hidden, gain, gate_up, down, kept, grad_result):
    normed_b, inverse, gate, upward, active_b = kept
    units = gate_up.shape[2]
    grad_b = grad_result.astype(jnp.bfloat16)
    grad_down = outer_sum(active_b, grad_b)
    grad_active = inner_back(grad_b, down)
    sigma = jax.nn.sigmoid(gate)
    grad_gate = grad_active * upward * sigma * (1.0 + gate * (1.0 - sigma))
    grad_upward = grad_active * gate * sigma
    grad_joined = jnp.concatenate([grad_gate, grad_upward], axis=1).astype(jnp.bfloat16)
    flat_weight = gate_up.reshape(gate_up.shape[0], 2 * units)
    grad_gate_up = outer_sum(normed_b, grad_joined).reshape(gate_up.shape)
    grad_normed = tensor_total(inner_back(grad_joined, flat_weight))
    grad_inner, grad_gain = normalize_back(hidden, inverse, gain, grad_normed)
    return (grad_result + grad_inner, grad_gain, grad_gate_up, grad_down)


def score_block(grouped, near_keys, positions, key_positions, key_ok, factor):
    raw = (
        jnp.einsum("qkgd,skd->kgqs", grouped, near_keys, preferred_element_type=jnp.float32)
        * factor
    )
    allowed = (key_positions[None, :] <= positions[:, None]) & key_ok[None, :]
    return jnp.where(allowed, raw, -1e30)


def local(
    tokens,
    lengths,
    norm_conv,
    conv_in,
    conv_kernel,
    conv_out,
    norm_mlp_one,
    gate_up_one,
    down_one,
    norm_attn,
    query_weight,
    kv_weight,
    query_gain,
    key_gain,
    attn_out,
    norm_mlp_two,
    gate_up_two,
    down_two,
    cotangent,
):
    row_count = tokens.shape[0]
    width = tokens.shape[1]
    channels = conv_out.shape[0]
    local_heads = query_weight.shape[1] // HEAD
    local_kv = kv_weight.shape[2] // HEAD
    device = lax.axis_index("dp")
    sequence = device // SPAN
    place_index = device % SPAN
    length = lengths[sequence]
    positions = place_index * row_count + jnp.arange(row_count, dtype=jnp.int32)
    is_valid = positions < length
    grad_result = cotangent.astype(jnp.float32) * is_valid[:, None].astype(jnp.float32)
    frequency = THETA ** (-2.0 * jnp.arange(HEAD // 2, dtype=jnp.float32) / HEAD)
    angles = positions.astype(jnp.float32)[:, None] * frequency[None, :]
    angles = jnp.concatenate([angles, angles], axis=-1)[:, None, :]
    cosine = jnp.cos(angles)
    sine_table = jnp.sin(angles)
    factor = HEAD ** (-0.5)
    kernel = conv_kernel.astype(jnp.float32)
    rim_rows = KW - 1
    inputs = tokens.astype(jnp.float32)
    normed_conv, inverse_conv = normalize(inputs, norm_conv)
    normed_conv_b = normed_conv.astype(jnp.bfloat16)
    weight_in = conv_in.reshape(width, 3 * channels)
    projected = matmul(normed_conv_b, weight_in)
    before = projected[:, :channels]
    after = projected[:, channels : 2 * channels]
    signal = projected[:, 2 * channels :]
    mixed = before * signal
    rim_in = shifted(mixed[row_count - rim_rows :], "dp", 1)
    rim_in = jnp.where(place_index > 0, rim_in, 0.0)
    padded = jnp.concatenate([rim_in, mixed], axis=0)
    convolved = kernel[0] * padded[0:row_count]
    for offset in range(1, KW):
        convolved = convolved + kernel[offset] * padded[offset : offset + row_count]
    gated_b = (after * convolved).astype(jnp.bfloat16)
    hidden_one = inputs + tensor_total(matmul(gated_b, conv_out))
    mlp_one_out, kept_one = mlp_forward(hidden_one, norm_mlp_one, gate_up_one, down_one)
    hidden_two = hidden_one + mlp_one_out
    normed_attn, inverse_attn = normalize(hidden_two, norm_attn)
    normed_attn_b = normed_attn.astype(jnp.bfloat16)
    query_raw = matmul(normed_attn_b, query_weight).reshape(row_count, local_heads, HEAD)
    kv_flat = kv_weight.reshape(width, 2 * local_kv * HEAD)
    joined = matmul(normed_attn_b, kv_flat)
    key_raw = joined[:, : local_kv * HEAD].reshape(row_count, local_kv, HEAD)
    value_rows = (
        joined[:, local_kv * HEAD :].reshape(row_count, local_kv, HEAD).astype(jnp.bfloat16)
    )
    query_norm, query_inverse = normalize(query_raw, query_gain)
    key_norm, key_inverse = normalize(key_raw, key_gain)
    query_rot = rotate(query_norm, cosine, sine_table).astype(jnp.bfloat16)
    key_rot = rotate(key_norm, cosine, sine_table).astype(jnp.bfloat16)
    grouped = query_rot.reshape(row_count, local_kv, GROUP, HEAD)
    stacked = jnp.stack([key_rot, value_rows])
    pieces = [stacked]
    for distance in range(1, SPAN):
        pieces.append(shifted(stacked, "dp", distance))
    nearby = jnp.concatenate(pieces, axis=1)
    key_positions = jnp.concatenate([positions - distance * row_count for distance in range(SPAN)])
    key_ok = (key_positions >= 0) & (key_positions < length)
    near_keys = nearby[0]
    near_values = nearby[1]
    scores = score_block(grouped, near_keys, positions, key_positions, key_ok, factor)
    peak = jnp.max(scores, axis=-1, keepdims=True)
    expo = jnp.exp(scores - peak)
    total = jnp.sum(expo, axis=-1, keepdims=True)
    log_total = peak + jnp.log(total)
    weights_b = (expo / total).astype(jnp.bfloat16)
    attended = jnp.einsum(
        "kgqs,skd->qkgd", weights_b, near_values, preferred_element_type=jnp.float32
    )
    attended_b = attended.reshape(row_count, local_heads * HEAD).astype(jnp.bfloat16)
    hidden_three = hidden_two + tensor_total(matmul(attended_b, attn_out))
    mlp_two_out, kept_two = mlp_forward(hidden_three, norm_mlp_two, gate_up_two, down_two)
    output = (hidden_three + mlp_two_out).astype(jnp.bfloat16)
    grad_three, grad_norm_mlp_two, grad_gate_up_two, grad_down_two = mlp_backward(
        hidden_three, norm_mlp_two, gate_up_two, down_two, kept_two, grad_result
    )
    grad_branch = grad_three.astype(jnp.bfloat16)
    grad_attn_out = outer_sum(attended_b, grad_branch)
    grad_attended = (
        inner_back(grad_branch, attn_out)
        .astype(jnp.bfloat16)
        .reshape(row_count, local_kv, GROUP, HEAD)
    )
    scores = score_block(grouped, near_keys, positions, key_positions, key_ok, factor)
    probs = jnp.exp(scores - log_total)
    probs_b = probs.astype(jnp.bfloat16)
    grad_probs = jnp.einsum(
        "qkgd,skd->kgqs", grad_attended, near_values, preferred_element_type=jnp.float32
    )
    delta = jnp.sum(probs * grad_probs, axis=-1, keepdims=True)
    grad_scores = (probs * (grad_probs - delta) * factor).astype(jnp.bfloat16)
    grad_query = jnp.einsum(
        "kgqs,skd->qkgd", grad_scores, near_keys, preferred_element_type=jnp.float32
    ).reshape(row_count, local_heads, HEAD)
    grad_keys_near = jnp.einsum(
        "kgqs,qkgd->skd", grad_scores, grouped, preferred_element_type=jnp.float32
    )
    grad_values_near = jnp.einsum(
        "kgqs,qkgd->skd", probs_b, grad_attended, preferred_element_type=jnp.float32
    )
    grad_nearby = jnp.stack([grad_keys_near, grad_values_near])
    owned = grad_nearby[:, :row_count]
    for distance in range(1, SPAN):
        owned = owned + shifted(
            grad_nearby[:, distance * row_count : (distance + 1) * row_count], "dp", -distance
        )
    grad_query_raw, part_query_gain = normalize_back(
        query_raw, query_inverse, query_gain, rotate_back(grad_query, cosine, sine_table)
    )
    grad_key_raw, part_key_gain = normalize_back(
        key_raw, key_inverse, key_gain, rotate_back(owned[0], cosine, sine_table)
    )
    grad_query_b = grad_query_raw.reshape(row_count, local_heads * HEAD).astype(jnp.bfloat16)
    grad_joined_b = jnp.concatenate(
        [
            grad_key_raw.reshape(row_count, local_kv * HEAD),
            owned[1].reshape(row_count, local_kv * HEAD),
        ],
        axis=1,
    ).astype(jnp.bfloat16)
    grad_query_weight = outer_sum(normed_attn_b, grad_query_b)
    grad_kv_weight = outer_sum(normed_attn_b, grad_joined_b).reshape(width, 2, local_kv * HEAD)
    partial_normed = inner_back(grad_query_b, query_weight) + inner_back(grad_joined_b, kv_flat)
    grad_normed, grad_query_gain, grad_key_gain = lax.psum(
        (partial_normed, part_query_gain, part_key_gain), "tensor"
    )
    grad_inner, grad_norm_attn = normalize_back(hidden_two, inverse_attn, norm_attn, grad_normed)
    grad_two = grad_three + grad_inner
    grad_one, grad_norm_mlp_one, grad_gate_up_one, grad_down_one = mlp_backward(
        hidden_one, norm_mlp_one, gate_up_one, down_one, kept_one, grad_two
    )
    grad_branch_one = grad_one.astype(jnp.bfloat16)
    grad_conv_out = outer_sum(gated_b, grad_branch_one)
    grad_gated = inner_back(grad_branch_one, conv_out)
    grad_after = grad_gated * convolved
    grad_convolved = grad_gated * after
    grad_kernel = jnp.stack(
        [
            jnp.sum(grad_convolved * padded[offset : offset + row_count], axis=0)
            for offset in range(KW)
        ]
    )
    grad_padded = jnp.pad(kernel[0] * grad_convolved, ((0, rim_rows), (0, 0)))
    for offset in range(1, KW):
        grad_padded = grad_padded + jnp.pad(
            kernel[offset] * grad_convolved, ((offset, rim_rows - offset), (0, 0))
        )
    rim_out = jnp.where(place_index > 0, grad_padded[:rim_rows], 0.0)
    rim_back = shifted(rim_out, "dp", -1)
    grad_mixed = grad_padded[rim_rows:] + jnp.pad(rim_back, ((row_count - rim_rows, 0), (0, 0)))
    grad_projected = jnp.concatenate(
        [grad_mixed * signal, grad_after, grad_mixed * before], axis=1
    ).astype(jnp.bfloat16)
    grad_conv_in = outer_sum(normed_conv_b, grad_projected).reshape(width, 3, channels)
    grad_normed_conv = tensor_total(inner_back(grad_projected, weight_in))
    grad_inner_conv, grad_norm_conv = normalize_back(
        inputs, inverse_conv, norm_conv, grad_normed_conv
    )
    grad_inputs = grad_one + grad_inner_conv
    small_sums = lax.psum(
        (
            grad_norm_conv,
            grad_norm_mlp_one,
            grad_norm_attn,
            grad_norm_mlp_two,
            grad_kernel,
            grad_query_gain,
            grad_key_gain,
        ),
        "dp",
    )
    every_sum = (
        lax.psum_scatter(grad_conv_in, "dp", scatter_dimension=0, tiled=True),
        lax.psum_scatter(grad_conv_out, "dp", scatter_dimension=1, tiled=True),
        lax.psum_scatter(grad_gate_up_one, "dp", scatter_dimension=0, tiled=True),
        lax.psum_scatter(grad_down_one, "dp", scatter_dimension=1, tiled=True),
        lax.psum_scatter(grad_query_weight, "dp", scatter_dimension=0, tiled=True),
        lax.psum_scatter(grad_kv_weight, "dp", scatter_dimension=0, tiled=True),
        lax.psum_scatter(grad_attn_out, "dp", scatter_dimension=1, tiled=True),
        lax.psum_scatter(grad_gate_up_two, "dp", scatter_dimension=0, tiled=True),
        lax.psum_scatter(grad_down_two, "dp", scatter_dimension=1, tiled=True),
    )
    first_sums = every_sum[0:4]
    second_sums = every_sum[4:9]
    return (
        output,
        grad_inputs,
        small_sums[0],
        first_sums[0],
        small_sums[4],
        first_sums[1],
        small_sums[1],
        first_sums[2],
        first_sums[3],
        small_sums[2],
        second_sums[0],
        second_sums[1],
        small_sums[5],
        small_sums[6],
        second_sums[2],
        small_sums[3],
        second_sums[3],
        second_sums[4],
    )


def solution(mesh):
    in_specs = (
        P("dp", None),
        P(),
        P(),
        P(None, None, "tensor"),
        P(None, "tensor"),
        P("tensor", None),
        P(),
        P(None, None, "tensor"),
        P("tensor", None),
        P(),
        P(None, "tensor"),
        P(None, None, "tensor"),
        P(),
        P(),
        P("tensor", None),
        P(),
        P(None, None, "tensor"),
        P("tensor", None),
        P("dp", None),
    )
    out_specs = (
        P("dp", None),
        P("dp", None),
        P(),
        P("dp", None, "tensor"),
        P(None, "tensor"),
        P("tensor", "dp"),
        P(),
        P("dp", None, "tensor"),
        P("tensor", "dp"),
        P(),
        P("dp", "tensor"),
        P("dp", None, "tensor"),
        P(),
        P(),
        P("tensor", "dp"),
        P(),
        P("dp", None, "tensor"),
        P("tensor", "dp"),
    )
    return jax.shard_map(local, mesh=mesh, in_specs=in_specs, out_specs=out_specs, check_vma=False)
```

profile of v0, /device:TPU:0, one launch (start us, length us, event | category | flops | bytes accessed | tf_op | source)
XLA Modules:
  0.0 2987.3 jit_solution(14793658153648663215)
XLA Ops:
  32.3 71.3 %all-reduce.21.cloned.1.call-done = f32[512,1536]{1,0:T(8,128)} async-done(((f32[512,1536]{1,0:T(8,128)}), f32[512,1536]{1,0:T(8,128)}) %all-reduce.21.cloned.1.call-update) | async-done | bytes 3145744 | tf_op jit(solution)/shard_map/psum | solution.py:65
  132.2 64.0 %all-reduce.23.cloned.1.call-done = f32[512,1536]{1,0:T(8,128)} async-done(((f32[512,1536]{1,0:T(8,128)}), f32[512,1536]{1,0:T(8,128)}) %all-reduce.23.cloned.1.call-update) | async-done | bytes 3145744 | tf_op jit(solution)/shard_map/psum | solution.py:65
  212.1 13.4 collective-permute-start.1
  264.3 68.5 %all-reduce.25.cloned.1.call-done = f32[512,1536]{1,0:T(8,128)} async-done(((f32[512,1536]{1,0:T(8,128)}), f32[512,1536]{1,0:T(8,128)}) %all-reduce.25.cloned.1.call-update) | async-done | bytes 3145744 | tf_op jit(solution)/shard_map/psum | solution.py:65
  336.3 13.2 fusion.111
  368.9 68.1 %all-reduce.27.cloned.1.call-done = f32[512,1536]{1,0:T(8,128)} async-done(((f32[512,1536]{1,0:T(8,128)}), f32[512,1536]{1,0:T(8,128)}) %all-reduce.27.cloned.1.call-update) | async-done | bytes 3145744 | tf_op jit(solution)/shard_map/psum | solution.py:65
  457.1 33.0 %fusion.12 = f32[2,64,3,512]{3,1,2,0:T(8,128)S(1)} fusion(f32[2,2048,512,3]{2,1,3,0:T(8,128)} %fusion.74, f32[2,3,512,2048]{2,3,1,0:T(8,128)} %copy-done.2, f32[2,3,512]{2,1,0:T(4,128)S(1)} %log_add_fusion, bf16[2,2048,2,64]{1,3,2,0:T(8,128)(2,1)S(1)} %copy-done.44), kind=kOutput, calls=%fused_computation.17 | convolution fusion | flops 849351680 | bytes 102006784 | tf_op jit(solution)/shard_map/kgqs,skd->qkgd/dot_general | solution.py:219
  490.1 34.3 %fusion.25 = f32[1,2048,2,64]{1,3,2,0:T(8,128)} fusion(bf16[512,2,3,64]{0,3,2,1:T(8,128)(2,1)} %fusion.43, f32[2,2048,512,3]{2,1,3,0:T(8,128)} %fusion.74, f32[2,3,512,2048]{2,3,1,0:T(8,128)} %copy-done.2, f32[2,3,512]{2,1,0:T(4,128)S(1)} %log_add_fusion), kind=kOutput, calls=%fused_computation.70 | convolution fusion | flops 849351680 | bytes 51785728 | tf_op jit(solution)/shard_map/kgqs,qkgd->skd/dot_general | solution.py:222
  542.1 11.7 collective-permute-done.6
  567.6 89.5 %all-reduce.29.cloned.1.call-done = f32[512,1536]{1,0:T(8,128)} async-done(((f32[512,1536]{1,0:T(8,128)}), f32[512,1536]{1,0:T(8,128)}) %all-reduce.29.cloned.1.call-update) | async-done | bytes 3145744 | tf_op jit(solution)/shard_map/psum | solution.py:251
  692.6 60.7 %all-reduce.31.cloned.1.call-done = f32[512,1536]{1,0:T(8,128)} async-done(((f32[512,1536]{1,0:T(8,128)}), f32[512,1536]{1,0:T(8,128)}) %all-reduce.31.cloned.1.call-update) | async-done | bytes 3145744 | tf_op jit(solution)/shard_map/psum | solution.py:65
  774.7 14.9 fusion.31
  789.6 32.6 %copy.91 = f32[1536,2,1728]{2,1,0:T(2,128)} copy(f32[1536,2,1728]{0,2,1:T(8,128)} %bitcast.230) | data formatting | bytes 42467328 | tf_op jit(solution)/shard_map/reshape | solution.py:90
  829.0 15.9 fusion.29
  845.0 32.6 %copy.88 = f32[1536,2,1728]{2,1,0:T(2,128)} copy(f32[1536,2,1728]{0,2,1:T(8,128)} %bitcast.229) | data formatting | bytes 42467328 | tf_op jit(solution)/shard_map/reshape | solution.py:90
  934.9 38.7 %all-reduce.7 = (f32[1536]{0:T(1024)}, f32[3,384]{1,0:T(4,128)}, f32[1536]{0:T(1024)}, f32[1536]{0:T(1024)}, f32[64]{0:T(128)}, /*index=5*/f32[64]{0:T(128)}, f32[1536]{0:T(1024)}) all-reduce(f32[1536]{0:T(1024)S(1)} %get-tuple-element.42, f32[3,384]{1,0:T(4,128)S(1)} %pad_maximum_fusion.19, ...), channel_id=1, replica_groups=mesh['dp'=8,'tensor'=4] {'dp'}, use_global_device_ids=true, to_apply=%region_24.25 | all-reduce | flops 7424 | bytes 59392 | tf_op jit(solution)/shard_map/psum | solution.py:287
  981.6 571.8 %all-reduce.33.cloned.1.call-done = f32[1536,2,1728]{2,1,0:T(2,128)} async-done(((f32[1536,2,1728]{2,1,0:T(2,128)}), f32[1536,2,1728]{2,1,0:T(2,128)}) %all-reduce.33.cloned.1.call-update) | async-done | bytes 21233680
  1557.8 696.7 %all-reduce.35.cloned.1.call-done = (f32[1536,2,1728]{2,1,0:T(2,128)}, f32[1536,2,128]{2,1,0:T(2,128)}) async-done(((f32[1536,2,1728]{2,1,0:T(2,128)}, f32[1536,2,128]{2,1,0:T(2,128)}), (f32[1536,2,1728]{2,1,0:T(2,128)}, f32[1536,2,128]{2,1,0:T(2,128)})) %all-reduce.35.cloned.1.call-update) | async-done | bytes 22806544
  2260.4 66.1 %reduce-scatter.13.cloned.1.call-done = f32[192,384]{1,0:T(8,128)} async-done(((f32[1536,384]{1,0:T(8,128)}), f32[192,384]{1,0:T(8,128)}) %reduce-scatter.13.cloned.1.call-update) | async-done | bytes 294928 | tf_op jit(solution)/shard_map/reduce_scatter | solution.py:304
  2326.5 72.1 %reduce-scatter.15.cloned.1.call-done = f32[384,192]{0,1:T(8,128)} async-done(((f32[384,1536]{0,1:T(8,128)}), f32[384,192]{0,1:T(8,128)}) %reduce-scatter.15.cloned.1.call-update) | async-done | bytes 294928 | tf_op jit(solution)/shard_map/reduce_scatter | solution.py:306
  2398.6 71.9 %reduce-scatter.9.cloned.1.call-done = f32[384,192]{0,1:T(8,128)} async-done(((f32[384,1536]{0,1:T(8,128)}), f32[384,192]{0,1:T(8,128)}) %reduce-scatter.9.cloned.1.call-update) | async-done | bytes 294928 | tf_op jit(solution)/shard_map/reduce_scatter | solution.py:301
  2470.5 132.3 %reduce-scatter.7.cloned.1.call-done = f32[192,3,384]{2,0,1:T(8,128)} async-done(((f32[1536,3,384]{2,0,1:T(8,128)}), f32[192,3,384]{2,0,1:T(8,128)}) %reduce-scatter.7.cloned.1.call-update) | async-done | bytes 884752 | tf_op jit(solution)/shard_map/reduce_scatter | solution.py:300
  2602.8 188.9 %reduce-scatter.17.cloned.1.call-done = f32[1728,192]{0,1:T(8,128)} async-done(((f32[1728,1536]{0,1:T(8,128)}), f32[1728,192]{0,1:T(8,128)}) %reduce-scatter.17.cloned.1.call-update) | async-done | bytes 1327120 | tf_op jit(solution)/shard_map/reduce_scatter | solution.py:308
  2791.7 188.9 %reduce-scatter.11.cloned.1.call-done = f32[1728,192]{0,1:T(8,128)} async-done(((f32[1728,1536]{0,1:T(8,128)}), f32[1728,192]{0,1:T(8,128)}) %reduce-scatter.11.cloned.1.call-update) | async-done | bytes 1327120 | tf_op jit(solution)/shard_map/reduce_scatter | solution.py:303
  (353 shorter events, 320.0 us)
Async XLA Ops:
  7.2 96.4 %all-reduce.21.cloned.1.call-start = ((), (), s32[]{:S(2)}) async-start(), calls=%async_computation.6 | async-start | bytes 6291456 | tf_op jit(solution)/shard_map/psum | solution.py:65
  19.7 6.2 collective-permute-start
  32.3 163.9 %all-reduce.23.cloned.1.call-start = ((), (), s32[]{:S(2)}) async-start(), calls=%async_computation.7 | async-start | bytes 6291456 | tf_op jit(solution)/shard_map/psum | solution.py:65
  127.4 205.4 %all-reduce.25.cloned.1.call-start = ((), (), s32[]{:S(2)}) async-start(), calls=%async_computation.8 | async-start | bytes 6291456 | tf_op jit(solution)/shard_map/psum | solution.py:65
  202.9 26.7 collective-permute-start.3
  208.0 21.7 collective-permute-start.2
  212.1 17.6 collective-permute-start.1
  263.6 173.4 %all-reduce.27.cloned.1.call-start = ((), (), s32[]{:S(2)}) async-start(), calls=%async_computation.9 | async-start | bytes 6291456 | tf_op jit(solution)/shard_map/psum | solution.py:65
  368.3 288.8 %all-reduce.29.cloned.1.call-start = ((), (), s32[]{:S(2)}) async-start(), calls=%async_computation.10 | async-start | bytes 6291456 | tf_op jit(solution)/shard_map/psum | solution.py:251
  536.1 17.8 collective-permute-start.6
  537.5 26.3 collective-permute-start.5
  538.8 25.1 collective-permute-start.4
  567.6 185.7 %all-reduce.31.cloned.1.call-start = ((), (), s32[]{:S(2)}) async-start(), calls=%async_computation.11 | async-start | bytes 6291456 | tf_op jit(solution)/shard_map/psum | solution.py:65
  684.6 247.3 %all-reduce.37.cloned.1.call-start = ((), (), s32[]{:S(2)}) async-start(), calls=%async_computation.20 | async-start | bytes 12582912 | tf_op jit(solution)/shard_map/psum | solution.py:65
  764.7 5.8 collective-permute-start.7
  774.6 778.8 %all-reduce.33.cloned.1.call-start = ((), (), s32[]{:S(2)}) async-start(), calls=%async_computation.18 | async-start | bytes 44040192
  822.3 1432.2 %all-reduce.35.cloned.1.call-start = ((), (), s32[]{:S(2)}) async-start(), calls=%async_computation.19 | async-start | bytes 47185920
  877.6 1448.9 %reduce-scatter.13.cloned.1.call-start = ((), (), s32[]{:S(2)}) async-start(), calls=%async_computation.15 | async-start | bytes 2654208 | tf_op jit(solution)/shard_map/reduce_scatter | solution.py:304
  881.0 1517.6 %reduce-scatter.15.cloned.1.call-start = ((), (), s32[]{:S(2)}) async-start(), calls=%async_computation.16 | async-start | bytes 2654208 | tf_op jit(solution)/shard_map/reduce_scatter | solution.py:306
  885.5 1585.0 %reduce-scatter.9.cloned.1.call-start = ((), (), s32[]{:S(2)}) async-start(), calls=%async_computation.13 | async-start | bytes 2654208 | tf_op jit(solution)/shard_map/reduce_scatter | solution.py:301
  890.1 1712.8 %reduce-scatter.7.cloned.1.call-start = ((), (), s32[]{:S(2)}) async-start(), calls=%async_computation.12 | async-start | bytes 7962624 | tf_op jit(solution)/shard_map/reduce_scatter | solution.py:300
  903.3 1888.4 %reduce-scatter.17.cloned.1.call-start = ((), (), s32[]{:S(2)}) async-start(), calls=%async_computation.17 | async-start | bytes 12386304 | tf_op jit(solution)/shard_map/reduce_scatter | solution.py:308
  914.0 2066.6 %reduce-scatter.11.cloned.1.call-start = ((), (), s32[]{:S(2)}) async-start(), calls=%async_computation.14 | async-start | bytes 12386304 | tf_op jit(solution)/shard_map/reduce_scatter | solution.py:303
  1553.4 1427.2 %copy-start.1 = (bf16[384,1536]{1,0:T(8,128)(2,1)S(1)}, bf16[384,1536]{1,0:T(8,128)(2,1)}, u32[]{:S(2)}) copy-start(bf16[384,1536]{1,0:T(8,128)(2,1)} %param.33) | copy-start | bytes 3538948
  (90 other events, 1851.8 us)
Sparse Core Ops, SparseCore 0:
  32.4 71.2 all-reduce.20
  127.5 68.5 all-reduce.22
  263.7 69.0 all-reduce.24
  368.4 68.5 all-reduce.26
  567.7 89.3 all-reduce.28
  684.7 68.5 all-reduce.30
  774.8 119.8 all-reduce.36
  898.7 654.6 all-reduce.32
  1557.7 696.7 all-reduce.34
  2258.4 68.0 reduce-scatter.12
  2330.6 67.9 reduce-scatter.14
  2402.5 67.9 reduce-scatter.8
  2474.8 128.0 reduce-scatter.6
  2607.4 184.3 reduce-scatter.16
  2796.2 184.3 reduce-scatter.10
where the time goes:
time: 3000 us; the launch traced here: 2990 us
  waiting for transfers between devices  2440 us (81%)
  matrix products  265 us (9%)
  local copies, waits for them, and re-layouts  127 us (4%)
  other arithmetic  61.5 us (2%)
  blocking collectives  44.8 us (1%)
  starting transfers between devices  35.6 us (1%)
    unnamed x17, waiting for transfers between devices  1270 us
    psum x6, waiting for transfers between devices, tensor_total(): return lax.psum(partial_value, 'tensor')  333 us
    reduce_scatter x1, waiting for transfers between devices, local(): lax.psum_scatter(grad_down_two, 'dp', scatter_dimension=1, tiled=True)  189 us
    reduce_scatter x1, waiting for transfers between devices, local(): lax.psum_scatter(grad_down_one, 'dp', scatter_dimension=1, tiled=True)  189 us
    reduce_scatter x1, waiting for transfers between devices, local(): lax.psum_scatter(grad_conv_in, 'dp', scatter_dimension=0, tiled=True)  132 us
    psum x1, waiting for transfers between devices, local(): lax.psum((partial_normed, part_query_gain, part_key_gain), 'tensor')  89.5 us
    reduce_scatter x1, waiting for transfers between devices, local(): lax.psum_scatter(grad_attn_out, 'dp', scatter_dimension=1, tiled=True)  72.1 us
    reduce_scatter x1, waiting for transfers between devices, local(): lax.psum_scatter(grad_conv_out, 'dp', scatter_dimension=1, tiled=True)  71.9 us
  transfers between devices with their start and end apart: 23, of which 18 were waited for; matrix products, arithmetic and copies ran while one was open for 6% of the time, Pallas kernels for 0%

commit v1 on v0

v1 whole, which is shorter than its diff:
```python
import jax
import jax.numpy as jnp
from jax import lax
from jax.sharding import PartitionSpec as P

HEAD = 64
KW = 3
SPAN = 4
GROUP = 3


EPSILON = 1e-05
THETA = 1000000.0
BF16 = jnp.bfloat16
F32 = jnp.float32


def matmul(left, right):
    return jnp.dot(left, right, preferred_element_type=F32)


def outer_sum(left, right):
    return lax.dot_general(left, right, (((0,), (0,)), ((), ())), preferred_element_type=F32)


def inner_back(left, right):
    return lax.dot_general(left, right, (((1,), (1,)), ((), ())), preferred_element_type=F32)


def normalize(values, gain):
    inverse = lax.rsqrt(jnp.mean(values * values, axis=-1, keepdims=True) + EPSILON)
    return (values * inverse * gain, inverse)


def normalize_back(values, inverse, gain, grad_result):
    weighted = grad_result * gain
    grad_gain = jnp.sum(grad_result * values * inverse, axis=tuple(range(values.ndim - 1)))
    inner = jnp.mean(weighted * values, axis=-1, keepdims=True)
    grad_values = inverse * (weighted - values * inverse * inverse * inner)
    return (grad_values, grad_gain)


def rotate(values, cosine, sine_table):
    middle = values.shape[-1] // 2
    turned = jnp.concatenate([-values[..., middle:], values[..., :middle]], axis=-1)
    return values * cosine + turned * sine_table


def rotate_back(grads, cosine, sine_table):
    middle = grads.shape[-1] // 2
    scaled = grads * sine_table
    turned = jnp.concatenate([scaled[..., middle:], -scaled[..., :middle]], axis=-1)
    return grads * cosine + turned


def swap(block, axis, bit):
    route = [(i, i ^ bit) for i in range(lax.axis_size(axis))]
    return lax.ppermute(block, axis, route)


def scatter_rows(partial_b):
    rows = partial_b.shape[0]
    half, quarter = rows // 2, rows // 4
    got = swap(partial_b[half:], "tensor", 1)
    far = (partial_b[quarter:half].astype(F32) + got[quarter:].astype(F32)).astype(BF16)
    got_far = swap(far, "tensor", 2)
    own = partial_b[:quarter].astype(F32) + got[:quarter].astype(F32)
    return own + got_far.astype(F32)


def gather_rows(own):
    pair = jnp.concatenate([own, swap(own, "tensor", 2)], axis=0)
    return jnp.concatenate([pair, swap(pair, "tensor", 1)], axis=0)


def block_owners(index):
    return [index, index ^ 2, index ^ 1, index ^ 3]


def to_local(values, index):
    quarter = values.shape[0] // 4
    return jnp.concatenate(
        [lax.dynamic_slice_in_dim(values, o * quarter, quarter) for o in block_owners(index)]
    )


def to_true(values, index):
    quarter = values.shape[0] // 4
    places = []
    for block in range(4):
        shift = block ^ index
        place = ((shift & 1) << 1) | (shift >> 1)
        places.append(lax.dynamic_slice_in_dim(values, place * quarter, quarter))
    return jnp.concatenate(places)


def ring_order(count):
    return list(range(0, count, 2)) + [i for i in range(count - 1, -1, -1) if i % 2 == 1]


class Ring:
    def __init__(self, count):
        self.count = count
        self.order = ring_order(count)
        place = [0] * count
        for at, device in enumerate(self.order):
            place[device] = at
        self.place = jnp.array(place, jnp.int32)[lax.axis_index("dp")]
        self.table = jnp.array(self.order, jnp.int32)
        pairs = [(self.order[i], self.order[(i + 1) % count]) for i in range(count)]
        self.routes = (pairs, [(b, a) for a, b in pairs])

    def owner(self, distance):
        return self.table[lax.rem(self.place + distance + self.count, self.count)]

    def sum_scatter(self, grads):
        rows = grads.shape[0] // self.count
        half = rows // 2
        sums = []
        for side in range(2):
            sign = -1 if side == 0 else 1
            held = None
            for step in range(self.count):
                owner = self.owner(sign * (step + 1)) if step < self.count - 1 else lax.axis_index("dp")
                term = lax.dynamic_slice_in_dim(grads, owner * rows + side * half, half if side == 0 else rows - half)
                if held is None:
                    total = term
                else:
                    total = held.astype(F32) + term.astype(F32)
                if step < self.count - 1:
                    held = lax.ppermute(total.astype(BF16), "dp", self.routes[side])
            sums.append(total)
        return jnp.concatenate(sums, axis=0)


def split_gate_up(weight):
    return weight[:, 0, :], weight[:, 1, :]


def score_block(grouped, near_keys, positions, key_positions, key_ok, factor):
    raw = (
        jnp.einsum("qkgd,skd->kgqs", grouped, near_keys, preferred_element_type=jnp.float32)
        * factor
    )
    allowed = (key_positions[None, :] <= positions[:, None]) & key_ok[None, :]
    return jnp.where(allowed, raw, -1e30)


def mlp_hidden(normed_b, gate_w, up_w):
    gate = matmul(normed_b, gate_w)
    upward = matmul(normed_b, up_w)
    active_b = (jax.nn.silu(gate) * upward).astype(BF16)
    return gate, upward, active_b


def mlp_back_hidden(grad_b, down, gate, upward):
    grad_active = inner_back(grad_b, down)
    sigma = jax.nn.sigmoid(gate)
    grad_gate = (grad_active * upward * sigma * (1.0 + gate * (1.0 - sigma))).astype(BF16)
    grad_upward = (grad_active * gate * sigma).astype(BF16)
    return grad_gate, grad_upward


def local(
    tokens,
    lengths,
    norm_conv,
    conv_in,
    conv_kernel,
    conv_out,
    norm_mlp_one,
    gate_up_one,
    down_one,
    norm_attn,
    query_weight,
    kv_weight,
    query_gain,
    key_gain,
    attn_out,
    norm_mlp_two,
    gate_up_two,
    down_two,
    cotangent,
):
    row_count = tokens.shape[0]
    width = tokens.shape[1]
    quarter = row_count // 4
    channels = conv_out.shape[0]
    local_heads = query_weight.shape[1] // HEAD
    local_kv = kv_weight.shape[2] // HEAD
    device = lax.axis_index("dp")
    devices = lax.axis_size("dp")
    index = lax.axis_index("tensor")
    sequence = device // SPAN
    place_index = device % SPAN
    length = lengths[sequence]
    ring = Ring(devices)
    offsets = jnp.concatenate(
        [o * quarter + jnp.arange(quarter, dtype=jnp.int32) for o in block_owners(index)]
    )
    positions = place_index * row_count + offsets
    is_valid = positions < length
    frequency = THETA ** (-2.0 * jnp.arange(HEAD // 2, dtype=jnp.float32) / HEAD)
    angles = positions.astype(jnp.float32)[:, None] * frequency[None, :]
    angles = jnp.concatenate([angles, angles], axis=-1)[:, None, :]
    cosine = jnp.cos(angles)
    sine_table = jnp.sin(angles)
    factor = HEAD ** (-0.5)
    kernel = conv_kernel.astype(jnp.float32)
    rim_rows = KW - 1
    gate_one, up_one = split_gate_up(gate_up_one)
    gate_two, up_two = split_gate_up(gate_up_two)
    forward_route = [(i, i + 1) for i in range(devices - 1) if (i + 1) % SPAN]
    backward_route = [(b, a) for a, b in forward_route]

    inputs = tokens.astype(F32)
    normed_conv, inverse_conv = normalize(inputs, norm_conv)
    normed_conv_b = normed_conv.astype(BF16)
    weight_in = conv_in.reshape(width, 3 * channels)
    projected = matmul(normed_conv_b, weight_in)
    before = projected[:, :channels]
    after = projected[:, channels : 2 * channels]
    signal = projected[:, 2 * channels :]
    mixed = before * signal
    rim_in = lax.ppermute(mixed[row_count - rim_rows :], "dp", forward_route)
    padded = jnp.concatenate([rim_in, mixed], axis=0)
    convolved = kernel[0] * padded[0:row_count]
    for offset in range(1, KW):
        convolved = convolved + kernel[offset] * padded[offset : offset + row_count]
    gated_b = to_local((after * convolved).astype(BF16), index)
    inputs_own = lax.dynamic_slice_in_dim(tokens, index * quarter, quarter).astype(F32)
    one_own = inputs_own + scatter_rows(matmul(gated_b, conv_out).astype(BF16))

    norm_one, inverse_one = normalize(one_own, norm_mlp_one)
    norm_one_b = gather_rows(norm_one.astype(BF16))
    gate_a, up_a, active_one = mlp_hidden(norm_one_b, gate_one, up_one)
    two_own = one_own + scatter_rows(matmul(active_one, down_one).astype(BF16))

    normed_attn, inverse_attn = normalize(two_own, norm_attn)
    normed_attn_b = gather_rows(normed_attn.astype(BF16))
    kv_flat = kv_weight.reshape(width, 2 * local_kv * HEAD)
    joined = matmul(normed_attn_b, kv_flat)
    key_raw = joined[:, : local_kv * HEAD].reshape(row_count, local_kv, HEAD)
    value_rows = joined[:, local_kv * HEAD :].reshape(row_count, local_kv, HEAD).astype(BF16)
    key_norm, key_inverse = normalize(key_raw, key_gain)
    key_rot = rotate(key_norm, cosine, sine_table).astype(BF16)
    stacked = jnp.stack([key_rot, value_rows])
    pieces = [stacked]
    for distance in range(1, SPAN):
        route = [(i, i + distance) for i in range(devices) if i % SPAN + distance < SPAN]
        pieces.append(lax.ppermute(stacked, "dp", route))
    query_raw = matmul(normed_attn_b, query_weight).reshape(row_count, local_heads, HEAD)
    query_norm, query_inverse = normalize(query_raw, query_gain)
    query_rot = rotate(query_norm, cosine, sine_table).astype(BF16)
    grouped = query_rot.reshape(row_count, local_kv, GROUP, HEAD)
    nearby = jnp.concatenate(pieces, axis=1)
    key_positions = jnp.concatenate([positions - distance * row_count for distance in range(SPAN)])
    key_ok = (key_positions >= 0) & (key_positions < length)
    near_keys = nearby[0]
    near_values = nearby[1]
    scores = score_block(grouped, near_keys, positions, key_positions, key_ok, factor)
    peak = jnp.max(scores, axis=-1, keepdims=True)
    expo = jnp.exp(scores - peak)
    total = jnp.sum(expo, axis=-1, keepdims=True)
    log_total = peak + jnp.log(total)
    weights_b = (expo / total).astype(BF16)
    attended = jnp.einsum(
        "kgqs,skd->qkgd", weights_b, near_values, preferred_element_type=jnp.float32
    )
    attended_b = attended.reshape(row_count, local_heads * HEAD).astype(BF16)
    three_own = two_own + scatter_rows(matmul(attended_b, attn_out).astype(BF16))

    norm_two, inverse_two = normalize(three_own, norm_mlp_two)
    norm_two_b = gather_rows(norm_two.astype(BF16))
    gate_b, up_b, active_two = mlp_hidden(norm_two_b, gate_two, up_two)
    grad_result = to_local(cotangent, index).astype(F32) * is_valid[:, None].astype(F32)
    grad_result_b = grad_result.astype(BF16)
    sum_down_two = ring.sum_scatter(outer_sum(grad_result_b, active_two).astype(BF16))
    grad_gate, grad_up = mlp_back_hidden(grad_result_b, down_two, gate_b, up_b)
    sum_gate_two = ring.sum_scatter(outer_sum(norm_two_b, grad_gate).astype(BF16))
    sum_up_two = ring.sum_scatter(outer_sum(norm_two_b, grad_up).astype(BF16))
    partial_normed = inner_back(grad_gate, gate_two) + inner_back(grad_up, up_two)
    grad_normed = scatter_rows(partial_normed.astype(BF16))
    grad_inner, grad_norm_mlp_two = normalize_back(three_own, inverse_two, norm_mlp_two, grad_normed)
    grad_three = grad_result[:quarter] + grad_inner

    output_own = (three_own + scatter_rows(matmul(active_two, down_two).astype(BF16))).astype(BF16)
    output = to_true(gather_rows(output_own), index)

    grad_branch = gather_rows(grad_three.astype(BF16))
    grad_attn_out = outer_sum(grad_branch, attended_b)
    grad_attended = (
        inner_back(grad_branch, attn_out)
        .astype(BF16)
        .reshape(row_count, local_kv, GROUP, HEAD)
    )
    scores = score_block(grouped, near_keys, positions, key_positions, key_ok, factor)
    probs = jnp.exp(scores - log_total)
    probs_b = probs.astype(BF16)
    grad_probs = jnp.einsum(
        "qkgd,skd->kgqs", grad_attended, near_values, preferred_element_type=jnp.float32
    )
    delta = jnp.sum(probs * grad_probs, axis=-1, keepdims=True)
    grad_scores = (probs * (grad_probs - delta) * factor).astype(BF16)
    grad_query = jnp.einsum(
        "kgqs,skd->qkgd", grad_scores, near_keys, preferred_element_type=jnp.float32
    ).reshape(row_count, local_heads, HEAD)
    grad_keys_near = jnp.einsum(
        "kgqs,qkgd->skd", grad_scores, grouped, preferred_element_type=jnp.float32
    )
    grad_values_near = jnp.einsum(
        "kgqs,qkgd->skd", probs_b, grad_attended, preferred_element_type=jnp.float32
    )
    grad_nearby = jnp.stack([grad_keys_near, grad_values_near])
    owned = grad_nearby[:, :row_count]
    for distance in range(1, SPAN):
        route = [(i + distance, i) for i in range(devices) if i % SPAN + distance < SPAN]
        sent = grad_nearby[:, distance * row_count : (distance + 1) * row_count].astype(BF16)
        owned = owned + lax.ppermute(sent, "dp", route).astype(F32)
    grad_query_raw, part_query_gain = normalize_back(
        query_raw, query_inverse, query_gain, rotate_back(grad_query, cosine, sine_table)
    )
    grad_key_raw, part_key_gain = normalize_back(
        key_raw, key_inverse, key_gain, rotate_back(owned[0], cosine, sine_table)
    )
    grad_query_b = grad_query_raw.reshape(row_count, local_heads * HEAD).astype(BF16)
    grad_joined_b = jnp.concatenate(
        [
            grad_key_raw.reshape(row_count, local_kv * HEAD),
            owned[1].reshape(row_count, local_kv * HEAD),
        ],
        axis=1,
    ).astype(BF16)
    grad_qkv_b = jnp.concatenate([grad_query_b, grad_joined_b], axis=1)
    attn_grads = jnp.concatenate([grad_attn_out, outer_sum(normed_attn_b, grad_qkv_b)], axis=1)
    sum_attn = ring.sum_scatter(attn_grads.astype(BF16))
    partial_normed = inner_back(grad_query_b, query_weight) + inner_back(grad_joined_b, kv_flat)
    grad_normed = scatter_rows(partial_normed.astype(BF16))
    grad_inner, grad_norm_attn = normalize_back(two_own, inverse_attn, norm_attn, grad_normed)
    grad_two = grad_three + grad_inner

    grad_two_b = gather_rows(grad_two.astype(BF16))
    sum_down_one = ring.sum_scatter(outer_sum(grad_two_b, active_one).astype(BF16))
    grad_gate, grad_up = mlp_back_hidden(grad_two_b, down_one, gate_a, up_a)
    sum_gate_one = ring.sum_scatter(outer_sum(norm_one_b, grad_gate).astype(BF16))
    sum_up_one = ring.sum_scatter(outer_sum(norm_one_b, grad_up).astype(BF16))
    partial_normed = inner_back(grad_gate, gate_one) + inner_back(grad_up, up_one)
    grad_normed = scatter_rows(partial_normed.astype(BF16))
    grad_inner, grad_norm_mlp_one = normalize_back(one_own, inverse_one, norm_mlp_one, grad_normed)
    grad_one = grad_two + grad_inner

    grad_one_b = gather_rows(grad_one.astype(BF16))
    grad_conv_out = outer_sum(grad_one_b, gated_b)
    grad_gated = to_true(inner_back(grad_one_b, conv_out), index)
    grad_after = grad_gated * convolved
    grad_convolved = grad_gated * after
    grad_kernel = jnp.stack(
        [
            jnp.sum(grad_convolved * padded[offset : offset + row_count], axis=0)
            for offset in range(KW)
        ]
    )
    grad_padded = jnp.pad(kernel[0] * grad_convolved, ((0, rim_rows), (0, 0)))
    for offset in range(1, KW):
        grad_padded = grad_padded + jnp.pad(
            kernel[offset] * grad_convolved, ((offset, rim_rows - offset), (0, 0))
        )
    rim_back = lax.ppermute(grad_padded[:rim_rows], "dp", backward_route)
    grad_mixed = grad_padded[rim_rows:] + jnp.pad(rim_back, ((row_count - rim_rows, 0), (0, 0)))
    grad_projected = jnp.concatenate(
        [grad_mixed * signal, grad_after, grad_mixed * before], axis=1
    ).astype(BF16)
    conv_grads = jnp.concatenate([grad_conv_out, outer_sum(normed_conv_b, grad_projected)], axis=1)
    sum_conv = ring.sum_scatter(conv_grads.astype(BF16))
    partial_normed = inner_back(to_local(grad_projected, index), weight_in)
    grad_normed = scatter_rows(partial_normed.astype(BF16))
    norm_input_own, inverse_own = normalize(inputs_own, norm_conv)
    grad_inner, grad_norm_conv = normalize_back(inputs_own, inverse_own, norm_conv, grad_normed)
    grad_inputs = to_true(gather_rows(grad_one + grad_inner), index)

    small = jnp.concatenate(
        [
            grad_norm_conv,
            grad_norm_mlp_one,
            grad_norm_attn,
            grad_norm_mlp_two,
            part_query_gain,
            part_key_gain,
        ]
    )
    for bit in (1, 2):
        small = small + swap(small, "tensor", bit)
    small = jnp.concatenate([small, grad_kernel.reshape(-1)])
    bit = 1
    while bit < devices:
        small = small + swap(small, "dp", bit)
        bit *= 2
    tap_sums = small[4 * width + 2 * HEAD :].reshape(KW, channels)

    out_rows = width // devices
    return (
        output,
        grad_inputs,
        small[:width],
        sum_conv[:, channels:].reshape(out_rows, 3, channels),
        tap_sums,
        sum_conv[:, :channels].T,
        small[width : 2 * width],
        jnp.stack([sum_gate_one, sum_up_one], axis=1),
        sum_down_one.T,
        small[2 * width : 3 * width],
        sum_attn[:, local_heads * HEAD : 2 * local_heads * HEAD],
        sum_attn[:, 2 * local_heads * HEAD :].reshape(out_rows, 2, local_kv * HEAD),
        small[4 * width : 4 * width + HEAD],
        small[4 * width + HEAD : 4 * width + 2 * HEAD],
        sum_attn[:, : local_heads * HEAD].T,
        small[3 * width : 4 * width],
        jnp.stack([sum_gate_two, sum_up_two], axis=1),
        sum_down_two.T,
    )


def solution(mesh):
    in_specs = (
        P("dp", None),
        P(),
        P(),
        P(None, None, "tensor"),
        P(None, "tensor"),
        P("tensor", None),
        P(),
        P(None, None, "tensor"),
        P("tensor", None),
        P(),
        P(None, "tensor"),
        P(None, None, "tensor"),
        P(),
        P(),
        P("tensor", None),
        P(),
        P(None, None, "tensor"),
        P("tensor", None),
        P("dp", None),
    )
    out_specs = (
        P("dp", None),
        P("dp", None),
        P(),
        P("dp", None, "tensor"),
        P(None, "tensor"),
        P("tensor", "dp"),
        P(),
        P("dp", None, "tensor"),
        P("tensor", "dp"),
        P(),
        P("dp", "tensor"),
        P("dp", None, "tensor"),
        P(),
        P(),
        P("tensor", "dp"),
        P(),
        P("dp", None, "tensor"),
        P("tensor", "dp"),
    )
    return jax.shard_map(local, mesh=mesh, in_specs=in_specs, out_specs=out_specs, check_vma=False)
```

time: 3000 us -> 1050 us (0.35)
  waiting for transfers between devices: 2440 us -> 444 us
  starting transfers between devices: 35.6 us -> 163 us
  other arithmetic: 61.5 us -> 135 us
  local copies, waits for them, and re-layouts: 127 us -> 60.1 us
  matrix products: 265 us -> 213 us
  blocking collectives: 44.8 us -> 0 us
    unnamed x17 -> x0, waiting for transfers between devices: 1270 us -> none
    reduce_scatter x6 -> x0, waiting for transfers between devices: 720 us -> none  [the longest x1 189 us: local(): lax.psum_scatter(grad_down_two, 'dp', scatter_dimension=1, tiled=True)]
    psum x7 -> x0, waiting for transfers between devices: 422 us -> none  [the longest x6 333 us: tensor_total(): return lax.psum(partial_value, 'tensor')]
    ppermute x8 -> x157, waiting for transfers between devices: 26.4 us -> 444 us  [the longest x112 376 us: sum_scatter(): held = lax.ppermute(total.astype(BF16), 'dp', self.routes[side])]
    ppermute x8 -> x157, starting transfers between devices: 33.8 us -> 163 us  [the longest x112 121 us: sum_scatter(): held = lax.ppermute(total.astype(BF16), 'dp', self.routes[side])]
    reshape x4 -> x2, local copies, waits for them, and re-layouts: 76.9 us -> 1.3 us  [the longest x1 0.7 us: local(): small = jnp.concatenate([small, grad_kernel.reshape(-1)])]
    convert_element_type x7 -> x77, other arithmetic: 11.1 us -> 56.3 us  [the longest x58 40.6 us: sum_scatter(): held = lax.ppermute(total.astype(BF16), 'dp', self.routes[side])]
    psum x2 -> x0, blocking collectives: 44.8 us -> none  [the longest x1 38.7 us: local(): lax.psum((grad_norm_conv, grad_norm_mlp_one, grad_norm_attn, grad_norm_ml...]
  transfers between devices with their start and end apart: 23 -> 157, of which waited for: 18 -> 107; matrix products, arithmetic and copies ran while one was open for 6% -> 29% of each run, Pallas kernels for 0% -> 0%
where the time goes in v1:
time: 1050 us; the launch traced here: 1040 us
  waiting for transfers between devices  444 us (42%)
  matrix products  213 us (20%)
  starting transfers between devices  163 us (16%)
  other arithmetic  135 us (13%)
  local copies, waits for them, and re-layouts  60.1 us (6%)
  between operations  22 us (2%)
    ppermute x112, waiting for transfers between devices, sum_scatter(): held = lax.ppermute(total.astype(BF16), 'dp', self.routes[side])  376 us
    ppermute x112, starting transfers between devices, sum_scatter(): held = lax.ppermute(total.astype(BF16), 'dp', self.routes[side])  121 us
    ppermute x37, waiting for transfers between devices, swap(): return lax.ppermute(block, axis, route)  47.7 us
    convert_element_type x58, other arithmetic, sum_scatter(): held = lax.ppermute(total.astype(BF16), 'dp', self.routes[side])  40.6 us
    dot_general x11, matrix products, matmul(): return jnp.dot(left, right, preferred_element_type=F32)  40.4 us
    unnamed x378, local copies, waits for them, and re-layouts  37.7 us
    dot_general x11, matrix products, inner_back(): lax.dot_general(left, right, (((1,), (1,)), ((), ())), preferred_element_...  36.9 us
    dot_general x1, matrix products, local(): jnp.einsum('kgqs,qkgd->skd', grad_scores, grouped, preferred_element_type...  33 us
  transfers between devices with their start and end apart: 157, of which 107 were waited for; matrix products, arithmetic and copies ran while one was open for 29% of the time, Pallas kernels for 0%

profile of v1, /device:TPU:0, one launch (start us, length us, event | category | flops | bytes accessed | tf_op | source)
XLA Modules:
  0.0 1037.2 jit_solution(1512245678314912337)
XLA Ops:
  29.8 9.7 collective-permute-done.2
  43.0 8.8 collective-permute-done.3
  76.1 8.4 collective-permute-done.6
  88.4 8.1 collective-permute-done.7
  120.0 10.5 %fusion.188 = (f32[2,3,512]{2,1,0:T(4,128)S(1)}, f32[2,3,512,2048]{2,3,1,0:T(8,128)}) fusion(bf16[512,2,3,64]{0,3,2,1:T(8,128)(2,1)S(1)} %fusion.85, bf16[2,2048,2,64]{1,3,2,0:T(8,128)(2,1)S(1)} %pad_maximum_fusion.15, pred[512,2048]{0,1:T(8,128)(4,1)S(1)} %copy-done.83), kind=kOutput, calls=%fused_computation.583 | convolution fusion | flops 824177664 | bytes 27144192 | tf_op jit(solution)/shard_map/qkgd,skd->kgqs/dot_general | solution.py:142
  130.6 10.2 fusion.4
  140.8 10.5 %fusion.58 = bf16[2,64,3,512]{3,1,2,0:T(8,128)(2,1)S(1)} fusion(f32[2,3,512,2048]{2,3,1,0:T(8,128)} %get-tuple-element.294, f32[2,3,512]{2,1,0:T(4,128)S(1)} %fusion.4, f32[2,3,512]{2,1,0:T(4,128)S(1)} %get-tuple-element.293, bf16[2,2048,2,64]{1,3,2,0:T(8,128)(2,1)S(1)} %pad_maximum_fusion.15), kind=kOutput, calls=%fused_computation.179 | convolution fusion | flops 824377344 | bytes 26116096 | tf_op jit(solution)/shard_map/kgqs,skd->qkgd/dot_general | solution.py:267
  182.2 7.5 fusion.92
  197.9 9.0 multiply_convert_fusion.3
  439.5 10.1 fusion.107
  449.6 10.2 fusion.54
  459.8 32.9 %fusion.12 = f32[2,64,3,512]{3,1,2,0:T(8,128)S(1)} fusion(f32[2,2048,512,3]{2,1,3,0:T(8,128)} %fusion.107, f32[2,3,512,2048]{2,3,1,0:T(8,128)} %get-tuple-element.294, f32[2,3,512]{2,1,0:T(4,128)S(1)} %copy-done.122, bf16[2,2048,2,64]{1,3,2,0:T(8,128)(2,1)S(1)} %copy-done.58), kind=kOutput, calls=%fused_computation.49 | convolution fusion | flops 849351680 | bytes 102006784 | tf_op jit(solution)/shard_map/kgqs,skd->qkgd/dot_general | solution.py:305
  492.7 33.0 %fusion.53 = f32[1,2048,2,64]{1,3,2,0:T(8,128)S(1)} fusion(bf16[512,2,3,64]{0,3,2,1:T(8,128)(2,1)} %copy-done.90, f32[2,2048,512,3]{2,1,3,0:T(8,128)} %fusion.107, f32[2,3,512,2048]{2,3,1,0:T(8,128)} %get-tuple-element.294, f32[2,3,512]{2,1,0:T(4,128)S(1)} %copy-done.122), kind=kOutput, calls=%fused_computation.149 | convolution fusion | flops 849351680 | bytes 51785728 | tf_op jit(solution)/shard_map/kgqs,qkgd->skd/dot_general | solution.py:308
  533.5 9.6 collective-permute-done.24
  628.5 6.7 collective-permute-done.104
  646.9 7.3 collective-permute-done.106
  666.0 6.7 multiply_convert_fusion.1
  873.9 7.0 collective-permute-done.35
  890.4 7.2 collective-permute-done.52
  910.6 8.8 collective-permute-done.54
  939.6 8.1 collective-permute-done.57
  962.4 8.3 collective-permute-done.46
  1012.5 9.2 collective-permute-done.50
  1027.1 6.7 collective-permute-done.51
  (939 shorter events, 760.7 us)
Async XLA Ops:
  155.6 24.4 %collective-permute-start.13 = (bf16[128,1536]{1,0:T(8,128)(2,1)S(1)}, bf16[128,1536]{1,0:T(8,128)(2,1)}, u32[]{:S(2)}, u32[]{:S(2)}) collective-permute-start(bf16[128,1536]{1,0:T(8,128)(2,1)S(1)} %add_convert_fusion.90), channel_id=1, source_target_pairs={{0,2},{1,3},{2,0},{3,1},{4,6},{5,7},{6,4},{7,5},{8,10},{9,11},{10,... | collective-permute-start | bytes 1179656 | tf_op jit(solution)/shard_map/ppermute | solution.py:58
  216.7 79.8 %collective-permute-start.16 = (bf16[256,1536]{1,0:T(8,128)(2,1)S(1)}, bf16[256,1536]{1,0:T(8,128)(2,1)S(1)}, u32[]{:S(2)}, u32[]{:S(2)}) collective-permute-start(bf16[256,1536]{1,0:T(8,128)(2,1)S(1)} %slice.387), channel_id=1, source_target_pairs={{0,1},{1,0},{2,3},{3,2},{4,5},{5,4},{6,7},{7,6},{8,9},{9,8},{10,11... | collective-permute-start | bytes 2359304 | tf_op jit(solution)/shard_map/ppermute | solution.py:58
  217.3 26.7 %collective-permute-start.143 = (bf16[96,1728]{0,1:T(8,128)(2,1)S(1)}, bf16[96,1728]{0,1:T(8,128)(2,1)S(1)}, u32[]{:S(2)}, u32[]{:S(2)}) collective-permute-start(bf16[96,1728]{0,1:T(8,128)(2,1)S(1)} %get-tuple-element.122), channel_id=1, source_target_pairs={{0,8},{8,16},{16,24},{24,28},{28,20},{20,12},{12,4},{4,0},{1,9},{9... | collective-permute-start | bytes 995336 | tf_op jit(solution)/shard_map/ppermute | solution.py:131
  221.1 23.0 %collective-permute-start.150 = (bf16[96,1728]{0,1:T(8,128)(2,1)S(1)}, bf16[96,1728]{0,1:T(8,128)(2,1)S(1)}, u32[]{:S(2)}, u32[]{:S(2)}) collective-permute-start(bf16[96,1728]{0,1:T(8,128)(2,1)S(1)} %get-tuple-element.123), channel_id=1, source_target_pairs={{8,0},{16,8},{24,16},{28,24},{20,28},{12,20},{4,12},{0,4},{9,1},{1... | collective-permute-start | bytes 995336 | tf_op jit(solution)/shard_map/ppermute | solution.py:131
  231.9 65.7 %collective-permute-start.20 = (bf16[256,1536]{1,0:T(8,128)(2,1)S(1)}, bf16[256,1536]{1,0:T(8,128)(2,1)S(1)}, u32[]{:S(2)}, u32[]{:S(2)}) collective-permute-start(bf16[256,1536]{1,0:T(8,128)(2,1)S(1)} %slice.393), channel_id=1, source_target_pairs={{0,1},{1,0},{2,3},{3,2},{4,5},{5,4},{6,7},{7,6},{8,9},{9,8},{10,11... | collective-permute-start | bytes 2359304 | tf_op jit(solution)/shard_map/ppermute | solution.py:58
  298.9 24.5 %collective-permute-start.138 = (bf16[96,1728]{0,1:T(8,128)(2,1)S(1)}, bf16[96,1728]{0,1:T(8,128)(2,1)S(1)}, u32[]{:S(2)}, u32[]{:S(2)}) collective-permute-start(bf16[96,1728]{0,1:T(8,128)(2,1)S(1)} %get-tuple-element.151), channel_id=1, source_target_pairs={{8,0},{16,8},{24,16},{28,24},{20,28},{12,20},{4,12},{0,4},{9,1},{1... | collective-permute-start | bytes 995336 | tf_op jit(solution)/shard_map/ppermute | solution.py:131
  356.7 23.6 %collective-permute-start.140 = (bf16[96,1728]{0,1:T(8,128)(2,1)S(1)}, bf16[96,1728]{0,1:T(8,128)(2,1)S(1)}, u32[]{:S(2)}, u32[]{:S(2)}) collective-permute-start(bf16[96,1728]{0,1:T(8,128)(2,1)S(1)} %get-tuple-element.147), channel_id=1, source_target_pairs={{8,0},{16,8},{24,16},{28,24},{20,28},{12,20},{4,12},{0,4},{9,1},{1... | collective-permute-start | bytes 995336 | tf_op jit(solution)/shard_map/ppermute | solution.py:131
  361.3 259.3 %collective-permute-start.19 = (bf16[256,1536]{1,0:T(8,128)(2,1)}, bf16[256,1536]{1,0:T(8,128)(2,1)}, u32[]{:S(2)}, u32[]{:S(2)}) collective-permute-start(bf16[256,1536]{1,0:T(8,128)(2,1)} %pad_maximum_fusion.20), channel_id=1, source_target_pairs={{0,1},{1,0},{2,3},{3,2},{4,5},{5,4},{6,7},{7,6},{8,9},{9,8},{10,11... | collective-permute-start | bytes 2359304 | tf_op jit(solution)/shard_map/ppermute | solution.py:58
  364.9 73.0 %collective-permute-start.23 = (bf16[256,1536]{1,0:T(8,128)(2,1)S(1)}, bf16[256,1536]{1,0:T(8,128)(2,1)S(1)}, u32[]{:S(2)}, u32[]{:S(2)}) collective-permute-start(bf16[256,1536]{1,0:T(8,128)(2,1)S(1)} %pad_maximum_fusion.21), channel_id=1, source_target_pairs={{0,1},{1,0},{2,3},{3,2},{4,5},{5,4},{6,7},{7,6},{8,9},{9,8},{10,11... | collective-permute-start | bytes 2359304 | tf_op jit(solution)/shard_map/ppermute | solution.py:58
  582.5 23.1 %collective-permute-start.28 = (bf16[128,1536]{1,0:T(8,128)(2,1)}, bf16[128,1536]{1,0:T(8,128)(2,1)}, u32[]{:S(2)}, u32[]{:S(2)}) collective-permute-start(bf16[128,1536]{1,0:T(8,128)(2,1)} %add_convert_fusion.86), channel_id=1, source_target_pairs={{0,2},{1,3},{2,0},{3,1},{4,6},{5,7},{6,4},{7,5},{8,10},{9,11},{10,... | collective-permute-start | bytes 1179656 | tf_op jit(solution)/shard_map/ppermute | solution.py:58
  628.5 27.3 %collective-permute-start.30 = (bf16[256,1536]{1,0:T(8,128)(2,1)}, bf16[256,1536]{1,0:T(8,128)(2,1)}, u32[]{:S(2)}, u32[]{:S(2)}) collective-permute-start(bf16[256,1536]{1,0:T(8,128)(2,1)} %pad_maximum_fusion.23), channel_id=1, source_target_pairs={{0,1},{1,0},{2,3},{3,2},{4,5},{5,4},{6,7},{7,6},{8,9},{9,8},{10,11... | collective-permute-start | bytes 2359304 | tf_op jit(solution)/shard_map/ppermute | solution.py:58
  655.7 35.9 %collective-permute-start.107 = (bf16[96,1024]{0,1:T(8,128)(2,1)S(1)}, bf16[96,1024]{0,1:T(8,128)(2,1)S(1)}, u32[]{:S(2)}, u32[]{:S(2)}) collective-permute-start(bf16[96,1024]{0,1:T(8,128)(2,1)S(1)} %add_convert_fusion.99), channel_id=1, source_target_pairs={{0,8},{8,16},{16,24},{24,28},{28,20},{20,12},{12,4},{4,0},{1,9},{9... | collective-permute-start | bytes 589832 | tf_op jit(solution)/shard_map/ppermute | solution.py:131
  664.0 33.8 %collective-permute-start.87 = (bf16[96,1728]{0,1:T(8,128)(2,1)}, bf16[96,1728]{0,1:T(8,128)(2,1)}, u32[]{:S(2)}, u32[]{:S(2)}) collective-permute-start(bf16[96,1728]{0,1:T(8,128)(2,1)} %get-tuple-element.170), channel_id=1, source_target_pairs={{0,8},{8,16},{16,24},{24,28},{28,20},{20,12},{12,4},{4,0},{1,9},{9... | collective-permute-start | bytes 995336 | tf_op jit(solution)/shard_map/ppermute | solution.py:131
  664.7 33.8 %collective-permute-start.94 = (bf16[96,1728]{0,1:T(8,128)(2,1)}, bf16[96,1728]{0,1:T(8,128)(2,1)}, u32[]{:S(2)}, u32[]{:S(2)}) collective-permute-start(bf16[96,1728]{0,1:T(8,128)(2,1)} %get-tuple-element.171), channel_id=1, source_target_pairs={{8,0},{16,8},{24,16},{28,24},{20,28},{12,20},{4,12},{0,4},{9,1},{1... | collective-permute-start | bytes 995336 | tf_op jit(solution)/shard_map/ppermute | solution.py:131
  680.6 63.9 %collective-permute-start.31 = (bf16[256,1536]{1,0:T(8,128)(2,1)}, bf16[256,1536]{1,0:T(8,128)(2,1)}, u32[]{:S(2)}, u32[]{:S(2)}) collective-permute-start(bf16[256,1536]{1,0:T(8,128)(2,1)} %slice.414), channel_id=1, source_target_pairs={{0,1},{1,0},{2,3},{3,2},{4,5},{5,4},{6,7},{7,6},{8,9},{9,8},{10,11... | collective-permute-start | bytes 2359304 | tf_op jit(solution)/shard_map/ppermute | solution.py:58
  744.4 23.3 %collective-permute-start.75 = (bf16[96,1728]{0,1:T(8,128)(2,1)S(1)}, bf16[96,1728]{0,1:T(8,128)(2,1)S(1)}, u32[]{:S(2)}, u32[]{:S(2)}) collective-permute-start(bf16[96,1728]{0,1:T(8,128)(2,1)S(1)} %get-tuple-element.198), channel_id=1, source_target_pairs={{0,8},{8,16},{16,24},{24,28},{28,20},{20,12},{12,4},{4,0},{1,9},{9... | collective-permute-start | bytes 995336 | tf_op jit(solution)/shard_map/ppermute | solution.py:131
  772.9 23.3 %collective-permute-start.76 = (bf16[96,1728]{0,1:T(8,128)(2,1)S(1)}, bf16[96,1728]{0,1:T(8,128)(2,1)S(1)}, u32[]{:S(2)}, u32[]{:S(2)}) collective-permute-start(bf16[96,1728]{0,1:T(8,128)(2,1)S(1)} %get-tuple-element.196), channel_id=1, source_target_pairs={{0,8},{8,16},{16,24},{24,28},{28,20},{20,12},{12,4},{4,0},{1,9},{9... | collective-permute-start | bytes 995336 | tf_op jit(solution)/shard_map/ppermute | solution.py:131
  801.3 23.3 %collective-permute-start.77 = (bf16[96,1728]{0,1:T(8,128)(2,1)S(1)}, bf16[96,1728]{0,1:T(8,128)(2,1)S(1)}, u32[]{:S(2)}, u32[]{:S(2)}) collective-permute-start(bf16[96,1728]{0,1:T(8,128)(2,1)S(1)} %get-tuple-element.194), channel_id=1, source_target_pairs={{0,8},{8,16},{16,24},{24,28},{28,20},{20,12},{12,4},{4,0},{1,9},{9... | collective-permute-start | bytes 995336 | tf_op jit(solution)/shard_map/ppermute | solution.py:131
  809.1 59.7 %collective-permute-start.34 = (bf16[256,1536]{1,0:T(8,128)(2,1)S(1)}, bf16[256,1536]{1,0:T(8,128)(2,1)S(1)}, u32[]{:S(2)}, u32[]{:S(2)}) collective-permute-start(bf16[256,1536]{1,0:T(8,128)(2,1)S(1)} %pad_maximum_fusion.24), channel_id=1, source_target_pairs={{0,1},{1,0},{2,3},{3,2},{4,5},{5,4},{6,7},{7,6},{8,9},{9,8},{10,11... | collective-permute-start | bytes 2359304 | tf_op jit(solution)/shard_map/ppermute | solution.py:58
  853.0 36.9 %collective-permute-start.65 = (bf16[96,1728]{0,1:T(8,128)(2,1)S(1)}, bf16[96,1728]{0,1:T(8,128)(2,1)S(1)}, u32[]{:S(2)}, u32[]{:S(2)}) collective-permute-start(bf16[96,1728]{0,1:T(8,128)(2,1)S(1)} %get-tuple-element.174), channel_id=1, source_target_pairs={{0,8},{8,16},{16,24},{24,28},{28,20},{20,12},{12,4},{4,0},{1,9},{9... | collective-permute-start | bytes 995336 | tf_op jit(solution)/shard_map/ppermute | solution.py:131
  856.5 33.5 %collective-permute-start.72 = (bf16[96,1728]{0,1:T(8,128)(2,1)S(1)}, bf16[96,1728]{0,1:T(8,128)(2,1)S(1)}, u32[]{:S(2)}, u32[]{:S(2)}) collective-permute-start(bf16[96,1728]{0,1:T(8,128)(2,1)S(1)} %get-tuple-element.175), channel_id=1, source_target_pairs={{8,0},{16,8},{24,16},{28,24},{20,28},{12,20},{4,12},{0,4},{9,1},{1... | collective-permute-start | bytes 995336 | tf_op jit(solution)/shard_map/ppermute | solution.py:131
  862.5 38.0 %collective-permute-start.79 = (bf16[96,1728]{0,1:T(8,128)(2,1)S(1)}, bf16[96,1728]{0,1:T(8,128)(2,1)S(1)}, u32[]{:S(2)}, u32[]{:S(2)}) collective-permute-start(bf16[96,1728]{0,1:T(8,128)(2,1)S(1)} %get-tuple-element.190), channel_id=1, source_target_pairs={{0,8},{8,16},{16,24},{24,28},{28,20},{20,12},{12,4},{4,0},{1,9},{9... | collective-permute-start | bytes 995336 | tf_op jit(solution)/shard_map/ppermute | solution.py:131
  866.0 34.6 %collective-permute-start.86 = (bf16[96,1728]{0,1:T(8,128)(2,1)S(1)}, bf16[96,1728]{0,1:T(8,128)(2,1)S(1)}, u32[]{:S(2)}, u32[]{:S(2)}) collective-permute-start(bf16[96,1728]{0,1:T(8,128)(2,1)S(1)} %get-tuple-element.191), channel_id=1, source_target_pairs={{8,0},{16,8},{24,16},{28,24},{20,28},{12,20},{4,12},{0,4},{9,1},{1... | collective-permute-start | bytes 995336 | tf_op jit(solution)/shard_map/ppermute | solution.py:131
  996.5 26.8 %collective-permute-start.39 = (f32[256,1536]{1,0:T(8,128)}, f32[256,1536]{1,0:T(8,128)}, u32[]{:S(2)}, u32[]{:S(2)}) collective-permute-start(f32[256,1536]{1,0:T(8,128)} %pad_maximum_fusion.13), channel_id=1, source_target_pairs={{0,1},{1,0},{2,3},{3,2},{4,5},{5,4},{6,7},{7,6},{8,9},{9,8},{10,11... | collective-permute-start | bytes 4718600 | tf_op jit(solution)/shard_map/ppermute | solution.py:58
  (317 other events, 4003.7 us)

commit v2 on v1

v2 whole, which is shorter than its diff:
```python
import jax
import jax.numpy as jnp
from jax import lax
from jax.experimental import pallas as pl
from jax.experimental.pallas import tpu as pltpu
from jax.sharding import PartitionSpec as P

HEAD = 64
KW = 3
SPAN = 4
GROUP = 3


EPSILON = 1e-05
THETA = 1000000.0
BF16 = jnp.bfloat16
F32 = jnp.float32


def matmul(left, right):
    return jnp.dot(left, right, preferred_element_type=F32)


def outer_sum(left, right):
    return lax.dot_general(left, right, (((0,), (0,)), ((), ())), preferred_element_type=F32)


def inner_back(left, right):
    return lax.dot_general(left, right, (((1,), (1,)), ((), ())), preferred_element_type=F32)


def normalize(values, gain):
    inverse = lax.rsqrt(jnp.mean(values * values, axis=-1, keepdims=True) + EPSILON)
    return (values * inverse * gain, inverse)


def normalize_back(values, inverse, gain, grad_result):
    weighted = grad_result * gain
    grad_gain = jnp.sum(grad_result * values * inverse, axis=tuple(range(values.ndim - 1)))
    inner = jnp.mean(weighted * values, axis=-1, keepdims=True)
    grad_values = inverse * (weighted - values * inverse * inverse * inner)
    return (grad_values, grad_gain)


def rotate(values, cosine, sine_table):
    middle = values.shape[-1] // 2
    turned = jnp.concatenate([-values[..., middle:], values[..., :middle]], axis=-1)
    return values * cosine + turned * sine_table


def rotate_back(grads, cosine, sine_table):
    middle = grads.shape[-1] // 2
    scaled = grads * sine_table
    turned = jnp.concatenate([scaled[..., middle:], -scaled[..., :middle]], axis=-1)
    return grads * cosine + turned


def swap(block, axis, bit):
    route = [(i, i ^ bit) for i in range(lax.axis_size(axis))]
    return lax.ppermute(block, axis, route)


CHUNKS = 4
MESH = pl.DeviceIdType.MESH


def greet(peers):
    barrier = pltpu.get_barrier_semaphore()
    for peer in peers:
        pl.semaphore_signal(barrier, inc=1, device_id=peer, device_id_type=MESH)
    pl.semaphore_wait(barrier, len(peers))


def tensor_peers():
    me = lax.axis_index("tensor")
    return [{"tensor": me ^ 1}, {"tensor": me ^ 2}]


def sum_and_gather(partial, gathered, gathered_t, near, across, far, send, recv, compute):
    core, other = tensor_peers()
    quarter = partial.shape[0] // 4
    size = quarter // CHUNKS
    copies = {}

    def copy(kind, at, src, dst, peer):
        number = kind * CHUNKS + at
        made = pltpu.make_async_remote_copy(
            src_ref=src,
            dst_ref=dst,
            send_sem=send.at[number],
            recv_sem=recv.at[number],
            device_id=peer,
            device_id_type=MESH,
        )
        made.start()
        copies[kind, at] = made

    def part(block, at):
        return pl.ds(block * quarter + at * size, size)

    def turn(block):
        if gathered_t is not None:
            rows = slice(block * quarter, (block + 1) * quarter)
            gathered_t[:, rows] = gathered[rows, :].T

    for at in range(CHUNKS):
        copy(0, at, partial.at[part(3, at)], near.at[part(1, at)], core)
    for at in range(CHUNKS):
        copy(1, at, partial.at[part(2, at)], near.at[part(0, at)], core)
    for at in range(CHUNKS):
        copies[0, at].wait_recv()
        far[part(0, at), :] = (
            partial[part(1, at), :].astype(F32) + near[part(1, at), :].astype(F32)
        ).astype(BF16)
        copy(2, at, far.at[part(0, at)], across.at[part(0, at)], other)
    for at in range(CHUNKS):
        copies[1, at].wait_recv()
        copies[2, at].wait_recv()
        total = (
            partial[part(0, at), :].astype(F32)
            + near[part(0, at), :].astype(F32)
            + across[part(0, at), :].astype(F32)
        )
        gathered[part(0, at), :] = compute(total, part(0, at), at == 0)
        copy(3, at, gathered.at[part(0, at)], gathered.at[part(1, at)], other)
        copy(4, at, gathered.at[part(0, at)], gathered.at[part(2, at)], core)
    turn(0)
    for at in range(CHUNKS):
        copies[3, at].wait_recv()
        copy(5, at, gathered.at[part(1, at)], gathered.at[part(3, at)], core)
    turn(1)
    for at in range(CHUNKS):
        copies[4, at].wait_recv()
    turn(2)
    for at in range(CHUNKS):
        copies[5, at].wait_recv()
    turn(3)
    for made in copies.values():
        made.wait_send()


def exchange_scratch(rows, width):
    quarter = rows // 4
    return [
        pltpu.VMEM((2 * quarter, width), BF16),
        pltpu.VMEM((quarter, width), BF16),
        pltpu.VMEM((quarter, width), BF16),
        pltpu.SemaphoreType.DMA((6 * CHUNKS,)),
        pltpu.SemaphoreType.DMA((6 * CHUNKS,)),
    ]


def spread(partial_b, extras, out_shapes, compute, collective_id):
    rows, width = partial_b.shape
    quarter = rows // 4

    def body(*refs):
        partial = refs[0]
        extra_refs = refs[1 : 1 + len(extras)]
        gathered, gathered_t = refs[1 + len(extras) : 3 + len(extras)]
        out_refs = refs[3 + len(extras) : 3 + len(extras) + len(out_shapes)]
        scratch = refs[3 + len(extras) + len(out_shapes) :]
        greet(tensor_peers())
        sum_and_gather(
            partial, gathered, gathered_t, *scratch,
            lambda total, at, first: compute(total, at, extra_refs, out_refs, first),
        )

    vmem = pl.BlockSpec(memory_space=pltpu.VMEM)
    return pl.pallas_call(
        body,
        in_specs=[vmem] * (1 + len(extras)),
        out_specs=[vmem] * (2 + len(out_shapes)),
        out_shape=[
            jax.ShapeDtypeStruct((rows, width), BF16),
            jax.ShapeDtypeStruct((width, rows), BF16),
        ]
        + [jax.ShapeDtypeStruct(shape, F32) for shape in out_shapes],
        scratch_shapes=exchange_scratch(rows, width),
        compiler_params=pltpu.CompilerParams(
            collective_id=collective_id, has_side_effects=True, vmem_limit_bytes=32 * 2**20
        ),
        cost_estimate=pl.CostEstimate(
            flops=20 * quarter * width, bytes_accessed=8 * rows * width, transcendentals=0
        ),
    )(partial_b, *extras)


def norm_spread(partial_b, residual, gain):
    def compute(total, rows, extra_refs, out_refs, first):
        hidden = extra_refs[0][rows, :] + total
        out_refs[0][rows, :] = hidden
        return normalize(hidden, extra_refs[1][...])[0].astype(BF16)

    return spread(partial_b, [residual, gain.reshape(1, -1)], [residual.shape], compute, 1)


def row_back(total, rows, first, hidden, gain, incoming, own, grad_gain):
    values = hidden[rows, :]
    inverse = lax.rsqrt(jnp.mean(values * values, axis=-1, keepdims=True) + EPSILON)
    made, term = normalize_back(values, inverse, gain[...], total)
    made = made + incoming[rows, :]
    if own is not None:
        own[rows, :] = made
    term = term.reshape(1, -1)
    grad_gain[...] = term if first else grad_gain[...] + term
    return made.astype(BF16)


def back_spread(partial_b, hidden, gain, incoming):
    def compute(total, rows, extra_refs, out_refs, first):
        return row_back(total, rows, first, *extra_refs, *out_refs)

    gathered, gathered_t, own, grad_gain = spread(
        partial_b,
        [hidden, gain.reshape(1, -1), incoming],
        [hidden.shape, (1, hidden.shape[1])],
        compute,
        3,
    )
    return gathered, gathered_t, own, grad_gain


def ring_peers(count):
    me = lax.axis_index("dp")
    even = lax.rem(me, 2) == 0
    place = jnp.where(even, me // 2, count - 1 - me // 2)

    def at(position):
        position = lax.rem(position + count, count)
        return jnp.where(position < count // 2, 2 * position, 2 * (count - 1 - position) + 1)

    return at(place + 1), at(place - 1), lambda distance: at(place + distance)


def finish(segments, small, last_partial, hidden, gain, incoming, out_partial, out_hidden, devices, sides):
    width, tokens = segments[0][0][0].shape
    rows = width // devices
    half = rows // sides
    steps = devices - 1
    row_count = last_partial.shape[0]
    lefts, rights = [], []
    plan = []
    for pairs in segments:
        entry = []
        for left, right in pairs:
            if not any(left is o for o in lefts):
                lefts.append(left)
            rights.append(right)
            entry.append(([o is left for o in lefts].index(True), len(rights) - 1))
        plan.append(entry)
    widths = [sum(right.shape[1] for _, right in pairs) for pairs in segments]
    count = len(segments)
    bits = []
    bit = 1
    while bit < devices:
        bits.append(bit)
        bit *= 2
    stages = 2 + len(bits)
    inputs = lefts + rights + [small, last_partial, hidden, gain.reshape(1, -1), incoming, out_partial, out_hidden]

    def body(*refs):
        left_refs = refs[: len(lefts)]
        right_refs = refs[len(lefts) : len(lefts) + len(rights)]
        refs = refs[len(lefts) + len(rights) :]
        small_ref, last_ref, hidden_ref, gain_ref, incoming_ref, outp_ref, outh_ref = refs[:7]
        sums = refs[7 : 7 + count]
        input_grad, output, small_out = refs[7 + count : 10 + count]
        held = refs[10 + count : 10 + 2 * count]
        (send, recv, near, across, far, x_send, x_recv, near2, across2, far2, y_send, y_recv,
         gain_term, slots, s_send, s_recv) = refs[10 + 2 * count :]
        following, previous, owner_at = ring_peers(devices)
        me = lax.axis_index("dp")
        small_peers = tensor_peers() + [{"dp": me ^ bit} for bit in bits]
        greet([{"dp": following}, {"dp": previous}] + small_peers)

        def copy(seg, side, step):
            number = (seg * sides + side) * steps + step
            return pltpu.make_async_remote_copy(
                src_ref=held[seg].at[side, step],
                dst_ref=held[seg].at[side, step + 1],
                send_sem=send.at[number],
                recv_sem=recv.at[number],
                device_id={"dp": following if side == 0 else previous},
                device_id_type=MESH,
            )

        def unit(seg, step, first=False, last=False):
            starts = []
            for side in range(sides):
                if last:
                    owner = me
                else:
                    owner = owner_at(-1 - step if side == 0 else 1 + step)
                starts.append(pl.multiple_of(owner * rows + side * half, 16))
            if not first:
                for side in range(sides):
                    copy(seg, side, step - 1).wait_recv()
            column = 0
            for left, right in plan[seg]:
                pieces = [left_refs[left][pl.ds(start, half), :] for start in starts]
                piece = pieces[0] if sides == 1 else jnp.concatenate(pieces, axis=0)
                made = jnp.dot(piece, right_refs[right][...], preferred_element_type=F32)
                at = slice(column, column + made.shape[1])
                for side in range(sides):
                    value = made[side * half : (side + 1) * half]
                    if not first:
                        value = value + held[seg][side, step, :, at].astype(F32)
                    if last:
                        sums[seg][side * half : (side + 1) * half, at] = value
                    else:
                        held[seg][side, step, :, at] = value.astype(BF16)
                column += made.shape[1]
            if not last:
                for side in range(sides):
                    copy(seg, side, step).start()

        for seg in range(count):
            unit(seg, 0, first=True)
        sum_and_gather(
            last_ref, input_grad, None, near, across, far, x_send, x_recv,
            lambda total, at, first: row_back(
                total, at, first, hidden_ref, gain_ref, incoming_ref, None, gain_term
            ),
        )
        if steps > 1:
            for seg in range(count):
                unit(seg, 1)
        sum_and_gather(
            outp_ref, output, None, near2, across2, far2, y_send, y_recv,
            lambda total, at, first: (outh_ref[at, :] + total).astype(BF16),
        )
        if steps > 2:
            for seg in range(count):
                unit(seg, 2)
        small_out[...] = small_ref[...]
        small_out[0:1, :] = gain_term[...]
        row = lax.broadcasted_iota(jnp.int32, small.shape, 0)
        for stage in range(stages):
            made = pltpu.make_async_remote_copy(
                src_ref=small_out,
                dst_ref=slots.at[stage],
                send_sem=s_send.at[stage],
                recv_sem=s_recv.at[stage],
                device_id=small_peers[stage],
                device_id_type=MESH,
            )
            made.start()
            made.wait()
            if stage < 2:
                small_out[...] += jnp.where(row < 5, slots[stage], 0.0)
            else:
                small_out[...] += slots[stage]

        @pl.loop(3, steps)
        def _(step):
            for seg in range(count):
                unit(seg, step)

        for seg in range(count):
            unit(seg, steps, last=True)

        @pl.loop(0, steps)
        def _(step):
            for seg in range(count):
                for side in range(sides):
                    copy(seg, side, step).wait_send()

    vmem = pl.BlockSpec(memory_space=pltpu.VMEM)
    copies = count * sides * steps
    return pl.pallas_call(
        body,
        in_specs=[vmem] * len(inputs),
        out_specs=[vmem] * (count + 3),
        out_shape=[jax.ShapeDtypeStruct((rows, w), F32) for w in widths]
        + [jax.ShapeDtypeStruct((row_count, width), BF16)] * 2
        + [jax.ShapeDtypeStruct(small.shape, F32)],
        scratch_shapes=[pltpu.VMEM((sides, devices, half, w), BF16) for w in widths]
        + [pltpu.SemaphoreType.DMA((copies,)), pltpu.SemaphoreType.DMA((copies,))]
        + exchange_scratch(row_count, width)
        + exchange_scratch(row_count, width)
        + [
            pltpu.VMEM((1, width), F32),
            pltpu.VMEM((stages,) + small.shape, F32),
            pltpu.SemaphoreType.DMA((stages,)),
            pltpu.SemaphoreType.DMA((stages,)),
        ],
        compiler_params=pltpu.CompilerParams(
            collective_id=4, has_side_effects=True, vmem_limit_bytes=62 * 2**20
        ),
    )(*inputs)


def block_owners(index):
    return [index, index ^ 2, index ^ 1, index ^ 3]


def to_local(values, index):
    quarter = values.shape[0] // 4
    return jnp.concatenate(
        [lax.dynamic_slice_in_dim(values, o * quarter, quarter) for o in block_owners(index)]
    )


def to_true(values, index):
    quarter = values.shape[0] // 4
    places = []
    for block in range(4):
        shift = block ^ index
        place = ((shift & 1) << 1) | (shift >> 1)
        places.append(lax.dynamic_slice_in_dim(values, place * quarter, quarter))
    return jnp.concatenate(places)


def ring_order(count):
    return list(range(0, count, 2)) + [i for i in range(count - 1, -1, -1) if i % 2 == 1]


class Ring:
    def __init__(self, count):
        self.count = count
        self.order = ring_order(count)
        place = [0] * count
        for at, device in enumerate(self.order):
            place[device] = at
        self.place = jnp.array(place, jnp.int32)[lax.axis_index("dp")]
        self.table = jnp.array(self.order, jnp.int32)
        pairs = [(self.order[i], self.order[(i + 1) % count]) for i in range(count)]
        self.routes = (pairs, [(b, a) for a, b in pairs])

    def owner(self, distance):
        return self.table[lax.rem(self.place + distance + self.count, self.count)]


def piece_plan(width, devices):
    rows = width // devices
    return (2, 2) if rows % 64 == 0 else (1, 1)


def outer_pieces(pairs, devices, parts, sides, stack):
    tokens, width = pairs[0][0].shape
    rows = width // devices
    pieces = parts * sides
    size = rows // pieces
    step = max(rows, 384 // rows * rows)
    while width % step:
        step -= rows
    owners = step // rows
    lefts = []
    for left, _ in pairs:
        if not any(left is o for o in lefts):
            lefts.append(left)
    which = [[o is left for o in lefts].index(True) for left, _ in pairs]
    widths = [right.shape[1] for _, right in pairs]
    count = len(pairs)
    if stack:
        shape = (devices * pieces, size * count, widths[0])
    else:
        shape = (devices * pieces, size, sum(widths))

    def body(*refs):
        left_refs, right_refs, out = refs[: len(lefts)], refs[len(lefts) : -1], refs[-1]
        column = 0
        for at in range(count):
            made = lax.dot_general(
                left_refs[which[at]][...],
                right_refs[at][...],
                (((0,), (0,)), ((), ())),
                preferred_element_type=F32,
            ).astype(BF16)
            for piece in range(owners * pieces):
                value = made[piece * size : (piece + 1) * size]
                if stack:
                    out[piece, at * size : (at + 1) * size, :] = value
                else:
                    out[piece, :, column : column + widths[at]] = value
            column += widths[at]

    block = (owners * pieces,) + shape[1:]
    return pl.pallas_call(
        body,
        grid=(width // step,),
        in_specs=[pl.BlockSpec((tokens, step), lambda i: (0, i)) for _ in lefts]
        + [pl.BlockSpec((tokens, w), lambda i: (0, 0)) for w in widths],
        out_specs=pl.BlockSpec(block, lambda i: (i, 0, 0)),
        out_shape=jax.ShapeDtypeStruct(shape, BF16),
        compiler_params=pltpu.CompilerParams(vmem_limit_bytes=56 * 2**20),
        cost_estimate=pl.CostEstimate(
            flops=2 * tokens * width * sum(widths),
            bytes_accessed=2 * width * sum(widths) + 2 * tokens * (width + sum(widths)),
            transcendentals=0,
        ),
    )(*lefts, *[right for _, right in pairs])


class Job:
    def __init__(self, ring, arrays, part, parts, sides):
        self.ring, self.arrays = ring, arrays
        self.part, self.parts, self.sides = part, parts, sides
        self.step = 0
        self.held = None
        self.sums = None

    def terms(self, side):
        ring = self.ring
        if self.step < ring.count - 1:
            owner = ring.owner((self.step + 1) * (-1 if side == 0 else 1))
        else:
            owner = lax.axis_index("dp")
        at = (owner * self.parts + self.part) * self.sides + side
        return [lax.dynamic_index_in_dim(g, at, keepdims=False) for g in self.arrays]

    def advance(self, tied):
        last = self.step == self.ring.count - 1
        if self.held is not None:
            self.held, tied = lax.optimization_barrier((self.held, tied))
        totals = []
        for side in range(self.sides):
            terms = self.terms(side)
            if self.held is not None:
                terms = [h.astype(F32) + t.astype(F32) for h, t in zip(self.held[side], terms)]
            totals.append(terms)
        self.step += 1
        if last:
            self.sums = totals
            return tied
        totals = [[t.astype(BF16) for t in side] for side in totals]
        totals, tied = lax.optimization_barrier((totals, tied))
        self.held = [
            [lax.ppermute(t, "dp", self.ring.routes[side]) for t in totals[side]]
            for side in range(self.sides)
        ]
        return tied

    def result(self, at, stacked=1):
        found = []
        for number in range(stacked):
            pieces = []
            for side in range(self.sides):
                value = self.sums[side][at]
                size = value.shape[0] // stacked
                pieces.append(value[number * size : (number + 1) * size])
            found.append(jnp.concatenate(pieces, axis=0))
        return found


def drive(main):
    jobs, turn, tied = [], 0, None
    running = True
    while running or jobs:
        if running:
            try:
                made = main.send(tied)
            except StopIteration as stop:
                outcome, running, tied = stop.value, False, None
            else:
                tied = made
                if isinstance(made, Job):
                    jobs.append(made)
                    continue
        if jobs:
            job = jobs[turn % len(jobs)]
            tied = job.advance(tied)
            if job.sums is None:
                turn += 1
            else:
                jobs.remove(job)
    return outcome


def split_gate_up(weight):
    return weight[:, 0, :], weight[:, 1, :]


def head_columns(ref, head):
    return ref[:, head * HEAD : (head + 1) * HEAD]


def cross(left, right):
    return lax.dot_general(left, right, (((1,), (1,)), ((), ())), preferred_element_type=F32)


def fill_bias(bias, length_ref, row_positions, column_positions):
    keys = column_positions[...]
    allowed = (keys <= row_positions[...]) & (keys < length_ref[0])
    bias[...] = jnp.where(allowed, 0.0, -1e30)


def attention_forward(query, pieces, place, length, positions):
    rows, columns = query.shape
    heads = columns // HEAD
    kv_columns = heads // GROUP * HEAD
    count = len(pieces)

    def body(place_ref, length_ref, row_pos, column_pos, q_ref, *refs):
        piece_refs, (out, out_t, log_total, near, bias, total_ref) = refs[:count], refs[count:]
        for at in range(1, count):
            near[at] = piece_refs[at][...]
        fill_bias(bias, length_ref, row_pos, column_pos)

        def part(q, keys, values_t, masked):
            scores = cross(keys, q)
            if masked:
                scores = scores + bias[...]
            expo = jnp.exp(scores)
            return (
                jnp.dot(values_t, expo.astype(BF16), preferred_element_type=F32),
                jnp.sum(expo, axis=0, keepdims=True),
            )

        for head in range(heads):
            first = head // GROUP * HEAD
            q = head_columns(q_ref, head)
            keys = piece_refs[0][:, first : first + HEAD]
            values = piece_refs[0][:, kv_columns + first : kv_columns + first + HEAD]
            made, total = part(q, keys, values.T, True)
            out_t[head * HEAD : (head + 1) * HEAD, :] = made
            total_ref[...] = total

            @pl.loop(1, place_ref[0] + 1)
            def _(at):
                keys = near[at, :, first : first + HEAD]
                values = near[at, :, kv_columns + first : kv_columns + first + HEAD]
                made, total = part(q, keys, values.T, False)
                out_t[head * HEAD : (head + 1) * HEAD, :] += made
                total_ref[...] += total

            total = total_ref[...]
            made = out_t[head * HEAD : (head + 1) * HEAD, :] / total
            out_t[head * HEAD : (head + 1) * HEAD, :] = made
            out[:, head * HEAD : (head + 1) * HEAD] = made.T.astype(BF16)
            log_total[head : head + 1, :] = jnp.log(total)

    vmem = pl.BlockSpec(memory_space=pltpu.VMEM)
    smem = pl.BlockSpec(memory_space=pltpu.SMEM)
    return pl.pallas_call(
        body,
        in_specs=[smem, smem] + [vmem] * (3 + count),
        out_specs=[vmem] * 3,
        out_shape=[
            jax.ShapeDtypeStruct((rows, columns), BF16),
            jax.ShapeDtypeStruct((columns, rows), F32),
            jax.ShapeDtypeStruct((heads, rows), F32),
        ],
        scratch_shapes=[
            pltpu.VMEM((count, rows, 2 * kv_columns), BF16),
            pltpu.VMEM((rows, rows), F32),
            pltpu.VMEM((1, rows), F32),
        ],
        compiler_params=pltpu.CompilerParams(vmem_limit_bytes=48 * 2**20),
        cost_estimate=pl.CostEstimate(
            flops=4 * rows * rows * count * columns * 4,
            bytes_accessed=10 * rows * columns,
            transcendentals=rows * rows * count * heads,
        ),
    )(
        place.reshape(1),
        length.reshape(1),
        positions.reshape(1, rows),
        positions.reshape(rows, 1),
        query,
        *pieces,
    )


def attention_backward(query, pieces, out_t, log_total, grad, place, length, positions):
    rows, columns = query.shape
    heads = columns // HEAD
    kv_heads = heads // GROUP
    kv_columns = kv_heads * HEAD
    count = len(pieces)

    def body(place_ref, length_ref, row_pos, column_pos, q_ref, o_ref, log_ref, g_ref, *refs):
        piece_refs, (grad_q, own, far, near, bias, grad_q_t, delta) = refs[:count], refs[count:]
        for at in range(1, count):
            near[at] = piece_refs[at][...]
        fill_bias(bias, length_ref, row_pos, column_pos)
        grad_q_t[...] = jnp.zeros_like(grad_q_t)
        for head in range(heads):
            at = slice(head * HEAD, (head + 1) * HEAD)
            grad_t = g_ref[:, at].astype(F32).T
            delta[head : head + 1, :] = jnp.sum(grad_t * o_ref[at, :], axis=0, keepdims=True)

        def part(read, write, masked):
            for group in range(kv_heads):
                first = group * HEAD
                keys = read(first)
                values = read(kv_columns + first)
                keys_t = keys.T
                grad_k = grad_v = None
                for head in range(group * GROUP, (group + 1) * GROUP):
                    at = slice(head * HEAD, (head + 1) * HEAD)
                    q, grads = q_ref[:, at], g_ref[:, at]
                    scores = cross(keys, q) - log_ref[head : head + 1, :]
                    if masked:
                        scores = scores + bias[...]
                    probs = jnp.exp(scores)
                    made = jnp.dot(probs.astype(BF16), grads, preferred_element_type=F32)
                    grad_v = made if grad_v is None else grad_v + made
                    grad_probs = cross(values, grads)
                    grad_scores = (probs * (grad_probs - delta[head : head + 1, :])).astype(BF16)
                    made = jnp.dot(grad_scores, q, preferred_element_type=F32)
                    grad_k = made if grad_k is None else grad_k + made
                    grad_q_t[at, :] += jnp.dot(keys_t, grad_scores, preferred_element_type=F32)
                write(first, grad_k)
                write(kv_columns + first, grad_v)

        def write_own(column, value):
            own[:, column : column + HEAD] = value

        part(lambda column: piece_refs[0][:, column : column + HEAD], write_own, True)

        @pl.loop(1, place_ref[0] + 1)
        def _(at):
            def write_far(column, value):
                far[at - 1, :, column : column + HEAD] = value.astype(BF16)

            part(lambda column: near[at, :, column : column + HEAD], write_far, False)

        for head in range(heads):
            at = slice(head * HEAD, (head + 1) * HEAD)
            grad_q[:, at] = grad_q_t[at, :].T * HEAD ** (-0.5)

    vmem = pl.BlockSpec(memory_space=pltpu.VMEM)
    smem = pl.BlockSpec(memory_space=pltpu.SMEM)
    return pl.pallas_call(
        body,
        in_specs=[smem, smem] + [vmem] * (6 + count),
        out_specs=[vmem] * 3,
        out_shape=[
            jax.ShapeDtypeStruct((rows, columns), F32),
            jax.ShapeDtypeStruct((rows, 2 * kv_columns), F32),
            jax.ShapeDtypeStruct((count - 1, rows, 2 * kv_columns), BF16),
        ],
        scratch_shapes=[
            pltpu.VMEM((count, rows, 2 * kv_columns), BF16),
            pltpu.VMEM((rows, rows), F32),
            pltpu.VMEM((columns, rows), F32),
            pltpu.VMEM((heads, rows), F32),
        ],
        compiler_params=pltpu.CompilerParams(vmem_limit_bytes=48 * 2**20),
        cost_estimate=pl.CostEstimate(
            flops=10 * rows * rows * count * columns * 4,
            bytes_accessed=20 * rows * columns,
            transcendentals=rows * rows * count * heads,
        ),
    )(
        place.reshape(1),
        length.reshape(1),
        positions.reshape(1, rows),
        positions.reshape(rows, 1),
        query,
        out_t,
        log_total,
        grad,
        *pieces,
    )


def mlp_hidden(normed_b, gate_w, up_w):
    gate = matmul(normed_b, gate_w)
    upward = matmul(normed_b, up_w)
    active_b = (jax.nn.silu(gate) * upward).astype(BF16)
    return gate, upward, active_b


def mlp_back_hidden(grad_b, down, gate, upward):
    grad_active = inner_back(grad_b, down)
    sigma = jax.nn.sigmoid(gate)
    grad_gate = (grad_active * upward * sigma * (1.0 + gate * (1.0 - sigma))).astype(BF16)
    grad_upward = (grad_active * gate * sigma).astype(BF16)
    return grad_gate, grad_upward


def local(
    tokens,
    lengths,
    norm_conv,
    conv_in,
    conv_kernel,
    conv_out,
    norm_mlp_one,
    gate_up_one,
    down_one,
    norm_attn,
    query_weight,
    kv_weight,
    query_gain,
    key_gain,
    attn_out,
    norm_mlp_two,
    gate_up_two,
    down_two,
    cotangent,
):
    row_count = tokens.shape[0]
    width = tokens.shape[1]
    quarter = row_count // 4
    channels = conv_out.shape[0]
    local_heads = query_weight.shape[1] // HEAD
    local_kv = kv_weight.shape[2] // HEAD
    device = lax.axis_index("dp")
    devices = lax.axis_size("dp")
    index = lax.axis_index("tensor")
    sequence = device // SPAN
    place_index = device % SPAN
    length = lengths[sequence]
    ring = Ring(devices)
    offsets = jnp.concatenate(
        [o * quarter + jnp.arange(quarter, dtype=jnp.int32) for o in block_owners(index)]
    )
    positions = place_index * row_count + offsets
    is_valid = positions < length
    frequency = THETA ** (-2.0 * jnp.arange(HEAD // 2, dtype=jnp.float32) / HEAD)
    angles = positions.astype(jnp.float32)[:, None] * frequency[None, :]
    angles = jnp.concatenate([angles, angles], axis=-1)[:, None, :]
    cosine = jnp.cos(angles)
    sine_table = jnp.sin(angles)
    factor = HEAD ** (-0.5)
    kernel = conv_kernel.astype(jnp.float32)
    rim_rows = KW - 1
    gate_one, up_one = split_gate_up(gate_up_one)
    gate_two, up_two = split_gate_up(gate_up_two)
    forward_route = [(i, i + 1) for i in range(devices - 1) if (i + 1) % SPAN]
    backward_route = [(b, a) for a, b in forward_route]

    inputs = tokens.astype(F32)
    normed_conv, inverse_conv = normalize(inputs, norm_conv)
    normed_conv_b = normed_conv.astype(BF16)
    weight_in = conv_in.reshape(width, 3 * channels)
    projected = matmul(normed_conv_b, weight_in)
    before = projected[:, :channels]
    after = projected[:, channels : 2 * channels]
    signal = projected[:, 2 * channels :]
    mixed = before * signal
    rim_in = lax.ppermute(mixed[row_count - rim_rows :], "dp", forward_route)
    padded = jnp.concatenate([rim_in, mixed], axis=0)
    convolved = kernel[0] * padded[0:row_count]
    for offset in range(1, KW):
        convolved = convolved + kernel[offset] * padded[offset : offset + row_count]
    gated_b = to_local((after * convolved).astype(BF16), index)
    inputs_own = lax.dynamic_slice_in_dim(tokens, index * quarter, quarter).astype(F32)

    norm_one_b, norm_one_t, one_own = norm_spread(
        matmul(gated_b, conv_out).astype(BF16), inputs_own, norm_mlp_one
    )
    gate_a, up_a, active_one = mlp_hidden(norm_one_b, gate_one, up_one)

    normed_attn_b, normed_attn_t, two_own = norm_spread(
        matmul(active_one, down_one).astype(BF16), one_own, norm_attn
    )
    kv_flat = kv_weight.reshape(width, 2 * local_kv * HEAD)
    joined = matmul(normed_attn_b, kv_flat)
    key_raw = joined[:, : local_kv * HEAD].reshape(row_count, local_kv, HEAD)
    value_rows = joined[:, local_kv * HEAD :].reshape(row_count, local_kv, HEAD).astype(BF16)
    key_norm, key_inverse = normalize(key_raw, key_gain)
    key_rot = rotate(key_norm, cosine, sine_table).astype(BF16)
    stacked = jnp.concatenate(
        [key_rot.reshape(row_count, -1), value_rows.reshape(row_count, -1)], axis=1
    )
    pieces = [stacked]
    for distance in range(1, SPAN):
        route = [(i, i + distance) for i in range(devices) if i % SPAN + distance < SPAN]
        pieces.append(lax.ppermute(stacked, "dp", route))
    query_raw = matmul(normed_attn_b, query_weight).reshape(row_count, local_heads, HEAD)
    query_norm, query_inverse = normalize(query_raw, query_gain)
    query_rot = rotate(query_norm, cosine, sine_table).astype(BF16)
    query_b = (query_rot * factor).astype(BF16).reshape(row_count, local_heads * HEAD)
    attended_b, attended_t, log_total = attention_forward(
        query_b, pieces, place_index, length, positions
    )
    norm_two_b, _, three_own = norm_spread(
        matmul(attended_b, attn_out).astype(BF16), two_own, norm_mlp_two
    )
    gate_b, up_b, active_two = mlp_hidden(norm_two_b, gate_two, up_two)
    grad_result = to_local(cotangent, index).astype(F32) * is_valid[:, None].astype(F32)
    grad_result_b = grad_result.astype(BF16)

    def backward():
        grad_gate, grad_up = mlp_back_hidden(grad_result_b, down_two, gate_b, up_b)
        parts, sides = 1, piece_plan(width, devices)[1]
        two_grads = outer_pieces(
            [(grad_result_b, active_two), (norm_two_b, grad_gate), (norm_two_b, grad_up)],
            devices, parts, sides, True,
        )
        jobs_two = [Job(ring, [two_grads], part, parts, sides) for part in range(parts)]
        for job in jobs_two:
            yield job
        grad_gate, grad_up = yield (grad_gate, grad_up)
        partial_normed = inner_back(grad_gate, gate_two) + inner_back(grad_up, up_two)

        partial_b = yield partial_normed.astype(BF16)
        grad_branch, grad_branch_t, grad_three, grad_norm_mlp_two = back_spread(
            partial_b, three_own, norm_mlp_two, grad_result[:quarter]
        )
        grad_branch = yield grad_branch

        grad_attended = inner_back(grad_branch, attn_out).astype(BF16)
        grad_attended = yield grad_attended
        grad_query, owned, grad_far = attention_backward(
            query_b, pieces, attended_t, log_total, grad_attended, place_index, length, positions
        )
        grad_query, owned, grad_far = yield (grad_query, owned, grad_far)
        grad_query = grad_query.reshape(row_count, local_heads, HEAD)
        arrived = []
        for distance in range(1, SPAN):
            route = [(i + distance, i) for i in range(devices) if i % SPAN + distance < SPAN]
            arrived.append(lax.ppermute(grad_far[distance - 1], "dp", route))
        grad_query_raw, part_query_gain = normalize_back(
            query_raw, query_inverse, query_gain, rotate_back(grad_query, cosine, sine_table)
        )
        yield ()
        for piece in arrived:
            owned = owned + piece.astype(F32)
        grad_key = owned[:, : local_kv * HEAD].reshape(row_count, local_kv, HEAD)
        grad_key_raw, part_key_gain = normalize_back(
            key_raw, key_inverse, key_gain, rotate_back(grad_key, cosine, sine_table)
        )
        grad_query_b = grad_query_raw.reshape(row_count, local_heads * HEAD).astype(BF16)
        grad_joined_b = jnp.concatenate(
            [
                grad_key_raw.reshape(row_count, local_kv * HEAD),
                owned[:, local_kv * HEAD :],
            ],
            axis=1,
        ).astype(BF16)
        grad_query_b, grad_joined_b = yield (grad_query_b, grad_joined_b)
        partial_normed = inner_back(grad_query_b, query_weight) + inner_back(grad_joined_b, kv_flat)

        partial_b = yield partial_normed.astype(BF16)
        grad_two_b, grad_two_t, grad_two, grad_norm_attn = back_spread(
            partial_b, two_own, norm_attn, grad_three
        )
        grad_two_b = yield grad_two_b

        grad_gate, grad_up = mlp_back_hidden(grad_two_b, down_one, gate_a, up_a)
        grad_gate, grad_up = yield (grad_gate, grad_up)
        grad_gate, grad_up = yield (grad_gate, grad_up)
        partial_normed = inner_back(grad_gate, gate_one) + inner_back(grad_up, up_one)
        partial_b = yield partial_normed.astype(BF16)
        grad_one_b, grad_one_t, grad_one, grad_norm_mlp_one = back_spread(
            partial_b, one_own, norm_mlp_one, grad_two
        )
        grad_one_b = yield grad_one_b

        grad_gated = to_true(inner_back(grad_one_b, conv_out), index)
        grad_after = grad_gated * convolved
        grad_convolved = grad_gated * after
        grad_kernel = jnp.stack(
            [
                jnp.sum(grad_convolved * padded[offset : offset + row_count], axis=0)
                for offset in range(KW)
            ]
        )
        grad_padded = jnp.pad(kernel[0] * grad_convolved, ((0, rim_rows), (0, 0)))
        for offset in range(1, KW):
            grad_padded = grad_padded + jnp.pad(
                kernel[offset] * grad_convolved, ((offset, rim_rows - offset), (0, 0))
            )
        rim_back = lax.ppermute(grad_padded[:rim_rows], "dp", backward_route)
        yield ()
        grad_mixed = grad_padded[rim_rows:] + jnp.pad(rim_back, ((row_count - rim_rows, 0), (0, 0)))
        grad_projected = jnp.concatenate(
            [grad_mixed * signal, grad_after, grad_mixed * before], axis=1
        ).astype(BF16)
        partial_b = inner_back(to_local(grad_projected, index), weight_in).astype(BF16)
        partial_b = yield partial_b
        while jobs_two[0].sums is None:
            yield ()
        small = jnp.concatenate(
            [
                jnp.zeros((1, width), F32),
                grad_norm_mlp_one,
                grad_norm_attn,
                grad_norm_mlp_two,
                jnp.pad(
                    jnp.concatenate([part_query_gain, part_key_gain]), (0, width - 2 * HEAD)
                ).reshape(1, width),
                jnp.pad(grad_kernel, ((0, 0), (0, width - channels))),
            ],
            axis=0,
        )
        late_active, partial_b = lax.optimization_barrier((active_two, partial_b))
        out_partial = matmul(late_active, down_two).astype(BF16)
        made = finish(
            [
                [
                    (grad_branch_t, attended_b),
                    (normed_attn_t, grad_query_b),
                    (normed_attn_t, grad_joined_b),
                ],
                [(grad_two_t, active_one)],
                [(norm_one_t, grad_gate)],
                [(norm_one_t, grad_up)],
                [(grad_one_t, gated_b), (normed_conv_b.T, grad_projected)],
            ],
            small,
            partial_b,
            inputs_own,
            norm_conv,
            grad_one,
            out_partial,
            three_own,
            devices,
            sides,
        )
        return made, jobs_two[0].result(0, 3)

    made, sums_two = drive(backward())
    sum_attn, sum_down_one, sum_gate_one, sum_up_one, sum_conv, grad_inputs, output, small = made
    sum_down_two, sum_gate_two, sum_up_two = sums_two
    grad_inputs = to_true(grad_inputs, index).astype(F32)
    output = to_true(output, index)

    out_rows = width // devices
    return (
        output,
        grad_inputs,
        small[0],
        sum_conv[:, channels:].reshape(out_rows, 3, channels),
        small[5:, :channels],
        sum_conv[:, :channels].T,
        small[1],
        jnp.stack([sum_gate_one, sum_up_one], axis=1),
        sum_down_one.T,
        small[2],
        sum_attn[:, local_heads * HEAD : 2 * local_heads * HEAD],
        sum_attn[:, 2 * local_heads * HEAD :].reshape(out_rows, 2, local_kv * HEAD),
        small[4, :HEAD],
        small[4, HEAD : 2 * HEAD],
        sum_attn[:, : local_heads * HEAD].T,
        small[3],
        jnp.stack([sum_gate_two, sum_up_two], axis=1),
        sum_down_two.T,
    )


def solution(mesh):
    in_specs = (
        P("dp", None),
        P(),
        P(),
        P(None, None, "tensor"),
        P(None, "tensor"),
        P("tensor", None),
        P(),
        P(None, None, "tensor"),
        P("tensor", None),
        P(),
        P(None, "tensor"),
        P(None, None, "tensor"),
        P(),
        P(),
        P("tensor", None),
        P(),
        P(None, None, "tensor"),
        P("tensor", None),
        P("dp", None),
    )
    out_specs = (
        P("dp", None),
        P("dp", None),
        P(),
        P("dp", None, "tensor"),
        P(None, "tensor"),
        P("tensor", "dp"),
        P(),
        P("dp", None, "tensor"),
        P("tensor", "dp"),
        P(),
        P("dp", "tensor"),
        P("dp", None, "tensor"),
        P(),
        P(),
        P("tensor", "dp"),
        P(),
        P("dp", None, "tensor"),
        P("tensor", "dp"),
    )
    return jax.shard_map(local, mesh=mesh, in_specs=in_specs, out_specs=out_specs, check_vma=False)
```

time: 1050 us -> 804 us (0.77)
  Pallas kernels: 0 us -> 415 us
  waiting for transfers between devices: 444 us -> 112 us
  matrix products: 213 us -> 81 us
  starting transfers between devices: 163 us -> 34.8 us
  other arithmetic: 135 us -> 58.7 us
  local copies, waits for them, and re-layouts: 60.1 us -> 76.1 us
    pallas_call x0 -> x10, Pallas kernels: none -> 415 us  [the longest x1 256 us: finish(): pl.pallas_call(body, in_specs=[vmem] * len(inputs), out_specs=[vmem] * (c...]
    ppermute x153 -> x18, waiting for transfers between devices: 440 us -> 112 us  [the longest x14 85.3 us: advance(): lax.ppermute(t, 'dp', self.ring.routes[side])]
    dot_general x16 -> x0, matrix products: 136 us -> none  [the longest x1 33 us: local(): jnp.einsum('kgqs,qkgd->skd', grad_scores, grouped, preferred_element_type...]
    ppermute x153 -> x18, starting transfers between devices: 148 us -> 23.2 us  [the longest x14 17.9 us: advance(): lax.ppermute(t, 'dp', self.ring.routes[side])]
    convert_element_type x73 -> x7, other arithmetic: 52 us -> 24.4 us  [the longest x6 22.3 us: advance(): totals = [[t.astype(BF16) for t in side] for side in totals]]
    add x19 -> x5, other arithmetic: 15.9 us -> 3.75 us  [the longest x1 2.55 us: advance(): h.astype(F32) + t.astype(F32)]
    mul x0 -> x10, local copies, waits for them, and re-layouts: none -> 10.7 us  [the longest x6 7.23 us: rotate(): return values * cosine + turned * sine_table]
    concatenate x19 -> x10, other arithmetic: 12.6 us -> 1.98 us  [the longest x1 0.95 us: local(): jnp.concatenate([key_rot.reshape(row_count, -1), value_rows.reshape(row_c...]
  transfers between devices with their start and end apart: 157 -> 22, of which waited for: 107 -> 12; matrix products, arithmetic and copies ran while one was open for 29% -> 7% of each run, Pallas kernels for 0% -> 4%
where the time goes in v2:
time: 804 us; the launch traced here: 799 us
  Pallas kernels  415 us (52%)
  waiting for transfers between devices  112 us (14%)
  matrix products  81 us (10%)
  local copies, waits for them, and re-layouts  76.1 us (9%)
  other arithmetic  58.7 us (7%)
  starting transfers between devices  34.8 us (4%)
  between operations  21.1 us (3%)
    pallas_call x1, Pallas kernels, finish(): pl.pallas_call(body, in_specs=[vmem] * len(inputs), out_specs=[vmem] * (c...  256 us
    pallas_call x6, Pallas kernels, spread(): pl.pallas_call(body, in_specs=[vmem] * (1 + len(extras)), out_specs=[vmem...  135 us
    ppermute x14, waiting for transfers between devices, advance(): lax.ppermute(t, 'dp', self.ring.routes[side])  85.3 us
    dot_general x11, matrix products, matmul(): return jnp.dot(left, right, preferred_element_type=F32)  42.4 us
    dot_general x11, matrix products, inner_back(): lax.dot_general(left, right, (((1,), (1,)), ((), ())), preferred_element_...  38.6 us
    unnamed x269, local copies, waits for them, and re-layouts  32.8 us
    ppermute x3, waiting for transfers between devices, backward(): arrived.append(lax.ppermute(grad_far[distance - 1], 'dp', route))  27.1 us
    convert_element_type x6, other arithmetic, advance(): totals = [[t.astype(BF16) for t in side] for side in totals]  22.3 us
  transfers between devices with their start and end apart: 22, of which 12 were waited for; matrix products, arithmetic and copies ran while one was open for 7% of the time, Pallas kernels for 4%

profile of v2, /device:TPU:0, one launch (start us, length us, event | category | flops | bytes accessed | tf_op | source)
XLA Modules:
  0.0 799.2 jit_solution(15005146731820522882)
XLA Ops:
  2.9 6.2 copy.168
  15.2 5.0 collective-permute-start
  48.9 22.4 %shard_map.340 = (bf16[512,1536]{1,0:T(8,128)(2,1)S(1)}, bf16[1536,512]{1,0:T(8,128)(2,1)S(1)}, f32[128,1536]{1,0:T(8,128)S(1)}) custom-call(bf16[512,1536]{1,0:T(8,128)(2,1)S(1)} %convolution_convert_fusion.2.refs_0_, f32[128,1536]{1,0:T(8,128)S(1)} %get-tuple-element.369.refs_1_.refs_16_, f32[1,1536]{1,0:T(1,128)S(1)} %reshape.452.refs_2_), custom_call_target="tpu_custom_call" | custom-call | flops 3932160 | bytes 6291456 | tf_op jit(solution)/shard_map/pallas_call | solution.py:170
  72.5 5.9 fusion.14
  78.5 5.0 multiply_convert_fusion.5
  86.6 22.4 %shard_map.341 = (bf16[512,1536]{1,0:T(8,128)(2,1)S(1)}, bf16[1536,512]{1,0:T(8,128)(2,1)S(1)}, f32[128,1536]{1,0:T(8,128)S(1)}) custom-call(bf16[512,1536]{1,0:T(8,128)(2,1)S(1)} %convolution_convert_fusion.4.refs_0_, f32[128,1536]{1,0:T(8,128)S(1)} %get-tuple-element.102.refs_1_, f32[1,1536]{1,0:T(1,128)S(1)} %reshape.453.refs_2_), custom_call_target="tpu_custom_call" | custom-call | flops 3932160 | bytes 6291456 | tf_op jit(solution)/shard_map/pallas_call | solution.py:170
  147.8 23.6 %shard_map.343 = (bf16[512,1536]{1,0:T(8,128)(2,1)S(1)}, bf16[1536,512]{1,0:T(8,128)(2,1)}, f32[128,1536]{1,0:T(8,128)S(1)}) custom-call(bf16[512,1536]{1,0:T(8,128)(2,1)S(1)} %convolution_convert_fusion.1.refs_0_, f32[128,1536]{1,0:T(8,128)S(1)} %get-tuple-element.105.refs_1_, f32[1,1536]{1,0:T(1,128)S(1)} %reshape.457.refs_2_), custom_call_target="tpu_custom_call" | custom-call | flops 3932160 | bytes 6291456 | tf_op jit(solution)/shard_map/pallas_call | solution.py:170
  171.4 6.4 fusion.2
  182.8 7.3 multiply_convert_fusion.2
  190.2 14.3 %shard_map.344 = bf16[16,288,1728]{2,1,0:T(8,128)(2,1)} custom-call(bf16[512,1536]{1,0:T(8,128)(2,1)} %get-tuple-element.303.refs_0_, bf16[512,1536]{1,0:T(8,128)(2,1)} %copy-done.28, bf16[512,1728]{1,0:T(8,128)(2,1)} %get-tuple-element.173.refs_2_, bf16[512,1728]{1,0:T(8,128)(2,1)} %get-tuple-element.109.refs_3_, bf16[512,1728]{1,0:T(8,128)(2,1)} %get-tuple-element.110.refs_4_), custom_call_target="tpu_custom_call" | custom-call | flops 8153726976 | bytes 22806528 | tf_op jit(solution)/shard_map/pallas_call | solution.py:480
  206.3 5.3 collective-permute-start.4
  220.8 13.6 %collective-permute-done.4 = bf16[288,1728]{1,0:T(8,128)(2,1)S(1)} collective-permute-done((bf16[288,1728]{1,0:T(8,128)(2,1)S(1)}, bf16[288,1728]{1,0:T(8,128)(2,1)S(1)}, u32[]{:S(2)}, u32[]{:S(2)}) %collective-permute-start.4) | collective-permute-done | bytes 995360 | tf_op jit(solution)/shard_map/ppermute | solution.py:530
  246.1 22.1 %shard_map.345 = (bf16[512,1536]{1,0:T(8,128)(2,1)S(1)}, bf16[1536,512]{1,0:T(8,128)(2,1)S(1)}, f32[128,1536]{1,0:T(8,128)S(1)}, f32[1,1536]{1,0:T(1,128)S(1)}) custom-call(bf16[512,1536]{1,0:T(8,128)(2,1)S(1)} %copy-done.13, f32[128,1536]{1,0:T(8,128)S(1)} %get-tuple-element.115.refs_1_.refs_20_, f32[1,1536]{1,0:T(1,128)S(1)} %reshape.457.refs_2_, ...), custom_call_target="tpu_custom_call" | custom-call | flops 3932160 | bytes 6291456 | tf_op jit(solution)/shard_map/pallas_call | solution.py:170
  282.8 16.0 %collective-permute-done.8 = bf16[288,1728]{1,0:T(8,128)(2,1)} collective-permute-done((bf16[288,1728]{1,0:T(8,128)(2,1)}, bf16[288,1728]{1,0:T(8,128)(2,1)}, u32[]{:S(2)}, u32[]{:S(2)}) %collective-permute-start.8) | collective-permute-done | bytes 995360 | tf_op jit(solution)/shard_map/ppermute | solution.py:530
  304.9 6.3 shard_map.346
  311.2 15.9 %collective-permute-done.10 = bf16[288,1728]{1,0:T(8,128)(2,1)S(1)} collective-permute-done((bf16[288,1728]{1,0:T(8,128)(2,1)S(1)}, bf16[288,1728]{1,0:T(8,128)(2,1)S(1)}, u32[]{:S(2)}, u32[]{:S(2)}) %collective-permute-start.10) | collective-permute-done | bytes 995360 | tf_op jit(solution)/shard_map/ppermute | solution.py:530
  349.6 25.6 %collective-permute-done.16 = bf16[512,256]{1,0:T(8,128)(2,1)S(1)} collective-permute-done((bf16[512,256]{1,0:T(8,128)(2,1)S(1)}, bf16[512,256]{1,0:T(8,128)(2,1)S(1)}, u32[]{:S(2)}, u32[]{:S(2)}) %collective-permute-start.16) | collective-permute-done | bytes 262176 | tf_op jit(solution)/shard_map/ppermute | solution.py:908
  383.8 19.2 %collective-permute-done.14 = bf16[288,1728]{1,0:T(8,128)(2,1)} collective-permute-done((bf16[288,1728]{1,0:T(8,128)(2,1)}, bf16[288,1728]{1,0:T(8,128)(2,1)}, u32[]{:S(2)}, u32[]{:S(2)}) %collective-permute-start.14) | collective-permute-done | bytes 995360 | tf_op jit(solution)/shard_map/ppermute | solution.py:530
  414.5 14.0 %collective-permute-done.19 = bf16[288,1728]{1,0:T(8,128)(2,1)} collective-permute-done((bf16[288,1728]{1,0:T(8,128)(2,1)}, bf16[288,1728]{1,0:T(8,128)(2,1)}, u32[]{:S(2)}, u32[]{:S(2)}) %collective-permute-start.19) | collective-permute-done | bytes 995360 | tf_op jit(solution)/shard_map/ppermute | solution.py:530
  434.1 21.7 %shard_map.347 = (bf16[512,1536]{1,0:T(8,128)(2,1)S(1)}, bf16[1536,512]{1,0:T(8,128)(2,1)S(1)}, f32[128,1536]{1,0:T(8,128)S(1)}, f32[1,1536]{1,0:T(1,128)S(1)}) custom-call(bf16[512,1536]{1,0:T(8,128)(2,1)S(1)} %fusion.39.refs_0_, f32[128,1536]{1,0:T(8,128)S(1)} %copy-done.7, f32[1,1536]{1,0:T(1,128)S(1)} %reshape.453.refs_2_, f32[128,1536]{1,0:T(8,128)S(1)} %copy-done.17), custom_call_target="tpu_custom_call" | custom-call | flops 3932160 | bytes 6291456 | tf_op jit(solution)/shard_map/pallas_call | solution.py:170
  457.0 7.8 multiply_convert_fusion.1
  470.9 22.4 %shard_map.348 = (bf16[512,1536]{1,0:T(8,128)(2,1)S(1)}, bf16[1536,512]{1,0:T(8,128)(2,1)S(1)}, f32[128,1536]{1,0:T(8,128)S(1)}, f32[1,1536]{1,0:T(1,128)S(1)}) custom-call(bf16[512,1536]{1,0:T(8,128)(2,1)S(1)} %fusion.36.refs_0_, f32[128,1536]{1,0:T(8,128)S(1)} %copy-done.5, f32[1,1536]{1,0:T(1,128)S(1)} %copy-done.25, ...), custom_call_target="tpu_custom_call" | custom-call | flops 3932160 | bytes 6291456 | tf_op jit(solution)/shard_map/pallas_call | solution.py:170
  513.1 6.6 convolution_convert_fusion.3.refs_19_
  519.7 255.7 %shard_map.349 = (f32[192,1024]{1,0:T(8,128)}, f32[192,1728]{1,0:T(8,128)}, f32[192,1728]{1,0:T(8,128)}, f32[192,1728]{1,0:T(8,128)}, f32[192,1536]{1,0:T(8,128)...) custom-call(bf16[1536,512]{1,0:T(8,128)(2,1)} %copy-done.10, ...), custom_call_target="tpu_custom_call" | custom-call | tf_op jit(solution)/shard_map/pallas_call | solution.py:371
  (464 shorter events, 207.3 us)
Async XLA Ops:
  0.7 146.1 %copy-start = (bf16[384,1536]{1,0:T(8,128)(2,1)S(1)}, bf16[384,1536]{1,0:T(8,128)(2,1)}, u32[]{:S(2)}) copy-start(bf16[384,1536]{1,0:T(8,128)(2,1)} %param.35) | copy-start | bytes 3538948
  15.2 30.2 %collective-permute-start = (f32[2,384]{1,0:T(2,128)S(1)}, f32[2,384]{1,0:T(2,128)S(1)}, u32[]{:S(2)}, u32[]{:S(2)}) collective-permute-start(f32[2,384]{1,0:T(2,128)S(1)} %slice.207), channel_id=1, source_target_pairs={{0,4},{4,8},{8,12},{16,20},{20,24},{24,28},{1,5},{5,9},{9,13},{17,... | collective-permute-start | bytes 9224 | tf_op jit(solution)/shard_map/ppermute | solution.py:836
  32.7 108.9 %copy-start.20 = (s32[512,1]{1,0:T(8,128)}, s32[512,1]{1,0:T(8,128)S(1)}, u32[]{:S(2)}) copy-start(s32[512,1]{1,0:T(8,128)S(1)} %broadcast_add_fusion.column_pos) | copy-start | bytes 6148
  118.0 23.5 %collective-permute-start.3 = (bf16[512,256]{1,0:T(8,128)(2,1)S(1)}, bf16[512,256]{1,0:T(8,128)(2,1)S(1)}, u32[]{:S(2)}, u32[]{:S(2)}) collective-permute-start(bf16[512,256]{1,0:T(8,128)(2,1)S(1)} %pad_maximum_fusion.8.refs_0_), channel_id=1, source_target_pairs={{0,12},{16,28},{1,13},{17,29},{2,14},{18,30},{3,15},{19,31}} | collective-permute-start | bytes 786440 | tf_op jit(solution)/shard_map/ppermute | solution.py:864
  120.4 21.2 %collective-permute-start.2 = (bf16[512,256]{1,0:T(8,128)(2,1)S(1)}, bf16[512,256]{1,0:T(8,128)(2,1)S(1)}, u32[]{:S(2)}, u32[]{:S(2)}) collective-permute-start(bf16[512,256]{1,0:T(8,128)(2,1)S(1)} %pad_maximum_fusion.8.refs_0_), channel_id=1, source_target_pairs={{0,8},{4,12},{16,24},{20,28},{1,9},{5,13},{17,25},{21,29},{2,10},{... | collective-permute-start | bytes 786440 | tf_op jit(solution)/shard_map/ppermute | solution.py:864
  122.2 19.4 %collective-permute-start.1 = (bf16[512,256]{1,0:T(8,128)(2,1)S(1)}, bf16[512,256]{1,0:T(8,128)(2,1)S(1)}, u32[]{:S(2)}, u32[]{:S(2)}) collective-permute-start(bf16[512,256]{1,0:T(8,128)(2,1)S(1)} %pad_maximum_fusion.8.refs_0_), channel_id=1, source_target_pairs={{0,4},{4,8},{8,12},{16,20},{20,24},{24,28},{1,5},{5,9},{9,13},{17,... | collective-permute-start | bytes 786440 | tf_op jit(solution)/shard_map/ppermute | solution.py:864
  206.3 28.1 %collective-permute-start.4 = (bf16[288,1728]{1,0:T(8,128)(2,1)S(1)}, bf16[288,1728]{1,0:T(8,128)(2,1)S(1)}, u32[]{:S(2)}, u32[]{:S(2)}) collective-permute-start(bf16[288,1728]{1,0:T(8,128)(2,1)S(1)} %get-tuple-element.107), channel_id=1, source_target_pairs={{0,8},{8,16},{16,24},{24,28},{28,20},{20,12},{12,4},{4,0},{1,9},{9... | collective-permute-start | bytes 2985992 | tf_op jit(solution)/shard_map/ppermute | solution.py:530
  211.6 25.0 %collective-permute-start.5 = (bf16[288,1728]{1,0:T(8,128)(2,1)S(1)}, bf16[288,1728]{1,0:T(8,128)(2,1)S(1)}, u32[]{:S(2)}, u32[]{:S(2)}) collective-permute-start(bf16[288,1728]{1,0:T(8,128)(2,1)S(1)} %get-tuple-element.108), channel_id=1, source_target_pairs={{8,0},{16,8},{24,16},{28,24},{20,28},{12,20},{4,12},{0,4},{9,1},{1... | collective-permute-start | bytes 2985992 | tf_op jit(solution)/shard_map/ppermute | solution.py:530
  240.0 28.3 %collective-permute-start.6 = (bf16[288,1728]{1,0:T(8,128)(2,1)}, bf16[288,1728]{1,0:T(8,128)(2,1)}, u32[]{:S(2)}, u32[]{:S(2)}) collective-permute-start(bf16[288,1728]{1,0:T(8,128)(2,1)} %get-tuple-element.118), channel_id=1, source_target_pairs={{0,8},{8,16},{16,24},{24,28},{28,20},{20,12},{12,4},{4,0},{1,9},{9... | collective-permute-start | bytes 2985992 | tf_op jit(solution)/shard_map/ppermute | solution.py:530
  241.4 26.9 %collective-permute-start.7 = (bf16[288,1728]{1,0:T(8,128)(2,1)}, bf16[288,1728]{1,0:T(8,128)(2,1)}, u32[]{:S(2)}, u32[]{:S(2)}) collective-permute-start(bf16[288,1728]{1,0:T(8,128)(2,1)} %get-tuple-element.119), channel_id=1, source_target_pairs={{8,0},{16,8},{24,16},{28,24},{20,28},{12,20},{4,12},{0,4},{9,1},{1... | collective-permute-start | bytes 2985992 | tf_op jit(solution)/shard_map/ppermute | solution.py:530
  273.3 25.5 %collective-permute-start.8 = (bf16[288,1728]{1,0:T(8,128)(2,1)}, bf16[288,1728]{1,0:T(8,128)(2,1)}, u32[]{:S(2)}, u32[]{:S(2)}) collective-permute-start(bf16[288,1728]{1,0:T(8,128)(2,1)} %get-tuple-element.124), channel_id=1, source_target_pairs={{0,8},{8,16},{16,24},{24,28},{28,20},{20,12},{12,4},{4,0},{1,9},{9... | collective-permute-start | bytes 2985992 | tf_op jit(solution)/shard_map/ppermute | solution.py:530
  275.0 25.2 %collective-permute-start.9 = (bf16[288,1728]{1,0:T(8,128)(2,1)S(1)}, bf16[288,1728]{1,0:T(8,128)(2,1)}, u32[]{:S(2)}, u32[]{:S(2)}) collective-permute-start(bf16[288,1728]{1,0:T(8,128)(2,1)S(1)} %get-tuple-element.125), channel_id=1, source_target_pairs={{8,0},{16,8},{24,16},{28,24},{20,28},{12,20},{4,12},{0,4},{9,1},{1... | collective-permute-start | bytes 2985992 | tf_op jit(solution)/shard_map/ppermute | solution.py:530
  302.8 24.3 %collective-permute-start.10 = (bf16[288,1728]{1,0:T(8,128)(2,1)S(1)}, bf16[288,1728]{1,0:T(8,128)(2,1)S(1)}, u32[]{:S(2)}, u32[]{:S(2)}) collective-permute-start(bf16[288,1728]{1,0:T(8,128)(2,1)S(1)} %get-tuple-element.130), channel_id=1, source_target_pairs={{0,8},{8,16},{16,24},{24,28},{28,20},{20,12},{12,4},{4,0},{1,9},{9... | collective-permute-start | bytes 2985992 | tf_op jit(solution)/shard_map/ppermute | solution.py:530
  304.6 23.7 %collective-permute-start.11 = (bf16[288,1728]{1,0:T(8,128)(2,1)S(1)}, bf16[288,1728]{1,0:T(8,128)(2,1)S(1)}, u32[]{:S(2)}, u32[]{:S(2)}) collective-permute-start(bf16[288,1728]{1,0:T(8,128)(2,1)S(1)} %get-tuple-element.131), channel_id=1, source_target_pairs={{8,0},{16,8},{24,16},{28,24},{20,28},{12,20},{4,12},{0,4},{9,1},{1... | collective-permute-start | bytes 2985992 | tf_op jit(solution)/shard_map/ppermute | solution.py:530
  341.0 36.0 %collective-permute-start.12 = (bf16[288,1728]{1,0:T(8,128)(2,1)}, bf16[288,1728]{1,0:T(8,128)(2,1)}, u32[]{:S(2)}, u32[]{:S(2)}) collective-permute-start(bf16[288,1728]{1,0:T(8,128)(2,1)} %get-tuple-element.143), channel_id=1, source_target_pairs={{0,8},{8,16},{16,24},{24,28},{28,20},{20,12},{12,4},{4,0},{1,9},{9... | collective-permute-start | bytes 2985992 | tf_op jit(solution)/shard_map/ppermute | solution.py:530
  342.8 34.3 %collective-permute-start.13 = (bf16[288,1728]{1,0:T(8,128)(2,1)}, bf16[288,1728]{1,0:T(8,128)(2,1)}, u32[]{:S(2)}, u32[]{:S(2)}) collective-permute-start(bf16[288,1728]{1,0:T(8,128)(2,1)} %get-tuple-element.144), channel_id=1, source_target_pairs={{8,0},{16,8},{24,16},{28,24},{20,28},{12,20},{4,12},{0,4},{9,1},{1... | collective-permute-start | bytes 2985992 | tf_op jit(solution)/shard_map/ppermute | solution.py:530
  343.1 32.1 %collective-permute-start.16 = (bf16[512,256]{1,0:T(8,128)(2,1)S(1)}, bf16[512,256]{1,0:T(8,128)(2,1)S(1)}, u32[]{:S(2)}, u32[]{:S(2)}) collective-permute-start(bf16[512,256]{1,0:T(8,128)(2,1)S(1)} %get-tuple-element.330), channel_id=1, source_target_pairs={{4,0},{8,4},{12,8},{20,16},{24,20},{28,24},{5,1},{9,5},{13,9},{21,... | collective-permute-start | bytes 786440 | tf_op jit(solution)/shard_map/ppermute | solution.py:908
  344.4 30.8 %collective-permute-start.18 = (bf16[512,256]{1,0:T(8,128)(2,1)S(1)}, bf16[512,256]{1,0:T(8,128)(2,1)S(1)}, u32[]{:S(2)}, u32[]{:S(2)}) collective-permute-start(bf16[512,256]{1,0:T(8,128)(2,1)S(1)} %get-tuple-element.331), channel_id=1, source_target_pairs={{12,0},{28,16},{13,1},{29,17},{14,2},{30,18},{15,3},{31,19}} | collective-permute-start | bytes 786440 | tf_op jit(solution)/shard_map/ppermute | solution.py:908
  345.7 31.0 %collective-permute-start.17 = (bf16[512,256]{1,0:T(8,128)(2,1)S(1)}, bf16[512,256]{1,0:T(8,128)(2,1)S(1)}, u32[]{:S(2)}, u32[]{:S(2)}) collective-permute-start(bf16[512,256]{1,0:T(8,128)(2,1)S(1)} %get-tuple-element.332), channel_id=1, source_target_pairs={{8,0},{12,4},{24,16},{28,20},{9,1},{13,5},{25,17},{29,21},{10,2},{... | collective-permute-start | bytes 786440 | tf_op jit(solution)/shard_map/ppermute | solution.py:908
  381.1 21.9 %collective-permute-start.14 = (bf16[288,1728]{1,0:T(8,128)(2,1)}, bf16[288,1728]{1,0:T(8,128)(2,1)}, u32[]{:S(2)}, u32[]{:S(2)}) collective-permute-start(bf16[288,1728]{1,0:T(8,128)(2,1)} %get-tuple-element.147), channel_id=1, source_target_pairs={{0,8},{8,16},{16,24},{24,28},{28,20},{20,12},{12,4},{4,0},{1,9},{9... | collective-permute-start | bytes 2985992 | tf_op jit(solution)/shard_map/ppermute | solution.py:530
  381.2 22.1 %collective-permute-start.15 = (bf16[288,1728]{1,0:T(8,128)(2,1)}, bf16[288,1728]{1,0:T(8,128)(2,1)}, u32[]{:S(2)}, u32[]{:S(2)}) collective-permute-start(bf16[288,1728]{1,0:T(8,128)(2,1)} %get-tuple-element.148), channel_id=1, source_target_pairs={{8,0},{16,8},{24,16},{28,24},{20,28},{12,20},{4,12},{0,4},{9,1},{1... | collective-permute-start | bytes 2985992 | tf_op jit(solution)/shard_map/ppermute | solution.py:530
  407.3 21.2 %collective-permute-start.19 = (bf16[288,1728]{1,0:T(8,128)(2,1)}, bf16[288,1728]{1,0:T(8,128)(2,1)}, u32[]{:S(2)}, u32[]{:S(2)}) collective-permute-start(bf16[288,1728]{1,0:T(8,128)(2,1)} %get-tuple-element.156), channel_id=1, source_target_pairs={{0,8},{8,16},{16,24},{24,28},{28,20},{20,12},{12,4},{4,0},{1,9},{9... | collective-permute-start | bytes 2985992 | tf_op jit(solution)/shard_map/ppermute | solution.py:530
  409.1 20.9 %collective-permute-start.20 = (bf16[288,1728]{1,0:T(8,128)(2,1)}, bf16[288,1728]{1,0:T(8,128)(2,1)}, u32[]{:S(2)}, u32[]{:S(2)}) collective-permute-start(bf16[288,1728]{1,0:T(8,128)(2,1)} %get-tuple-element.157), channel_id=1, source_target_pairs={{8,0},{16,8},{24,16},{28,24},{20,28},{12,20},{4,12},{0,4},{9,1},{1... | collective-permute-start | bytes 2985992 | tf_op jit(solution)/shard_map/ppermute | solution.py:530
  497.8 8.4 %collective-permute-start.21 = (f32[2,384]{1,0:T(2,128)S(1)}, f32[2,384]{1,0:T(2,128)S(1)}, u32[]{:S(2)}, u32[]{:S(2)}) collective-permute-start(f32[2,384]{1,0:T(2,128)S(1)} %pad_add_fusion.1), channel_id=1, source_target_pairs={{4,0},{8,4},{12,8},{20,16},{24,20},{28,24},{5,1},{9,5},{13,9},{21,... | collective-permute-start | bytes 9224 | tf_op jit(solution)/shard_map/ppermute | solution.py:960
  (130 other events, 1152.1 us)

commit v3 on v1

v3 whole, which is shorter than its diff:
```python
import jax
import jax.numpy as jnp
from jax import lax
from jax.experimental import pallas as pl
from jax.experimental.pallas import tpu as pltpu
from jax.sharding import PartitionSpec as P

HEAD = 64
KW = 3
SPAN = 4
GROUP = 3


EPSILON = 1e-05
THETA = 1000000.0
BF16 = jnp.bfloat16
F32 = jnp.float32


def matmul(left, right):
    return jnp.dot(left, right, preferred_element_type=F32)


def inner_back(left, right):
    return lax.dot_general(left, right, (((1,), (1,)), ((), ())), preferred_element_type=F32)


def normalize(values, gain):
    inverse = lax.rsqrt(jnp.mean(values * values, axis=-1, keepdims=True) + EPSILON)
    return (values * inverse * gain, inverse)


def normalize_back(values, inverse, gain, grad_result):
    weighted = grad_result * gain
    grad_gain = jnp.sum(grad_result * values * inverse, axis=tuple(range(values.ndim - 1)))
    inner = jnp.mean(weighted * values, axis=-1, keepdims=True)
    grad_values = inverse * (weighted - values * inverse * inverse * inner)
    return (grad_values, grad_gain)


CHUNKS = 4
SLOTS = 3
MESH = pl.DeviceIdType.MESH


class Refs:
    def __init__(self, names, refs):
        self.__dict__.update(zip(names, refs))


def run_kernel(body, inputs, outputs, scratch, collective_id, limit, flops):
    arrays, specs = [], []
    for value in inputs.values():
        array, space = value if isinstance(value, tuple) else (value, pltpu.VMEM)
        arrays.append(array)
        specs.append(pl.BlockSpec(memory_space=space))
    names = list(inputs) + list(outputs) + list(scratch)
    return pl.pallas_call(
        lambda *refs: body(Refs(names, refs)),
        in_specs=specs,
        out_specs=[pl.BlockSpec(memory_space=pltpu.VMEM)] * len(outputs),
        out_shape=[jax.ShapeDtypeStruct(*value) for value in outputs.values()],
        scratch_shapes=list(scratch.values()),
        compiler_params=pltpu.CompilerParams(
            collective_id=collective_id, has_side_effects=True, vmem_limit_bytes=limit * 2**20
        ),
        cost_estimate=pl.CostEstimate(
            flops=flops,
            bytes_accessed=sum(a.size * a.dtype.itemsize for a in arrays),
            transcendentals=0,
        ),
    )(*arrays)


def greet(peers):
    barrier = pltpu.get_barrier_semaphore()
    for peer in peers:
        pl.semaphore_signal(barrier, inc=1, device_id=peer, device_id_type=MESH)
    pl.semaphore_wait(barrier, len(peers))


def tensor_peers():
    me = lax.axis_index("tensor")
    return [dict(tensor=me ^ 1), dict(tensor=me ^ 2)]


def span_peers():
    me = lax.axis_index("dp")
    place = lax.rem(me, SPAN)
    return [dict(dp=me - place + lax.rem(place + k, SPAN)) for k in range(1, SPAN)]


def remote(src, dst, send, recv, peer):
    return pltpu.make_async_remote_copy(
        src_ref=src, dst_ref=dst, send_sem=send, recv_sem=recv, device_id=peer, device_id_type=MESH
    )


def exchange_scratch(rows, width):
    quarter = rows // 4
    return dict(
        near_rows=pltpu.VMEM((2 * quarter, width), BF16),
        across_rows=pltpu.VMEM((quarter, width), BF16),
        far_rows=pltpu.VMEM((quarter, width), BF16),
        x_send=pltpu.SemaphoreType.DMA((6 * CHUNKS,)),
        x_recv=pltpu.SemaphoreType.DMA((6 * CHUNKS,)),
    )


def sum_and_gather(r, partial, gathered, gathered_t, compute):
    near, across, far = r.near_rows, r.across_rows, r.far_rows
    core, other = tensor_peers()
    quarter = partial.shape[0] // 4
    size = quarter // CHUNKS
    copies = {}

    def copy(kind, at, src, dst, peer):
        number = kind * CHUNKS + at
        copies[kind, at] = remote(src, dst, r.x_send.at[number], r.x_recv.at[number], peer)
        copies[kind, at].start()

    def part(block, at):
        return pl.ds(block * quarter + at * size, size)

    def turn(block):
        if gathered_t is not None:
            rows = slice(block * quarter, (block + 1) * quarter)
            gathered_t[:, rows] = gathered[rows, :].T

    for at in range(CHUNKS):
        copy(0, at, partial.at[part(3, at)], near.at[part(1, at)], core)
    for at in range(CHUNKS):
        copy(1, at, partial.at[part(2, at)], near.at[part(0, at)], core)
    for at in range(CHUNKS):
        copies[0, at].wait_recv()
        far[part(0, at), :] = (
            partial[part(1, at), :].astype(F32) + near[part(1, at), :].astype(F32)
        ).astype(BF16)
        copy(2, at, far.at[part(0, at)], across.at[part(0, at)], other)
    yield 1
    for at in range(CHUNKS):
        copies[1, at].wait_recv()
        copies[2, at].wait_recv()
        total = (
            partial[part(0, at), :].astype(F32)
            + near[part(0, at), :].astype(F32)
            + across[part(0, at), :].astype(F32)
        )
        gathered[part(0, at), :] = compute(total, part(0, at), at == 0)
        copy(3, at, gathered.at[part(0, at)], gathered.at[part(1, at)], other)
        copy(4, at, gathered.at[part(0, at)], gathered.at[part(2, at)], core)
    turn(0)
    yield 1
    for at in range(CHUNKS):
        copies[3, at].wait_recv()
        copy(5, at, gathered.at[part(1, at)], gathered.at[part(3, at)], core)
    turn(1)
    for at in range(CHUNKS):
        copies[4, at].wait_recv()
    turn(2)
    for at in range(CHUNKS):
        copies[5, at].wait_recv()
    turn(3)
    for made in copies.values():
        made.wait_send()
    yield 1


def exhaust(main):
    for _ in main:
        pass


def spread(partial_b, extras, out_shapes, compute, collective_id):
    rows, width = partial_b.shape

    def body(r):
        greet(tensor_peers())
        exhaust(
            sum_and_gather(
                r, r.partial, r.gathered, r.gathered_t, lambda *values: compute(r, *values)
            )
        )

    outputs = dict(gathered=((rows, width), BF16), gathered_t=((width, rows), BF16))
    outputs.update({name: (shape, F32) for name, shape in out_shapes.items()})
    return run_kernel(
        body,
        dict(partial=partial_b, **extras),
        outputs,
        exchange_scratch(rows, width),
        collective_id,
        32,
        10 * rows * width,
    )


def norm_rows(total, rows, residual, gain, hidden):
    values = residual[rows, :] + total
    hidden[rows, :] = values
    return normalize(values, gain[...])[0].astype(BF16)


def norm_spread(partial_b, residual, gain):
    def compute(r, total, rows, first):
        return norm_rows(total, rows, r.residual, r.gain, r.hidden)

    return spread(
        partial_b,
        dict(residual=residual, gain=gain.reshape(1, -1)),
        dict(hidden=residual.shape),
        compute,
        1,
    )


def back_rows(total, rows, first, hidden, gain, incoming, own, grad_gain):
    values = hidden[rows, :]
    inverse = lax.rsqrt(jnp.mean(values * values, axis=-1, keepdims=True) + EPSILON)
    made, term = normalize_back(values, inverse, gain[...], total)
    made = made + incoming[rows, :]
    if own is not None:
        own[rows, :] = made
    term = term.reshape(1, -1)
    grad_gain[...] = term if first else grad_gain[...] + term
    return made.astype(BF16)


def back_spread(partial_b, hidden, gain, incoming):
    def compute(r, total, rows, first):
        return back_rows(total, rows, first, r.hidden, r.gain, r.incoming, r.own, r.grad_gain)

    return spread(
        partial_b,
        dict(hidden=hidden, gain=gain.reshape(1, -1), incoming=incoming),
        dict(own=hidden.shape, grad_gain=(1, hidden.shape[1])),
        compute,
        3,
    )


def ring_peers(count):
    me = lax.axis_index("dp")
    even = lax.rem(me, 2) == 0
    place = jnp.where(even, me // 2, count - 1 - me // 2)

    def at(position):
        position = lax.rem(position + count, count)
        return jnp.where(position < count // 2, 2 * position, 2 * (count - 1 - position) + 1)

    return at(place + 1), at(place - 1), lambda distance: at(place + distance)


class Rings:
    def __init__(self, devices, sides, segments, held, send, recv, credit, store):
        self.devices, self.sides, self.segments, self.held = devices, sides, segments, held
        self.send, self.recv, self.credit, self.store = send, recv, credit, store
        self.rows = segments[0][0][0].shape[0] // devices
        self.half = self.rows // sides
        self.steps = devices - 1
        self.following, self.previous, self.owner_at = ring_peers(devices)

    def peers(self):
        return [dict(dp=self.following), dict(dp=self.previous)]

    def copy(self, seg, side, step):
        number = (seg * self.sides + side) * self.steps + step
        return remote(
            self.held[seg].at[side, step % SLOTS],
            self.held[seg].at[side, (step + 1) % SLOTS],
            self.send.at[number],
            self.recv.at[number],
            dict(dp=self.following if side == 0 else self.previous),
        )

    def unit(self, seg, step):
        sides, half, steps = self.sides, self.half, self.steps
        last = step == steps
        slot = step % SLOTS
        starts = []
        for side in range(sides):
            if last:
                owner = lax.axis_index("dp")
            else:
                owner = self.owner_at(-1 - step if side == 0 else 1 + step)
            starts.append(pl.multiple_of(owner * self.rows + side * half, 16))
        if step:
            for side in range(sides):
                self.copy(seg, side, step - 1).wait_send()
                if step <= steps + 1 - SLOTS:
                    pl.semaphore_signal(
                        self.credit.at[seg * sides + side],
                        inc=1,
                        device_id=dict(dp=self.previous if side == 0 else self.following),
                        device_id_type=MESH,
                    )
                self.copy(seg, side, step - 1).wait_recv()
        column = 0
        for left, right in self.segments[seg]:
            pieces = [left[pl.ds(start, half), :] for start in starts]
            piece = pieces[0] if sides == 1 else jnp.concatenate(pieces, axis=0)
            made = jnp.dot(piece, right[...], preferred_element_type=F32)
            at = slice(column, column + made.shape[1])
            values = []
            for side in range(sides):
                value = made[side * half : (side + 1) * half]
                if step:
                    value = value + self.held[seg][side, slot, :, at].astype(F32)
                if last:
                    values.append(value)
                else:
                    self.held[seg][side, slot, :, at] = value.astype(BF16)
            if last:
                self.store(seg, column, values[0] if sides == 1 else jnp.concatenate(values, axis=0))
            column += made.shape[1]
        if not last:
            for side in range(sides):
                if step >= SLOTS - 1:
                    pl.semaphore_wait(self.credit.at[seg * sides + side], 1)
                self.copy(seg, side, step).start()


def ring_scratch(devices, sides, rows, widths):
    copies = len(widths) * sides * (devices - 1)
    made = {
        f"held{at}": pltpu.VMEM((sides, SLOTS, rows // sides, w), BF16)
        for at, w in enumerate(widths)
    }
    made["r_send"] = pltpu.SemaphoreType.DMA((copies,))
    made["r_recv"] = pltpu.SemaphoreType.DMA((copies,))
    made["r_credit"] = pltpu.SemaphoreType.REGULAR((len(widths) * sides,))
    return made


def interleave(main, units, first):
    units = iter(units)

    def some(number):
        for _ in range(number):
            unit = next(units, None)
            if unit is not None:
                unit()

    some(first)
    for number in main:
        some(number)
    for unit in units:
        unit()


def piece_sides(width, devices):
    return 2 if width // devices % 32 == 0 else 1


def block_owners(index):
    return [index, index ^ 2, index ^ 1, index ^ 3]


def to_local(values, index):
    quarter = values.shape[0] // 4
    return jnp.concatenate(
        [lax.dynamic_slice_in_dim(values, o * quarter, quarter) for o in block_owners(index)]
    )


def to_true(values, index):
    quarter = values.shape[0] // 4
    places = []
    for block in range(4):
        shift = block ^ index
        place = ((shift & 1) << 1) | (shift >> 1)
        places.append(lax.dynamic_slice_in_dim(values, place * quarter, quarter))
    return jnp.concatenate(places)


def cross(left, right):
    return lax.dot_general(left, right, (((1,), (1,)), ((), ())), preferred_element_type=F32)


def turn_t(values, cosine, sine, back):
    middle = HEAD // 2
    low, high = values[:middle], values[middle:]
    if back:
        return jnp.concatenate([low * cosine + high * sine, high * cosine - low * sine], axis=0)
    return jnp.concatenate([low * cosine - high * sine, high * cosine + low * sine], axis=0)


def head_norm_t(values, gain):
    inverse = lax.rsqrt(jnp.mean(values * values, axis=0, keepdims=True) + EPSILON)
    return values * inverse * gain


def head_back_t(values, gain, grad):
    inverse = lax.rsqrt(jnp.mean(values * values, axis=0, keepdims=True) + EPSILON)
    weighted = grad * gain
    inner = jnp.mean(weighted * values, axis=0, keepdims=True)
    return inverse * (weighted - values * inverse * inverse * inner), grad * values * inverse


def fill_bias(r):
    keys = r.column_positions[...]
    allowed = (keys <= r.row_positions[...]) & (keys < r.length[0])
    r.bias[...] = jnp.where(allowed, 0.0, -1e30)


def head_rows(head):
    return slice(head * HEAD, (head + 1) * HEAD)


def position_inputs(positions, length):
    rows = positions.shape[0]
    return dict(
        length=(length.reshape(1), pltpu.SMEM),
        row_positions=positions.reshape(1, rows),
        column_positions=positions.reshape(rows, 1),
    )


def attention_forward(
    normed_b, query_weight, kv_weight, query_gain, key_gain, attn_out, residual, gain, tables, where
):
    rows, width = normed_b.shape
    columns = query_weight.shape[1]
    kv_columns = kv_weight.shape[1] // 2
    heads, kv_heads = columns // HEAD, kv_columns // HEAD

    def body(r):
        me = lax.axis_index("dp")
        place = lax.rem(me, SPAN)
        greet(tensor_peers() + span_peers())

        def pass_on(distance):
            return remote(
                r.own, r.near.at[distance - 1], r.p_send.at[distance - 1], r.p_recv.at[distance - 1],
                dict(dp=me + distance),
            )

        cosine, sine = r.cosine[...], r.sine[...]
        made = jnp.dot(r.normed[...], r.kv_weight[...], preferred_element_type=F32)
        r.key_raw[...] = made[:, :kv_columns].T
        r.own[:, kv_columns:] = made[:, kv_columns:].astype(BF16)
        for group in range(kv_heads):
            keys = head_norm_t(r.key_raw[head_rows(group), :], r.key_gain[...])
            r.keys_t[head_rows(group), :] = turn_t(keys, cosine, sine, False).astype(BF16)
        r.own[:, :kv_columns] = r.keys_t[...].T
        for distance in range(1, SPAN):

            @pl.when(place + distance < SPAN)
            def _():
                pass_on(distance).start()

        made = jnp.dot(r.normed[...], r.query_weight[...], preferred_element_type=F32)
        r.query_raw[...] = made.T
        for head in range(heads):
            query = head_norm_t(r.query_raw[head_rows(head), :], r.query_gain[...])
            query = turn_t(query, cosine, sine, False).astype(BF16)
            r.query[head_rows(head), :] = query * jnp.asarray(HEAD ** (-0.5), BF16)
        fill_bias(r)

        def part(piece, first):
            for group in range(kv_heads):
                keys = piece[:, head_rows(group)]
                values_t = piece[:, kv_columns + group * HEAD : kv_columns + (group + 1) * HEAD].T
                for head in range(group * GROUP, (group + 1) * GROUP):
                    at = head_rows(head)
                    scores = jnp.dot(keys, r.query[at, :], preferred_element_type=F32)
                    if first:
                        scores = scores + r.bias[...]
                    expo = jnp.exp(scores)
                    total = jnp.sum(expo, axis=0, keepdims=True)
                    made = jnp.dot(values_t, expo.astype(BF16), preferred_element_type=F32)
                    if first:
                        r.total[head : head + 1, :] = total
                        r.attended_t[at, :] = made
                    else:
                        r.total[head : head + 1, :] += total
                        r.attended_t[at, :] += made

        part(r.own[...], True)
        for distance in range(1, SPAN):

            @pl.when(place >= distance)
            def _():
                pass_on(distance).wait_recv()
                part(r.near[distance - 1], False)

        for head in range(heads):
            at = head_rows(head)
            made = r.attended_t[at, :] / r.total[head : head + 1, :]
            r.attended_t[at, :] = made
            r.attended[:, at] = made.T.astype(BF16)
        r.log_total[...] = jnp.log(r.total[...])
        r.partial[...] = jnp.dot(
            r.attended[...], r.attn_out[...], preferred_element_type=F32
        ).astype(BF16)
        exhaust(
            sum_and_gather(
                r, r.partial, r.gathered, r.gathered_t,
                lambda total, at, first: norm_rows(total, at, r.residual, r.gain, r.hidden),
            )
        )
        for distance in range(1, SPAN):

            @pl.when(place + distance < SPAN)
            def _():
                pass_on(distance).wait_send()

    return run_kernel(
        body,
        dict(
            normed=normed_b,
            query_weight=query_weight,
            kv_weight=kv_weight,
            query_gain=query_gain.reshape(HEAD, 1),
            key_gain=key_gain.reshape(HEAD, 1),
            attn_out=attn_out,
            residual=residual,
            gain=gain.reshape(1, -1),
            cosine=tables[0],
            sine=tables[1],
            **where,
        ),
        dict(
            gathered=((rows, width), BF16),
            gathered_t=((width, rows), BF16),
            hidden=(residual.shape, F32),
            query_raw=((columns, rows), F32),
            key_raw=((kv_columns, rows), F32),
            query=((columns, rows), BF16),
            own=((rows, 2 * kv_columns), BF16),
            near=((SPAN - 1, rows, 2 * kv_columns), BF16),
            attended=((rows, columns), BF16),
            attended_t=((columns, rows), F32),
            log_total=((heads, rows), F32),
        ),
        dict(
            keys_t=pltpu.VMEM((kv_columns, rows), BF16),
            bias=pltpu.VMEM((rows, rows), F32),
            total=pltpu.VMEM((heads, rows), F32),
            partial=pltpu.VMEM((rows, width), BF16),
            p_send=pltpu.SemaphoreType.DMA((SPAN - 1,)),
            p_recv=pltpu.SemaphoreType.DMA((SPAN - 1,)),
            **exchange_scratch(rows, width),
        ),
        2,
        48,
        16 * rows * rows * SPAN * columns,
    )


def stream_product(r, lefts, weights, out):
    width = weights.shape[2]
    size = r.tile.shape[3]
    tiles = width // size

    def fetch(j):
        return [
            pltpu.make_async_copy(
                weights.at[k, :, pl.ds(j * size, size)], r.tile.at[j % 2, k], r.tile_sem.at[j % 2, k]
            )
            for k in range(len(lefts))
        ]

    for copy in fetch(0):
        copy.start()
    for j in range(tiles):
        if j + 1 < tiles:
            for copy in fetch(j + 1):
                copy.start()
        for copy in fetch(j):
            copy.wait()
        made = None
        for k, left in enumerate(lefts):
            term = jnp.dot(left[...], r.tile[j % 2, k], preferred_element_type=F32)
            made = term if made is None else made + term
        out[:, j * size : (j + 1) * size] = made.astype(BF16)
        if j % 2:
            yield 1


def stream_scratch(count, depth, size):
    return dict(
        tile=pltpu.VMEM((2, count, depth, size), BF16),
        tile_sem=pltpu.SemaphoreType.DMA((2, count)),
    )


def attention_backward(
    grad_b_t, norm_two_t, active, grad_gate, grad_up, gate_up_t, down, three, norm_mlp, incoming,
    kept, attn_out, query_weight, kv_weight, query_gain, key_gain, two, norm_attn, tables, where, devices,
):
    units, tokens_width = gate_up_t.shape[1:]
    query_raw, key_raw, query, own, near, attended_t, log_total = kept
    rows, width = active.shape[0], tokens_width
    columns = query_weight.shape[1]
    kv_columns = kv_weight.shape[1] // 2
    heads, kv_heads = columns // HEAD, kv_columns // HEAD
    sides = piece_sides(width, devices)
    block = width // devices
    segment_widths = [units] * 3

    def body(r):
        me = lax.axis_index("dp")
        place = lax.rem(me, SPAN)

        def store(seg, column, value):
            (r.sum_down, r.sum_gate, r.sum_up)[seg][...] = value

        rings = Rings(
            devices, sides,
            [[(r.grad_b_t, r.active)], [(r.norm_two_t, r.grad_gate)], [(r.norm_two_t, r.grad_up)]],
            [r.held0, r.held1, r.held2], r.r_send, r.r_recv, r.r_credit, store,
        )
        greet(rings.peers() + tensor_peers() + span_peers())

        def pass_back(distance):
            return remote(
                r.far.at[distance - 1], r.arrived.at[distance - 1],
                r.p_send.at[distance - 1], r.p_recv.at[distance - 1], dict(dp=me - distance),
            )

        def part(piece, write, masked):
            for group in range(kv_heads):
                keys = piece[:, head_rows(group)]
                value_at = slice(kv_columns + group * HEAD, kv_columns + (group + 1) * HEAD)
                values = piece[:, value_at]
                keys_t = keys.T
                grad_k = grad_v = None
                for head in range(group * GROUP, (group + 1) * GROUP):
                    at = head_rows(head)
                    q, grads = r.query[at, :], r.grads[:, at]
                    scores = jnp.dot(keys, q, preferred_element_type=F32)
                    scores = scores - r.log_total[head : head + 1, :]
                    if masked:
                        scores = scores + r.bias[...]
                    probs = jnp.exp(scores)
                    made = jnp.dot(probs.astype(BF16), grads, preferred_element_type=F32)
                    grad_v = made if grad_v is None else grad_v + made
                    grad_probs = cross(values, grads)
                    grad_scores = (probs * (grad_probs - r.delta[head : head + 1, :])).astype(BF16)
                    made = cross(grad_scores, q)
                    grad_k = made if grad_k is None else grad_k + made
                    made = jnp.dot(keys_t, grad_scores, preferred_element_type=F32)
                    if masked:
                        r.grad_q_t[at, :] = made
                    else:
                        r.grad_q_t[at, :] += made
                write(head_rows(group), grad_k)
                write(value_at, grad_v)

        def main():
            yield from stream_product(r, [r.grad_gate, r.grad_up], r.gate_up_t, r.partial)
            fill_bias(r)
            yield from sum_and_gather(
                r, r.partial, r.gathered, r.grad_three_t,
                lambda total, at, first: back_rows(
                    total, at, first, r.three, r.norm_mlp, r.incoming, r.grad_three, r.grad_norm_mlp
                ),
            )
            r.grads[...] = cross(r.gathered[...], r.attn_out[...]).astype(BF16)
            for head in range(heads):
                at = head_rows(head)
                grads_t = r.grads[:, at].astype(F32).T
                r.delta[head : head + 1, :] = jnp.sum(
                    grads_t * r.attended_t[at, :], axis=0, keepdims=True
                )
            yield 1

            def write_own(at, value):
                r.grad_own[:, at] = value

            part(r.own[...], write_own, True)
            yield 1
            for distance in range(1, SPAN):

                @pl.when(place >= distance)
                def _():
                    def write_far(at, value):
                        r.far[distance - 1, :, at] = value.astype(BF16)

                    part(r.near[distance - 1], write_far, False)
                    pass_back(distance).start()

                yield 1
            cosine, sine = r.cosine[...], r.sine[...]
            terms = None
            for head in range(heads):
                at = head_rows(head)
                grad = turn_t(r.grad_q_t[at, :] * HEAD ** (-0.5), cosine, sine, True)
                made, term = head_back_t(r.query_raw[at, :], r.query_gain[...], grad)
                terms = term if terms is None else terms + term
                r.grad_query[:, at] = made.T.astype(BF16)
            r.grad_query_gain[...] = jnp.sum(terms, axis=1, keepdims=True)
            yield 1
            for distance in range(1, SPAN):

                @pl.when(place + distance < SPAN)
                def _():
                    pass_back(distance).wait_recv()
                    r.grad_own[...] += r.arrived[distance - 1].astype(F32)

            terms = None
            for group in range(kv_heads):
                at = head_rows(group)
                grad = turn_t(r.grad_own[:, at].T, cosine, sine, True)
                made, term = head_back_t(r.key_raw[at, :], r.key_gain[...], grad)
                terms = term if terms is None else terms + term
                r.grad_kv[:, at] = made.T.astype(BF16)
            r.grad_key_gain[...] = jnp.sum(terms, axis=1, keepdims=True)
            r.grad_kv[:, kv_columns:] = r.grad_own[:, kv_columns:].astype(BF16)
            r.partial[...] = (
                cross(r.grad_query[...], r.query_weight[...]) + cross(r.grad_kv[...], r.kv_weight[...])
            ).astype(BF16)
            yield 1
            yield from sum_and_gather(
                r, r.partial, r.grad_two_b, r.grad_two_t,
                lambda total, at, first: back_rows(
                    total, at, first, r.two, r.norm_attn, r.grad_three, r.grad_two, r.grad_norm_attn
                ),
            )
            for distance in range(1, SPAN):

                @pl.when(place >= distance)
                def _():
                    pass_back(distance).wait_send()

            yield from stream_product(r, [r.active], r.down, r.partial)
            yield from sum_and_gather(
                r, r.partial, r.output, None,
                lambda total, at, first: (r.three[at, :] + total).astype(BF16),
            )

        order = [(seg, step) for step in range(devices) for seg in range(3)]
        interleave(main(), [lambda u=u: rings.unit(*u) for u in order], 3)

    quarter = rows // 4
    return run_kernel(
        body,
        dict(
            grad_b_t=grad_b_t,
            norm_two_t=norm_two_t,
            active=active,
            grad_gate=grad_gate,
            grad_up=grad_up,
            gate_up_t=(gate_up_t, pl.ANY),
            down=(down.reshape((1,) + down.shape), pl.ANY),
            three=three,
            norm_mlp=norm_mlp.reshape(1, -1),
            incoming=incoming,
            query_raw=query_raw,
            key_raw=key_raw,
            query=query,
            own=own,
            near=near,
            attended_t=attended_t,
            log_total=log_total,
            attn_out=attn_out,
            query_weight=query_weight,
            kv_weight=kv_weight,
            query_gain=query_gain.reshape(HEAD, 1),
            key_gain=key_gain.reshape(HEAD, 1),
            two=two,
            norm_attn=norm_attn.reshape(1, -1),
            cosine=tables[0],
            sine=tables[1],
            **where,
        ),
        dict(
            grad_three_t=((width, rows), BF16),
            grad_query=((rows, columns), BF16),
            grad_kv=((rows, 2 * kv_columns), BF16),
            grad_two_b=((rows, width), BF16),
            grad_two_t=((width, rows), BF16),
            grad_two=((quarter, width), F32),
            grad_norm_mlp=((1, width), F32),
            grad_norm_attn=((1, width), F32),
            grad_query_gain=((HEAD, 1), F32),
            grad_key_gain=((HEAD, 1), F32),
            sum_down=((block, units), F32),
            sum_gate=((block, units), F32),
            sum_up=((block, units), F32),
            output=((rows, width), BF16),
        ),
        dict(
            partial=pltpu.VMEM((rows, width), BF16),
            gathered=pltpu.VMEM((rows, width), BF16),
            grad_three=pltpu.VMEM((quarter, width), F32),
            grads=pltpu.VMEM((rows, columns), BF16),
            delta=pltpu.VMEM((heads, rows), F32),
            bias=pltpu.VMEM((rows, rows), F32),
            grad_q_t=pltpu.VMEM((columns, rows), F32),
            grad_own=pltpu.VMEM((rows, 2 * kv_columns), F32),
            far=pltpu.VMEM((SPAN - 1, rows, 2 * kv_columns), BF16),
            arrived=pltpu.VMEM((SPAN - 1, rows, 2 * kv_columns), BF16),
            p_send=pltpu.SemaphoreType.DMA((SPAN - 1,)),
            p_recv=pltpu.SemaphoreType.DMA((SPAN - 1,)),
            **stream_scratch(2, units, 256),
            **exchange_scratch(rows, width),
            **ring_scratch(devices, sides, block, segment_widths),
        ),
        3 + 2,
        61,
        2 * rows * width * units * 10,
    )


class Pump:
    def __init__(self, rings, ready):
        self.rings, self.ready = rings, list(ready)
        self.step = [0] * len(rings.segments)
        self.before = None

    def run(self, number):
        for _ in range(number):
            left = [s for s in self.ready if self.step[s] <= self.rings.steps]
            if not left:
                return
            seg = min(left, key=lambda s: (s == self.before, self.step[s], s))
            self.rings.unit(seg, self.step[seg])
            self.step[seg] += 1
            self.before = seg

    def rest(self):
        self.run(len(self.step) * (self.rings.steps + 1))


def first_backward(
    lefts, rights, grad_two_b, down, gate_up_t, gate, upward, one, norm_mlp, grad_two, conv_out,
    conv_in_t, projected, rim, kernel, inputs, norm_conv, small, devices,
):
    rows, width = grad_two_b.shape
    units = down.shape[0]
    channels = conv_out.shape[0]
    quarter = rows // 4
    block = width // devices
    sides = piece_sides(width, devices)
    grad_three_t, normed_attn_t, grad_two_t, norm_one_t, normed_conv_t = lefts
    attended, grad_query, grad_kv, active, gated = rights
    columns, kv_columns = grad_query.shape[1], grad_kv.shape[1]
    widths = [channels + columns + kv_columns, units, units, units, 4 * channels]
    bits = []
    bit = 1
    while bit < devices:
        bits.append(bit)
        bit *= 2
    stages = 2 + len(bits)
    size = TILE
    tiles = [(at, min(size, units - at)) for at in range(0, units, size)]

    def body(r):
        me = lax.axis_index("dp")
        index = lax.axis_index("tensor")
        place = lax.rem(me, SPAN)

        def store(seg, column, value):
            if seg == 0:
                at = (0, channels, channels + columns).index(column)
                (r.sum_attn_out, r.sum_query, r.sum_kv)[at][...] = value
            elif seg < 4:
                (r.sum_down, r.sum_gate, r.sum_up)[seg - 1][...] = value
            elif column == 0:
                r.sum_conv_out[...] = value
            else:
                for at in range(3):
                    r.sum_conv_in[at] = value[:, at * channels : (at + 1) * channels]

        rings = Rings(
            devices, sides,
            [
                [
                    (r.grad_three_t, r.attended),
                    (r.normed_attn_t, r.grad_query),
                    (r.normed_attn_t, r.grad_kv),
                ],
                [(r.grad_two_t, r.active)],
                [(r.norm_one_t, r.grad_gate)],
                [(r.norm_one_t, r.grad_up)],
                [(r.grad_one_t, r.gated), (r.normed_conv_t, r.grad_projected)],
            ],
            [r.held0, r.held1, r.held2, r.held3, r.held4], r.r_send, r.r_recv, r.r_credit, store,
        )
        pump = Pump(rings, [0, 1])
        small_peers = tensor_peers() + [dict(dp=me ^ bit) for bit in bits]
        greet(rings.peers() + small_peers + span_peers())

        def fetch(number):
            at, wide = tiles[number]
            slot = number % 2
            pairs = [
                (r.down.at[at : at + wide, :], r.down_tile.at[slot, 0:wide, :]),
                (r.gate.at[number], r.gate_tile.at[slot]),
                (r.upward.at[number], r.up_tile.at[slot]),
            ]
            return [
                pltpu.make_async_copy(a, b, r.h_sem.at[slot, k]) for k, (a, b) in enumerate(pairs)
            ]

        def fetch_conv(number):
            slot = number % 2
            return [
                pltpu.make_async_copy(
                    r.conv_in_t.at[k, pl.ds(number * size, size), :],
                    r.conv_tile.at[slot, k],
                    r.c_sem.at[slot, k],
                )
                for k in range(3)
            ]

        def main():
            first = pltpu.make_async_copy(r.grad_two_b, r.gathered, r.e_sem)
            first.start()
            for copy in fetch(0):
                copy.start()
            first.wait()
            for number, (at, wide) in enumerate(tiles):
                if number + 1 < len(tiles):
                    for copy in fetch(number + 1):
                        copy.start()
                for copy in fetch(number):
                    copy.wait()
                slot = number % 2
                grad = cross(r.gathered[...], r.down_tile[slot, 0:wide, :])
                gates, ups = r.gate_tile[slot, :, 0:wide], r.up_tile[slot, :, 0:wide]
                sigma = jax.nn.sigmoid(gates)
                r.grad_gate[:, at : at + wide] = (
                    grad * ups * sigma * (1.0 + gates * (1.0 - sigma))
                ).astype(BF16)
                r.grad_up[:, at : at + wide] = (grad * gates * sigma).astype(BF16)
                if number % 3 == 2:
                    yield 1
            pump.ready += [2, 3]
            yield 2
            yield from stream_product(r, [r.grad_gate, r.grad_up], r.gate_up_t, r.partial)
            yield from sum_and_gather(
                r, r.partial, r.gathered, r.grad_one_t,
                lambda total, at, first: back_rows(
                    total, at, first, r.one, r.norm_mlp, r.grad_two, r.grad_one, r.gain_term
                ),
            )
            r.small_out[...] = r.small[...]
            r.small_out[1:2, :] = r.gain_term[...]

            made = cross(r.gathered[...], r.conv_out[...])
            for at, owner in enumerate(block_owners(index)):
                start = pl.multiple_of(owner * quarter, quarter)
                r.grad_gated[pl.ds(start, quarter), :] = made[at * quarter : (at + 1) * quarter]
            before = r.projected[:, :channels]
            signal = r.projected[:, 2 * channels :]
            taps = r.kernel[...].astype(F32)
            pad = 8
            r.mixed[pad:, :] = before * signal
            r.mixed[pad - KW + 1 : pad, :] = r.rim[...]
            grad_gated = r.grad_gated[...]
            r.grad_conv[0:rows, :] = grad_gated * r.projected[:, channels : 2 * channels]
            r.grad_conv[rows:, :] = jnp.zeros_like(r.grad_conv[rows:, :])
            r.rim_out[...] = r.grad_conv[0:pad, :]
            rim_copy = remote(r.rim_out, r.rim_in, r.m_sem.at[0], r.m_sem.at[1], dict(dp=me - 1))

            @pl.when(place > 0)
            def _():
                rim_copy.start()

            yield 1
            convolved = None
            for k in range(KW):
                shifted = r.mixed[pad - KW + 1 + k : pad - KW + 1 + k + rows, :]
                term = taps[k : k + 1, :] * shifted
                convolved = term if convolved is None else convolved + term
                term = jnp.sum(r.grad_conv[0:rows, :] * shifted, axis=0, keepdims=True)
                r.small_out[5 + k : 6 + k, 0:channels] = term
            r.grad_projected[:, channels : 2 * channels] = (grad_gated * convolved).astype(BF16)

            @pl.when(place < SPAN - 1)
            def _():
                rim_copy.wait_recv()
                r.grad_conv[rows:, :] = r.rim_in[...]

            grad_mixed = None
            for k in range(KW):
                term = taps[k : k + 1, :] * r.grad_conv[KW - 1 - k : KW - 1 - k + rows, :]
                grad_mixed = term if grad_mixed is None else grad_mixed + term
            r.grad_projected[:, :channels] = (grad_mixed * signal).astype(BF16)
            r.grad_projected[:, 2 * channels :] = (grad_mixed * before).astype(BF16)

            @pl.when(place > 0)
            def _():
                rim_copy.wait_send()

            pump.ready += [4]
            yield 2
            for copy in fetch_conv(0):
                copy.start()
            for number in range(width // size):
                if number + 1 < width // size:
                    for copy in fetch_conv(number + 1):
                        copy.start()
                for copy in fetch_conv(number):
                    copy.wait()
                for at, owner in enumerate(block_owners(index)):
                    start = pl.multiple_of(owner * quarter, quarter)
                    made = None
                    for k in range(3):
                        piece = r.grad_projected[
                            pl.ds(start, quarter), k * channels : (k + 1) * channels
                        ]
                        term = cross(piece, r.conv_tile[number % 2, k])
                        made = term if made is None else made + term
                    r.partial[
                        at * quarter : (at + 1) * quarter, number * size : (number + 1) * size
                    ] = made.astype(BF16)
                if number % 2:
                    yield 1
            yield from sum_and_gather(
                r, r.partial, r.input_grad, None,
                lambda total, at, first: back_rows(
                    total, at, first, r.inputs, r.norm_conv, r.grad_one, None, r.gain_term
                ),
            )
            r.small_out[0:1, :] = r.gain_term[...]
            row = lax.broadcasted_iota(jnp.int32, small.shape, 0)
            for stage in range(stages):
                copy = remote(
                    r.small_out, r.slots.at[stage], r.s_send.at[stage], r.s_recv.at[stage],
                    small_peers[stage],
                )
                copy.start()
                yield 1
                copy.wait()
                if stage < 2:
                    r.small_out[...] += jnp.where(row < 5, r.slots[stage], 0.0)
                else:
                    r.small_out[...] += r.slots[stage]

        pump.run(2)
        for number in main():
            pump.run(number)
        pump.rest()

    return run_kernel(
        body,
        dict(
            grad_three_t=grad_three_t,
            normed_attn_t=normed_attn_t,
            grad_two_t=grad_two_t,
            norm_one_t=norm_one_t,
            normed_conv_t=normed_conv_t,
            attended=attended,
            grad_query=grad_query,
            grad_kv=grad_kv,
            active=active,
            gated=gated,
            grad_two_b=(grad_two_b, pl.ANY),
            down=(down, pl.ANY),
            gate_up_t=(gate_up_t, pl.ANY),
            gate=(gate, pl.ANY),
            upward=(upward, pl.ANY),
            one=one,
            norm_mlp=norm_mlp.reshape(1, -1),
            grad_two=grad_two,
            conv_out=conv_out,
            conv_in_t=(conv_in_t, pl.ANY),
            projected=projected,
            rim=rim,
            kernel=kernel,
            inputs=inputs,
            norm_conv=norm_conv.reshape(1, -1),
            small=small,
        ),
        dict(
            input_grad=((rows, width), BF16),
            small_out=(small.shape, F32),
            sum_attn_out=((block, channels), F32),
            sum_query=((block, columns), F32),
            sum_kv=((block, kv_columns), F32),
            sum_down=((block, units), F32),
            sum_gate=((block, units), F32),
            sum_up=((block, units), F32),
            sum_conv_out=((block, channels), F32),
            sum_conv_in=((3, block, channels), F32),
        ),
        dict(
            gathered=pltpu.VMEM((rows, width), BF16),
            partial=pltpu.VMEM((rows, width), BF16),
            grad_one_t=pltpu.VMEM((width, rows), BF16),
            grad_one=pltpu.VMEM((quarter, width), F32),
            grad_gate=pltpu.VMEM((rows, units), BF16),
            grad_up=pltpu.VMEM((rows, units), BF16),
            grad_projected=pltpu.VMEM((rows, 3 * channels), BF16),
            grad_gated=pltpu.VMEM((rows, channels), F32),
            mixed=pltpu.VMEM((rows + 8, channels), F32),
            grad_conv=pltpu.VMEM((rows + 8, channels), F32),
            rim_out=pltpu.VMEM((8, channels), F32),
            rim_in=pltpu.VMEM((8, channels), F32),
            m_sem=pltpu.SemaphoreType.DMA((2,)),
            e_sem=pltpu.SemaphoreType.DMA,
            down_tile=pltpu.VMEM((2, size, width), BF16),
            gate_tile=pltpu.VMEM((2, rows, size), F32),
            up_tile=pltpu.VMEM((2, rows, size), F32),
            h_sem=pltpu.SemaphoreType.DMA((2, 3)),
            conv_tile=pltpu.VMEM((2, 3, size, channels), BF16),
            c_sem=pltpu.SemaphoreType.DMA((2, 3)),
            gain_term=pltpu.VMEM((1, width), F32),
            slots=pltpu.VMEM((stages,) + small.shape, F32),
            s_send=pltpu.SemaphoreType.DMA((stages,)),
            s_recv=pltpu.SemaphoreType.DMA((stages,)),
            **stream_scratch(2, units, 128),
            **exchange_scratch(rows, width),
            **ring_scratch(devices, sides, block, widths),
        ),
        4,
        62,
        2 * rows * width * sum(widths) * 3,
    )


TILE = 256


def hidden_forward(normed_b, gate_up_t, down):
    rows, width = normed_b.shape
    units = down.shape[0]
    tiles = pl.cdiv(units, TILE)
    rest = units - (tiles - 1) * TILE

    def body(normed, weight, down_ref, partial, active, gate, upward, total):
        at = pl.program_id(0)
        a = cross(normed[...], weight[0])
        z = cross(normed[...], weight[1])
        gate[0] = a
        upward[0] = z
        s = (a * jax.nn.sigmoid(a) * z).astype(BF16)
        active[...] = s

        @pl.when(at == 0)
        def _():
            total[...] = jnp.dot(s, down_ref[...], preferred_element_type=F32)

        @pl.when((at > 0) & (at < tiles - 1))
        def _():
            total[...] += jnp.dot(s, down_ref[...], preferred_element_type=F32)

        @pl.when(at == tiles - 1)
        def _():
            last = jnp.dot(s[:, :rest], down_ref[0:rest, :], preferred_element_type=F32)
            partial[...] = (total[...] + last).astype(BF16)

    return pl.pallas_call(
        body,
        grid=(tiles,),
        in_specs=[
            pl.BlockSpec((rows, width), lambda i: (0, 0)),
            pl.BlockSpec((2, TILE, width), lambda i: (0, i, 0)),
            pl.BlockSpec((TILE, width), lambda i: (i, 0)),
        ],
        out_specs=[
            pl.BlockSpec((rows, width), lambda i: (0, 0)),
            pl.BlockSpec((rows, TILE), lambda i: (0, i)),
            pl.BlockSpec((1, rows, TILE), lambda i: (i, 0, 0)),
            pl.BlockSpec((1, rows, TILE), lambda i: (i, 0, 0)),
        ],
        out_shape=[
            jax.ShapeDtypeStruct((rows, width), BF16),
            jax.ShapeDtypeStruct((rows, units), BF16),
            jax.ShapeDtypeStruct((tiles, rows, TILE), F32),
            jax.ShapeDtypeStruct((tiles, rows, TILE), F32),
        ],
        scratch_shapes=[pltpu.VMEM((rows, width), F32)],
        compiler_params=pltpu.CompilerParams(vmem_limit_bytes=40 * 2**20),
    )(normed_b, gate_up_t, down)


def hidden_both(normed_b, gate_up_t, down, grad_b):
    rows, width = normed_b.shape
    units = down.shape[0]

    def body(normed, weight, down_ref, grad_ref, active, grad_gate, grad_up):
        a = cross(normed[...], weight[0])
        z = cross(normed[...], weight[1])
        grad = cross(grad_ref[...], down_ref[...])
        sigma = jax.nn.sigmoid(a)
        active[...] = (a * sigma * z).astype(BF16)
        grad_gate[...] = (grad * z * sigma * (1.0 + a * (1.0 - sigma))).astype(BF16)
        grad_up[...] = (grad * a * sigma).astype(BF16)

    whole = pl.BlockSpec((rows, width), lambda i: (0, 0))
    tile = pl.BlockSpec((rows, TILE), lambda i: (0, i))
    return pl.pallas_call(
        body,
        grid=(pl.cdiv(units, TILE),),
        in_specs=[
            whole,
            pl.BlockSpec((2, TILE, width), lambda i: (0, i, 0)),
            pl.BlockSpec((TILE, width), lambda i: (i, 0)),
            whole,
        ],
        out_specs=[tile] * 3,
        out_shape=[jax.ShapeDtypeStruct((rows, units), BF16)] * 3,
        compiler_params=pltpu.CompilerParams(vmem_limit_bytes=40 * 2**20),
    )(normed_b, gate_up_t, down, grad_b)


def local(
    tokens,
    lengths,
    norm_conv,
    conv_in,
    conv_kernel,
    conv_out,
    norm_mlp_one,
    gate_up_one,
    down_one,
    norm_attn,
    query_weight,
    kv_weight,
    query_gain,
    key_gain,
    attn_out,
    norm_mlp_two,
    gate_up_two,
    down_two,
    cotangent,
):
    row_count = tokens.shape[0]
    width = tokens.shape[1]
    quarter = row_count // 4
    channels = conv_out.shape[0]
    local_heads = query_weight.shape[1] // HEAD
    local_kv = kv_weight.shape[2] // HEAD
    device = lax.axis_index("dp")
    devices = lax.axis_size("dp")
    index = lax.axis_index("tensor")
    sequence = device // SPAN
    place_index = device % SPAN
    length = lengths[sequence]
    offsets = jnp.concatenate(
        [o * quarter + jnp.arange(quarter, dtype=jnp.int32) for o in block_owners(index)]
    )
    positions = place_index * row_count + offsets
    is_valid = positions < length
    frequency = THETA ** (-2.0 * jnp.arange(HEAD // 2, dtype=jnp.float32) / HEAD)
    angles = frequency[:, None] * positions.astype(jnp.float32)[None, :]
    tables = (jnp.cos(angles), jnp.sin(angles))
    where = position_inputs(positions, length)
    kernel = conv_kernel.astype(jnp.float32)
    rim_rows = KW - 1
    gate_up_one_t = jnp.transpose(gate_up_one, (1, 2, 0))
    gate_up_two_t = jnp.transpose(gate_up_two, (1, 2, 0))
    forward_route = [(i, i + 1) for i in range(devices - 1) if (i + 1) % SPAN]
    backward_route = [(b, a) for a, b in forward_route]

    inputs = tokens.astype(F32)
    normed_conv, inverse_conv = normalize(inputs, norm_conv)
    normed_conv_b = normed_conv.astype(BF16)
    weight_in = conv_in.reshape(width, 3 * channels)
    projected = matmul(normed_conv_b, weight_in)
    before = projected[:, :channels]
    after = projected[:, channels : 2 * channels]
    signal = projected[:, 2 * channels :]
    mixed = before * signal
    rim_in = lax.ppermute(mixed[row_count - rim_rows :], "dp", forward_route)
    padded = jnp.concatenate([rim_in, mixed], axis=0)
    convolved = kernel[0] * padded[0:row_count]
    for offset in range(1, KW):
        convolved = convolved + kernel[offset] * padded[offset : offset + row_count]
    gated_b = to_local((after * convolved).astype(BF16), index)
    inputs_own = lax.dynamic_slice_in_dim(tokens, index * quarter, quarter).astype(F32)

    norm_one_b, norm_one_t, one_own = norm_spread(
        matmul(gated_b, conv_out).astype(BF16), inputs_own, norm_mlp_one
    )
    partial_b, active_one, gate_a, up_a = hidden_forward(norm_one_b, gate_up_one_t, down_one)

    normed_attn_b, normed_attn_t, two_own = norm_spread(
        partial_b, one_own, norm_attn
    )
    kv_flat = kv_weight.reshape(width, 2 * local_kv * HEAD)
    (
        norm_two_b,
        norm_two_t,
        three_own,
        *kept,
        attended_b,
        attended_t,
        log_total,
    ) = attention_forward(
        normed_attn_b,
        query_weight,
        kv_flat,
        query_gain,
        key_gain,
        attn_out,
        two_own,
        norm_mlp_two,
        tables,
        where,
    )
    kept = (*kept, attended_t, log_total)

    grad_result = to_local(cotangent, index).astype(F32) * is_valid[:, None].astype(F32)
    grad_result_b = grad_result.astype(BF16)
    active_two, grad_gate_two, grad_up_two = hidden_both(
        norm_two_b, gate_up_two_t, down_two, grad_result_b
    )
    (
        grad_three_t,
        grad_query,
        grad_kv,
        grad_two_b,
        grad_two_t,
        grad_two,
        grad_norm_mlp_two,
        grad_norm_attn,
        part_query_gain,
        part_key_gain,
        sum_down_two,
        sum_gate_two,
        sum_up_two,
        output,
    ) = attention_backward(
        grad_result_b.T,
        norm_two_t,
        active_two,
        grad_gate_two,
        grad_up_two,
        gate_up_two_t,
        down_two,
        three_own,
        norm_mlp_two,
        grad_result[:quarter],
        kept,
        attn_out,
        query_weight,
        kv_flat,
        query_gain,
        key_gain,
        two_own,
        norm_attn,
        tables,
        where,
        devices,
    )

    small = jnp.concatenate(
        [
            jnp.zeros((2, width), F32),
            grad_norm_attn,
            grad_norm_mlp_two,
            jnp.pad(
                jnp.concatenate([part_query_gain[:, 0], part_key_gain[:, 0]]), (0, width - 2 * HEAD)
            ).reshape(1, width),
            jnp.zeros((KW, width), F32),
        ],
        axis=0,
    )
    (
        grad_inputs,
        small,
        sum_attn_out,
        sum_query,
        sum_kv,
        sum_down_one,
        sum_gate_one,
        sum_up_one,
        sum_conv_out,
        sum_conv_in,
    ) = first_backward(
        [grad_three_t, normed_attn_t, grad_two_t, norm_one_t, normed_conv_b.T],
        [attended_b, grad_query, grad_kv, active_one, gated_b],
        grad_two_b,
        down_one,
        gate_up_one_t,
        gate_a,
        up_a,
        one_own,
        norm_mlp_one,
        grad_two,
        conv_out,
        jnp.transpose(conv_in, (1, 0, 2)),
        projected,
        rim_in,
        conv_kernel,
        inputs_own,
        norm_conv,
        small,
        devices,
    )
    grad_inputs = to_true(grad_inputs, index).astype(F32)
    output = to_true(output, index)

    out_rows = width // devices
    return (
        output,
        grad_inputs,
        small[0],
        jnp.transpose(sum_conv_in, (1, 0, 2)),
        small[5:, :channels],
        sum_conv_out.T,
        small[1],
        jnp.stack([sum_gate_one, sum_up_one], axis=1),
        sum_down_one.T,
        small[2],
        sum_query,
        sum_kv.reshape(out_rows, 2, local_kv * HEAD),
        small[4, :HEAD],
        small[4, HEAD : 2 * HEAD],
        sum_attn_out.T,
        small[3],
        jnp.stack([sum_gate_two, sum_up_two], axis=1),
        sum_down_two.T,
    )


def solution(mesh):
    in_specs = (
        P("dp", None),
        P(),
        P(),
        P(None, None, "tensor"),
        P(None, "tensor"),
        P("tensor", None),
        P(),
        P(None, None, "tensor"),
        P("tensor", None),
        P(),
        P(None, "tensor"),
        P(None, None, "tensor"),
        P(),
        P(),
        P("tensor", None),
        P(),
        P(None, None, "tensor"),
        P("tensor", None),
        P("dp", None),
    )
    out_specs = (
        P("dp", None),
        P("dp", None),
        P(),
        P("dp", None, "tensor"),
        P(None, "tensor"),
        P("tensor", "dp"),
        P(),
        P("dp", None, "tensor"),
        P("tensor", "dp"),
        P(),
        P("dp", "tensor"),
        P("dp", None, "tensor"),
        P(),
        P(),
        P("tensor", "dp"),
        P(),
        P("dp", None, "tensor"),
        P("tensor", "dp"),
    )
    return jax.shard_map(local, mesh=mesh, in_specs=in_specs, out_specs=out_specs, check_vma=False)
```

time: 1050 us -> 643 us (0.61)
  Pallas kernels: 0 us -> 554 us
  waiting for transfers between devices: 444 us -> 0.01 us
  matrix products: 213 us -> 5.49 us
  starting transfers between devices: 163 us -> 5.95 us
  other arithmetic: 135 us -> 16.7 us
  between operations: 22 us -> 1.66 us
    pallas_call x0 -> x7, Pallas kernels: none -> 554 us  [the longest x5 528 us: run_kernel(): pl.pallas_call(lambda *refs: body(Refs(names, refs)), in_specs=specs, out...]
    ppermute x156 -> x0, waiting for transfers between devices: 443 us -> none  [the longest x112 376 us: sum_scatter(): held = lax.ppermute(total.astype(BF16), 'dp', self.routes[side])]
    dot_general x27 -> x0, matrix products: 172 us -> none  [the longest x11 36.9 us: inner_back(): lax.dot_general(left, right, (((1,), (1,)), ((), ())), preferred_element_...]
    ppermute x156 -> x0, starting transfers between devices: 158 us -> none  [the longest x112 121 us: sum_scatter(): held = lax.ppermute(total.astype(BF16), 'dp', self.routes[side])]
    convert_element_type x75 -> x3, other arithmetic: 52.1 us -> 3.15 us  [the longest x1 2.07 us: local(): grad_inputs = to_true(grad_inputs, index).astype(F32)]
    dot_general x11 -> x2, matrix products: 40.4 us -> 5.49 us  [matmul(): return jnp.dot(left, right, preferred_element_type=F32)]
    reduce_sum x10 -> x0, other arithmetic: 18.1 us -> none  [the longest x1 10.2 us: local(): total = jnp.sum(expo, axis=-1, keepdims=True)]
    add x19 -> x2, other arithmetic: 15.9 us -> 0.62 us  [local(): positions = place_index * row_count + offsets]
  transfers between devices with their start and end apart: 157 -> 1, of which waited for: 107 -> 0; matrix products, arithmetic and copies ran while one was open for 29% -> 3% of each run, Pallas kernels for 0% -> 0%
where the time goes in v3:
time: 643 us; the launch traced here: 639 us
  Pallas kernels  554 us (86%)
  local copies, waits for them, and re-layouts  55 us (9%)
  other arithmetic  16.7 us (3%)
    pallas_call x5, Pallas kernels, run_kernel(): pl.pallas_call(lambda *refs: body(Refs(names, refs)), in_specs=specs, out...  528 us
    unnamed x121, local copies, waits for them, and re-layouts  38 us
    pallas_call x1, Pallas kernels, hidden_forward(): pl.pallas_call(body, grid=(tiles,), in_specs=[pl.BlockSpec((rows, width),...  13.4 us
  transfers between devices with their start and end apart: 1, of which 0 were waited for; matrix products, arithmetic and copies ran while one was open for 3% of the time, Pallas kernels for 0%

profile of v3, /device:TPU:0, one launch (start us, length us, event | category | flops | bytes accessed | tf_op | source)
XLA Modules:
  0.0 639.0 jit_solution(17810452110864132301)
XLA Ops:
  0.7 1.7 copy.62
  2.8 6.2 copy.63
  9.0 4.5 fusion.11.refs_20_
  15.2 6.0 collective-permute-start
  21.3 1.6 fusion.10.refs_4_
  26.6 2.0 convert_multiply_fusion.2
  35.2 1.6 copy.67.refs_0_
  36.7 2.1 slice.77.refs_9_
  38.8 2.3 fusion.8
  42.9 22.4 %shard_map.322 = (bf16[512,1536]{1,0:T(8,128)(2,1)S(1)}, bf16[1536,512]{1,0:T(8,128)(2,1)S(1)}, f32[128,1536]{1,0:T(8,128)S(1)}) custom-call(bf16[512,1536]{1,0:T(8,128)(2,1)S(1)} %convolution_convert_fusion.refs_0_, f32[128,1536]{1,0:T(8,128)S(1)} %dynamic-slice_convert_fusion.refs_1_.refs_23_, f32[1,1536]{1,0:T(1,128)S(1)} %reshape.211.refs_2_.refs_16_), custom_call_target="tpu_custom_call" | custom-call | flops 7864320 | bytes 2365440 | tf_op jit(solution)/shard_map/pallas_call | solution.py:58
  66.5 13.4 %shard_map.323 = (bf16[512,1536]{1,0:T(8,128)(2,1)S(1)}, bf16[512,1728]{1,0:T(8,128)(2,1)S(1)}, f32[7,512,256]{2,1,0:T(8,128)S(1)}, f32[7,512,256]{2,1,0:T(8,128)S(1)}) custom-call(bf16[512,1536]{1,0:T(8,128)(2,1)S(1)} %get-tuple-element.66.normed, bf16[2,1728,1536]{2,1,0:T(8,128)(2,1)} %bitcast.54, bf16[1728,1536]{1,0:T(8,128)(2,1)} %refs_11_.1), custom_call_target="tpu_custom_call" | custom-call | tf_op jit(solution)/shard_map/pallas_call | solution.py:1147
  79.9 1.8 copy-done.13
  81.8 1.9 copy-done.14
  83.7 22.4 %shard_map.324 = (bf16[512,1536]{1,0:T(8,128)(2,1)S(1)}, bf16[1536,512]{1,0:T(8,128)(2,1)S(1)}, f32[128,1536]{1,0:T(8,128)S(1)}) custom-call(bf16[512,1536]{1,0:T(8,128)(2,1)S(1)} %get-tuple-element.67.refs_0_, f32[128,1536]{1,0:T(8,128)S(1)} %get-tuple-element.68.refs_1_.refs_15_, f32[1,1536]{1,0:T(1,128)S(1)} %reshape.212.refs_2_.refs_23_), custom_call_target="tpu_custom_call" | custom-call | flops 7864320 | bytes 2365440 | tf_op jit(solution)/shard_map/pallas_call | solution.py:58
  109.5 33.8 %shard_map.325 = (bf16[512,1536]{1,0:T(8,128)(2,1)}, bf16[1536,512]{1,0:T(8,128)(2,1)}, f32[128,1536]{1,0:T(8,128)S(1)}, f32[384,512]{1,0:T(8,128)S(1)}, f32[128...) custom-call(bf16[512,1536]{1,0:T(8,128)(2,1)} %copy-done.21, ...), custom_call_target="tpu_custom_call" | custom-call | flops 6442450944 | bytes 5646852 | tf_op jit(solution)/shard_map/pallas_call | solution.py:58
  143.4 2.6 copy-done.1
  146.0 12.7 %shard_map.326 = (bf16[512,1728]{1,0:T(8,128)(2,1)S(1)}, bf16[512,1728]{1,0:T(8,128)(2,1)S(1)}, bf16[512,1728]{1,0:T(8,128)(2,1)S(1)}) custom-call(bf16[512,1536]{1,0:T(8,128)(2,1)S(1)} %copy-done.1, bf16[2,1728,1536]{2,1,0:T(8,128)(2,1)} %bitcast.52, bf16[1728,1536]{1,0:T(8,128)(2,1)S(1)} %bitcast.49, bf16[512,1536]{1,0:T(8,128)(2,1)S(1)} %get-tuple-element.176.grad_ref), custom_call_target="tpu_custom_call" | custom-call | tf_op jit(solution)/shard_map/pallas_call | solution.py:1187
  162.5 202.9 %shard_map.327 = (bf16[1536,512]{1,0:T(8,128)(2,1)}, bf16[512,384]{1,0:T(8,128)(2,1)}, bf16[512,256]{1,0:T(8,128)(2,1)}, bf16[512,1536]{1,0:T(8,128)(2,1)}, bf16...) custom-call(bf16[1536,512]{1,0:T(8,128)(2,1)} %copy.67.refs_0_, ...), custom_call_target="tpu_custom_call" | custom-call | flops 27179089920 | bytes 33321476 | tf_op jit(solution)/shard_map/pallas_call | solution.py:58
  368.6 246.5 %shard_map.328 = (bf16[512,1536]{1,0:T(8,128)(2,1)}, f32[8,1536]{1,0:T(8,128)}, f32[192,384]{1,0:T(8,128)}, f32[192,384]{1,0:T(8,128)}, f32[192,256]{1,0:T(8,128...) custom-call(bf16[1536,512]{1,0:T(8,128)(2,1)} %get-tuple-element.85., ...), custom_call_target="tpu_custom_call" | custom-call | flops 36540776448 | bytes 45417728 | tf_op jit(solution)/shard_map/pallas_call | solution.py:58
  615.1 1.6 slice_reduce_fusion
  619.4 1.5 pad_maximum_fusion.1
  620.9 3.7 copy.71
  624.8 3.7 copy.70
  630.0 2.1 maximum_convert_fusion
  (162 shorter events, 36.5 us)
Async XLA Ops:
  15.2 23.6 %collective-permute-start = (f32[2,384]{1,0:T(2,128)}, f32[2,384]{1,0:T(2,128)}, u32[]{:S(2)}, u32[]{:S(2)}) collective-permute-start(f32[2,384]{1,0:T(2,128)} %slice.72), channel_id=1, source_target_pairs={{0,4},{4,8},{8,12},{16,20},{20,24},{24,28},{1,5},{5,9},{9,13},{17,... | collective-permute-start | bytes 9224 | tf_op jit(solution)/shard_map/ppermute | solution.py:1260
  24.6 18.3 %copy-start = (f32[128,1536]{1,0:T(8,128)}, f32[128,1536]{1,0:T(8,128)S(1)}, u32[]{:S(2)}) copy-start(f32[128,1536]{1,0:T(8,128)S(1)} %dynamic-slice_convert_fusion.refs_1_.refs_23_) | copy-start | bytes 2359300
  25.4 84.0 %copy-start.4 = (s32[512,1]{1,0:T(8,128)}, s32[512,1]{1,0:T(8,128)S(1)}, u32[]{:S(2)}) copy-start(s32[512,1]{1,0:T(8,128)S(1)} %broadcast_add_fusion.refs_12_.refs_28_) | copy-start | bytes 6148
  26.4 83.0 %copy-start.5 = (f32[32,512]{1,0:T(8,128)}, f32[32,512]{1,0:T(8,128)S(1)}, u32[]{:S(2)}) copy-start(f32[32,512]{1,0:T(8,128)S(1)} %get-tuple-element.195.refs_9_.refs_25_) | copy-start | bytes 196612
  26.4 82.9 %copy-start.6 = (f32[32,512]{1,0:T(8,128)}, f32[32,512]{1,0:T(8,128)S(1)}, u32[]{:S(2)}) copy-start(f32[32,512]{1,0:T(8,128)S(1)} %get-tuple-element.196.refs_8_.refs_24_) | copy-start | bytes 196612
  29.9 53.8 %copy-start.10 = (f32[1,1536]{1,0:T(1,128)}, f32[1,1536]{1,0:T(1,128)S(1)}, u32[]{:S(2)}) copy-start(f32[1,1536]{1,0:T(1,128)S(1)} %reshape.212.refs_2_.refs_23_) | copy-start | bytes 18436
  31.1 78.3 %copy-start.2 = (bf16[192,8,2,128]{3,1,2,0:T(8,128)(2,1)}, bf16[192,8,2,128]{3,1,2,0:T(8,128)(2,1)S(1)}, u32[]{:S(2)}) copy-start(bf16[192,8,2,128]{3,1,2,0:T(8,128)(2,1)S(1)} %copy.74) | copy-start | bytes 2359300
  66.5 17.1 %copy-start.3 = (f32[128,1536]{1,0:T(8,128)}, f32[128,1536]{1,0:T(8,128)S(1)}, u32[]{:S(2)}) copy-start(f32[128,1536]{1,0:T(8,128)S(1)} %get-tuple-element.68.refs_1_.refs_15_) | copy-start | bytes 2359300
  83.6 25.8 %copy-start.15 = (bf16[512,1728]{1,0:T(8,128)(2,1)}, bf16[512,1728]{1,0:T(8,128)(2,1)S(1)}, u32[]{:S(2)}) copy-start(bf16[512,1728]{1,0:T(8,128)(2,1)S(1)} %get-tuple-element.92.refs_8_) | copy-start | bytes 5308420
  83.6 25.8 %copy-start.7 = (f32[64,1]{1,0:T(8,128)S(1)}, f32[64,1]{1,0:T(8,128)}, u32[]{:S(2)}) copy-start(f32[64,1]{1,0:T(8,128)} %copy.65.refs_3_.refs_20_) | copy-start | bytes 772
  83.6 25.8 %copy-start.8 = (f32[64,1]{1,0:T(8,128)S(1)}, f32[64,1]{1,0:T(8,128)}, u32[]{:S(2)}) copy-start(f32[64,1]{1,0:T(8,128)} %copy.66.refs_4_.refs_21_) | copy-start | bytes 772
  83.6 25.8 %copy-start.11 = (f32[1,1536]{1,0:T(1,128)S(1)}, f32[1,1536]{1,0:T(1,128)}, u32[]{:S(2)}) copy-start(f32[1,1536]{1,0:T(1,128)} %reshape.216.refs_7_.refs_8_) | copy-start | bytes 18436
  83.6 25.8 %copy-start.12 = (s32[1,512]{1,0:T(1,128)S(1)}, s32[1,512]{1,0:T(1,128)}, u32[]{:S(2)}) copy-start(s32[1,512]{1,0:T(1,128)} %add_add_fusion.1.refs_11_.refs_27_) | copy-start | bytes 6148
  109.4 34.0 %slice-start = ((s8[5308416]{0:T(1024)(128)(4,1)}), s8[4194304]{0:T(1024)(128)(4,1)S(1)}, s32[]{:S(2)}) async-start(s8[5308416]{0:T(1024)(128)(4,1)} %bitcast.48), calls=%async_computation | async-start | bytes 8388608
  109.5 33.9 %slice-start.1 = ((s8[5308416]{0:T(1024)(128)(4,1)}), s8[1114112]{0:T(1024)(128)(4,1)S(1)}, s32[]{:S(2)}) async-start(s8[5308416]{0:T(1024)(128)(4,1)} %bitcast.48), calls=%async_computation.1 | async-start | bytes 2228224
  143.3 15.4 %copy-start.23 = (f32[128,1536]{1,0:T(8,128)}, f32[128,1536]{1,0:T(8,128)S(1)}, u32[]{:S(2)}) copy-start(f32[128,1536]{1,0:T(8,128)S(1)} %get-tuple-element.76.refs_7_) | copy-start | bytes 2359300
  143.3 15.4 %copy-start.24 = (f32[384,512]{1,0:T(8,128)}, f32[384,512]{1,0:T(8,128)S(1)}, u32[]{:S(2)}) copy-start(f32[384,512]{1,0:T(8,128)S(1)} %get-tuple-element.77.refs_10_) | copy-start | bytes 2359300
  143.3 15.4 %copy-start.25 = (bf16[3,512,256]{2,1,0:T(8,128)(2,1)}, bf16[3,512,256]{2,1,0:T(8,128)(2,1)S(1)}, u32[]{:S(2)}) copy-start(bf16[3,512,256]{2,1,0:T(8,128)(2,1)S(1)} %get-tuple-element.81.refs_14_) | copy-start | bytes 2359300
  143.3 15.4 %copy-start.26 = (f32[384,512]{1,0:T(8,128)}, f32[384,512]{1,0:T(8,128)S(1)}, u32[]{:S(2)}) copy-start(f32[384,512]{1,0:T(8,128)S(1)} %get-tuple-element.82.refs_15_) | copy-start | bytes 2359300
  143.3 15.4 %copy-start.27 = (bf16[512,384]{1,0:T(8,128)(2,1)}, bf16[512,384]{1,0:T(8,128)(2,1)S(1)}, u32[]{:S(2)}) copy-start(bf16[512,384]{1,0:T(8,128)(2,1)S(1)} %get-tuple-element.89.refs_5_) | copy-start | bytes 1179652
  143.3 15.4 %copy-start.28 = (bf16[384,512]{1,0:T(8,128)(2,1)}, bf16[384,512]{1,0:T(8,128)(2,1)S(1)}, u32[]{:S(2)}) copy-start(bf16[384,512]{1,0:T(8,128)(2,1)S(1)} %get-tuple-element.79.refs_12_) | copy-start | bytes 1179652
  143.3 15.4 %copy-start.29 = (f32[128,512]{1,0:T(8,128)}, f32[128,512]{1,0:T(8,128)S(1)}, u32[]{:S(2)}) copy-start(f32[128,512]{1,0:T(8,128)S(1)} %get-tuple-element.78.refs_11_) | copy-start | bytes 786436
  143.3 15.4 %copy-start.30 = (bf16[512,256]{1,0:T(8,128)(2,1)}, bf16[512,256]{1,0:T(8,128)(2,1)S(1)}, u32[]{:S(2)}) copy-start(bf16[512,256]{1,0:T(8,128)(2,1)S(1)} %get-tuple-element.80.refs_13_) | copy-start | bytes 786436
  368.6 250.8 %copy-start.38 = (f32[192,1728]{1,0:T(8,128)S(1)}, f32[192,1728]{1,0:T(8,128)}, u32[]{:S(2)}) copy-start(f32[192,1728]{1,0:T(8,128)} %get-tuple-element.111) | copy-start | bytes 3981316
  (32 other events, 106.3 us)

commit v4 on v3

--- a/solution.py
+++ b/solution.py
@@ -43,23 +43,95 @@
 MESH = pl.DeviceIdType.MESH
 
 
+class Lazy:
+    def __init__(self, value, dtype=None):
+        self.value, self.dtype = value, dtype
+
+
 class Refs:
     def __init__(self, names, refs):
         self.__dict__.update(zip(names, refs))
 
+    def begin(self, inputs, outputs, refs):
+        self.arriving, self.leaving, self.homes = {}, [], {}
+        for at, name in enumerate(inputs):
+            ref = self.__dict__[name]
+            copy = pltpu.make_async_copy(refs[at], ref, self.lazy_in.at[at])
+            copy.start()
+            self.arriving[id(ref)] = copy
+        for at, name in enumerate(outputs):
+            self.homes[id(self.__dict__[name])] = (refs[len(inputs) + at], at)
+
+    def need(self, *refs):
+        for ref in refs:
+            self.arriving.pop(id(ref)).wait()
+
+    def flush(self, *refs):
+        for ref in refs:
+            home, at = self.homes.pop(id(ref))
+            copy = pltpu.make_async_copy(ref, home, self.lazy_out.at[at, 0])
+            copy.start()
+            self.leaving.append(copy)
+
+    def flush_blocks(self, ref, owners):
+        home, at = self.homes.pop(id(ref))
+        rows = ref.shape[0] // 4
+        for block, owner in enumerate(owners):
+            copy = pltpu.make_async_copy(
+                ref.at[pl.ds(block * rows, rows)],
+                home.at[pl.ds(pl.multiple_of(owner * rows, rows), rows)],
+                self.lazy_out.at[at, block],
+            )
+            copy.start()
+            self.leaving.append(copy)
+
+    def end(self):
+        assert not self.homes
+        for copy in list(self.arriving.values()) + self.leaving:
+            copy.wait()
+
 
 def run_kernel(body, inputs, outputs, scratch, collective_id, limit, flops):
-    arrays, specs = [], []
-    for value in inputs.values():
-        array, space = value if isinstance(value, tuple) else (value, pltpu.VMEM)
+    arrays, specs, names, out_names = [], [], [], []
+    scratch = dict(scratch)
+    lazy_in = [name for name, value in inputs.items() if isinstance(value, Lazy)]
+    lazy_out = [name for name, value in outputs.items() if isinstance(value, Lazy)]
+    for name, value in inputs.items():
+        if isinstance(value, Lazy):
+            array, space = value.value, pl.ANY
+            scratch[name] = pltpu.VMEM(array.shape, array.dtype)
+            names.append(None)
+        else:
+            array, space = value if isinstance(value, tuple) else (value, pltpu.VMEM)
+            names.append(name)
         arrays.append(array)
         specs.append(pl.BlockSpec(memory_space=space))
-    names = list(inputs) + list(outputs) + list(scratch)
+    shapes, out_specs = [], []
+    for name, value in outputs.items():
+        if isinstance(value, Lazy):
+            shape, dtype, space = value.value, value.dtype, pl.ANY
+            scratch[name] = pltpu.VMEM(shape, dtype)
+            names.append(None)
+        else:
+            (shape, dtype), space = value, pltpu.VMEM
+            names.append(name)
+        shapes.append(jax.ShapeDtypeStruct(shape, dtype))
+        out_specs.append(pl.BlockSpec(memory_space=space))
+    scratch["lazy_in"] = pltpu.SemaphoreType.DMA((max(len(lazy_in), 1),))
+    scratch["lazy_out"] = pltpu.SemaphoreType.DMA((max(len(lazy_out), 1), 4))
+    names += list(scratch)
+
+    def whole(*refs):
+        r = Refs([n for n in names if n], [ref for n, ref in zip(names, refs) if n])
+        r.begin(lazy_in, lazy_out, [ref for n, ref in zip(names, refs) if not n])
+        body(r)
+        r.end()
+
     return pl.pallas_call(
-        lambda *refs: body(Refs(names, refs)),
+        whole,
         in_specs=specs,
-        out_specs=[pl.BlockSpec(memory_space=pltpu.VMEM)] * len(outputs),
-        out_shape=[jax.ShapeDtypeStruct(*value) for value in outputs.values()],
+        out_specs=out_specs,
+        out_shape=shapes,
         scratch_shapes=list(scratch.values()),
         compiler_params=pltpu.CompilerParams(
             collective_id=collective_id, has_side_effects=True, vmem_limit_bytes=limit * 2**20
@@ -171,47 +243,10 @@
         pass
 
 
-def spread(partial_b, extras, out_shapes, compute, collective_id):
-    rows, width = partial_b.shape
-
-    def body(r):
-        greet(tensor_peers())
-        exhaust(
-            sum_and_gather(
-                r, r.partial, r.gathered, r.gathered_t, lambda *values: compute(r, *values)
-            )
-        )
-
-    outputs = dict(gathered=((rows, width), BF16), gathered_t=((width, rows), BF16))
-    outputs.update({name: (shape, F32) for name, shape in out_shapes.items()})
-    return run_kernel(
-        body,
-        dict(partial=partial_b, **extras),
-        outputs,
-        exchange_scratch(rows, width),
-        collective_id,
-        32,
-        10 * rows * width,
-    )
-
-
 def norm_rows(total, rows, residual, gain, hidden):
     values = residual[rows, :] + total
     hidden[rows, :] = values
     return normalize(values, gain[...])[0].astype(BF16)
-
-
-def norm_spread(partial_b, residual, gain):
-    def compute(r, total, rows, first):
-        return norm_rows(total, rows, r.residual, r.gain, r.hidden)
-
-    return spread(
-        partial_b,
-        dict(residual=residual, gain=gain.reshape(1, -1)),
-        dict(hidden=residual.shape),
-        compute,
-        1,
-    )
 
 
 def back_rows(total, rows, first, hidden, gain, incoming, own, grad_gain):
@@ -224,19 +259,6 @@
     term = term.reshape(1, -1)
     grad_gain[...] = term if first else grad_gain[...] + term
     return made.astype(BF16)
-
-
-def back_spread(partial_b, hidden, gain, incoming):
-    def compute(r, total, rows, first):
-        return back_rows(total, rows, first, r.hidden, r.gain, r.incoming, r.own, r.grad_gain)
-
-    return spread(
-        partial_b,
-        dict(hidden=hidden, gain=gain.reshape(1, -1), incoming=incoming),
-        dict(own=hidden.shape, grad_gain=(1, hidden.shape[1])),
-        compute,
-        3,
-    )
 
 
 def ring_peers(count):
@@ -356,23 +378,6 @@
     return [index, index ^ 2, index ^ 1, index ^ 3]
 
 
-def to_local(values, index):
-    quarter = values.shape[0] // 4
-    return jnp.concatenate(
-        [lax.dynamic_slice_in_dim(values, o * quarter, quarter) for o in block_owners(index)]
-    )
-
-
-def to_true(values, index):
-    quarter = values.shape[0] // 4
-    places = []
-    for block in range(4):
-        shift = block ^ index
-        place = ((shift & 1) << 1) | (shift >> 1)
-        places.append(lax.dynamic_slice_in_dim(values, place * quarter, quarter))
-    return jnp.concatenate(places)
-
-
 def cross(left, right):
     return lax.dot_general(left, right, (((1,), (1,)), ((), ())), preferred_element_type=F32)
 
@@ -417,17 +422,21 @@
 
 
 def attention_forward(
-    normed_b, query_weight, kv_weight, query_gain, key_gain, attn_out, residual, gain, tables, where
+    normed_b, query_weight, kv_weight, query_gain, key_gain, attn_out, residual, gain, tables, where,
+    gate_up_t, down, grad_b,
 ):
     rows, width = normed_b.shape
     columns = query_weight.shape[1]
     kv_columns = kv_weight.shape[1] // 2
     heads, kv_heads = columns // HEAD, kv_columns // HEAD
+    units = down.shape[0]
 
     def body(r):
         me = lax.axis_index("dp")
         place = lax.rem(me, SPAN)
         greet(tensor_peers() + span_peers())
+        for copy in hidden_fetch(r, 0, TILE):
+            copy.start()
 
         def pass_on(distance):
             return remote(
@@ -435,6 +444,7 @@
                 dict(dp=me + distance),
             )
 
+        r.need(r.normed, r.kv_weight, r.cosine, r.sine)
         cosine, sine = r.cosine[...], r.sine[...]
         made = jnp.dot(r.normed[...], r.kv_weight[...], preferred_element_type=F32)
         r.key_raw[...] = made[:, :kv_columns].T
@@ -449,6 +459,7 @@
             def _():
                 pass_on(distance).start()
 
+        r.need(r.query_weight)
         made = jnp.dot(r.normed[...], r.query_weight[...], preferred_element_type=F32)
         r.query_raw[...] = made.T
         for head in range(heads):
@@ -477,12 +488,11 @@
                         r.attended_t[at, :] += made
 
         part(r.own[...], True)
-        for distance in range(1, SPAN):
-
-            @pl.when(place >= distance)
-            def _():
-                pass_on(distance).wait_recv()
-                part(r.near[distance - 1], False)
+
+        @pl.loop(1, place + 1)
+        def _(distance):
+            pass_on(distance).wait_recv()
+            part(r.near[distance - 1], False)
 
         for head in range(heads):
             at = head_rows(head)
@@ -490,6 +500,8 @@
             r.attended_t[at, :] = made
             r.attended[:, at] = made.T.astype(BF16)
         r.log_total[...] = jnp.log(r.total[...])
+        r.need(r.attn_out, r.residual, r.grad_b)
+        r.flush(r.query_raw, r.key_raw, r.query, r.own, r.near, r.attended, r.attended_t, r.log_total)
         r.partial[...] = jnp.dot(
             r.attended[...], r.attn_out[...], preferred_element_type=F32
         ).astype(BF16)
@@ -499,51 +511,72 @@
                 lambda total, at, first: norm_rows(total, at, r.residual, r.gain, r.hidden),
             )
         )
+        r.flush(r.gathered_t, r.hidden)
         for distance in range(1, SPAN):
 
             @pl.when(place + distance < SPAN)
             def _():
                 pass_on(distance).wait_send()
 
+        def tile(number, wide, gate_w, up_w, down_w):
+            lanes = tile_lanes(number, wide)
+            a = cross(r.gathered[...], gate_w)
+            z = cross(r.gathered[...], up_w)
+            grad = cross(r.grad_b[...], down_w)
+            sigma = jax.nn.sigmoid(a)
+            r.active[:, lanes] = (a * sigma * z).astype(BF16)
+            r.grad_gate[:, lanes] = (grad * z * sigma * (1.0 + a * (1.0 - sigma))).astype(BF16)
+            r.grad_up[:, lanes] = (grad * a * sigma).astype(BF16)
+
+        hidden_tiles(r, units, tile)
+        r.flush(r.active, r.grad_gate, r.grad_up)
+
     return run_kernel(
         body,
         dict(
-            normed=normed_b,
-            query_weight=query_weight,
-            kv_weight=kv_weight,
+            normed=Lazy(normed_b),
+            query_weight=Lazy(query_weight),
+            kv_weight=Lazy(kv_weight),
             query_gain=query_gain.reshape(HEAD, 1),
             key_gain=key_gain.reshape(HEAD, 1),
-            attn_out=attn_out,
-            residual=residual,
+            attn_out=Lazy(attn_out),
+            residual=Lazy(residual),
             gain=gain.reshape(1, -1),
-            cosine=tables[0],
-            sine=tables[1],
+            cosine=Lazy(tables[0]),
+            sine=Lazy(tables[1]),
+            gate_up_t=(gate_up_t, pl.ANY),
+            down=(down, pl.ANY),
+            grad_b=Lazy(grad_b),
             **where,
         ),
         dict(
-            gathered=((rows, width), BF16),
-            gathered_t=((width, rows), BF16),
-            hidden=(residual.shape, F32),
-            query_raw=((columns, rows), F32),
-            key_raw=((kv_columns, rows), F32),
-            query=((columns, rows), BF16),
-            own=((rows, 2 * kv_columns), BF16),
-            near=((SPAN - 1, rows, 2 * kv_columns), BF16),
-            attended=((rows, columns), BF16),
-            attended_t=((columns, rows), F32),
-            log_total=((heads, rows), F32),
+            active=Lazy((rows, units), BF16),
+            grad_gate=Lazy((rows, units), BF16),
+            grad_up=Lazy((rows, units), BF16),
+            gathered_t=Lazy((width, rows), BF16),
+            hidden=Lazy(residual.shape, F32),
+            query_raw=Lazy((columns, rows), F32),
+            key_raw=Lazy((kv_columns, rows), F32),
+            query=Lazy((columns, rows), BF16),
+            own=Lazy((rows, 2 * kv_columns), BF16),
+            near=Lazy((SPAN - 1, rows, 2 * kv_columns), BF16),
+            attended=Lazy((rows, columns), BF16),
+            attended_t=Lazy((columns, rows), F32),
+            log_total=Lazy((heads, rows), F32),
         ),
         dict(
             keys_t=pltpu.VMEM((kv_columns, rows), BF16),
             bias=pltpu.VMEM((rows, rows), F32),
             total=pltpu.VMEM((heads, rows), F32),
             partial=pltpu.VMEM((rows, width), BF16),
+            gathered=pltpu.VMEM((rows, width), BF16),
+            **hidden_scratch(width),
             p_send=pltpu.SemaphoreType.DMA((SPAN - 1,)),
             p_recv=pltpu.SemaphoreType.DMA((SPAN - 1,)),
             **exchange_scratch(rows, width),
         ),
         2,
-        48,
+        58,
         16 * rows * rows * SPAN * columns,
     )
 
@@ -604,7 +637,13 @@
         place = lax.rem(me, SPAN)
 
         def store(seg, column, value):
-            (r.sum_down, r.sum_gate, r.sum_up)[seg][...] = value
+            if seg == 0:
+                r.sum_down[...] = value
+                r.flush(r.sum_down)
+            else:
+                r.sum_gate_up[:, seg - 1, :] = value
+                if seg == 2:
+                    r.flush(r.sum_gate_up)
 
         rings = Rings(
             devices, sides,
@@ -651,12 +690,15 @@
         def main():
             yield from stream_product(r, [r.grad_gate, r.grad_up], r.gate_up_t, r.partial)
             fill_bias(r)
+            r.need(r.three, r.incoming)
             yield from sum_and_gather(
                 r, r.partial, r.gathered, r.grad_three_t,
                 lambda total, at, first: back_rows(
                     total, at, first, r.three, r.norm_mlp, r.incoming, r.grad_three, r.grad_norm_mlp
                 ),
             )
+            r.flush(r.grad_three_t)
+            r.need(r.attn_out, r.attended_t, r.own, r.near, r.query, r.log_total)
             r.grads[...] = cross(r.gathered[...], r.attn_out[...]).astype(BF16)
             for head in range(heads):
                 at = head_rows(head)
@@ -671,17 +713,17 @@
 
             part(r.own[...], write_own, True)
             yield 1
-            for distance in range(1, SPAN):
-
-                @pl.when(place >= distance)
-                def _():
-                    def write_far(at, value):
-                        r.far[distance - 1, :, at] = value.astype(BF16)
-
-                    part(r.near[distance - 1], write_far, False)
-                    pass_back(distance).start()
-
-                yield 1
+
+            @pl.loop(1, place + 1)
+            def _(distance):
+                def write_far(at, value):
+                    r.far[distance - 1, :, at] = value.astype(BF16)
+
+                part(r.near[distance - 1], write_far, False)
+                pass_back(distance).start()
+
+            yield 2
+            r.need(r.cosine, r.sine, r.query_raw, r.key_raw, r.query_weight, r.kv_weight, r.two)
             cosine, sine = r.cosine[...], r.sine[...]
             terms = None
             for head in range(heads):
@@ -708,6 +750,7 @@
                 r.grad_kv[:, at] = made.T.astype(BF16)
             r.grad_key_gain[...] = jnp.sum(terms, axis=1, keepdims=True)
             r.grad_kv[:, kv_columns:] = r.grad_own[:, kv_columns:].astype(BF16)
+            r.flush(r.grad_query, r.grad_kv)
             r.partial[...] = (
                 cross(r.grad_query[...], r.query_weight[...]) + cross(r.grad_kv[...], r.kv_weight[...])
             ).astype(BF16)
@@ -718,6 +761,7 @@
                     total, at, first, r.two, r.norm_attn, r.grad_three, r.grad_two, r.grad_norm_attn
                 ),
             )
+            r.flush(r.grad_two_b, r.grad_two_t, r.grad_two)
             for distance in range(1, SPAN):
 
                 @pl.when(place >= distance)
@@ -729,57 +773,63 @@
                 r, r.partial, r.output, None,
                 lambda total, at, first: (r.three[at, :] + total).astype(BF16),
             )
-
-        order = [(seg, step) for step in range(devices) for seg in range(3)]
-        interleave(main(), [lambda u=u: rings.unit(*u) for u in order], 3)
+            r.flush_blocks(r.output, block_owners(lax.axis_index("tensor")))
+
+        def first(seg):
+            r.need(*((r.grad_b_t, r.active), (r.norm_two_t, r.grad_gate), (r.grad_up,))[seg])
+            rings.unit(seg, 0)
+
+        order = [(seg, step) for step in range(1, devices) for seg in range(3)]
+        units_left = [lambda s=seg: first(s) for seg in range(3)]
+        units_left += [lambda u=u: rings.unit(*u) for u in order]
+        interleave(main(), units_left, 3)
 
     quarter = rows // 4
     return run_kernel(
         body,
         dict(
-            grad_b_t=grad_b_t,
-            norm_two_t=norm_two_t,
-            active=active,
-            grad_gate=grad_gate,
-            grad_up=grad_up,
+            grad_b_t=Lazy(grad_b_t),
+            active=Lazy(active),
+            norm_two_t=Lazy(norm_two_t),
+            grad_gate=Lazy(grad_gate),
+            grad_up=Lazy(grad_up),
             gate_up_t=(gate_up_t, pl.ANY),
             down=(down.reshape((1,) + down.shape), pl.ANY),
-            three=three,
+            three=Lazy(three),
             norm_mlp=norm_mlp.reshape(1, -1),
-            incoming=incoming,
-            query_raw=query_raw,
-            key_raw=key_raw,
-            query=query,
-            own=own,
-            near=near,
-            attended_t=attended_t,
-            log_total=log_total,
-            attn_out=attn_out,
-            query_weight=query_weight,
-            kv_weight=kv_weight,
+            incoming=Lazy(incoming),
+            query_raw=Lazy(query_raw),
+            key_raw=Lazy(key_raw),
+            query=Lazy(query),
+            own=Lazy(own),
+            near=Lazy(near),
+            attended_t=Lazy(attended_t),
+            log_total=Lazy(log_total),
+            attn_out=Lazy(attn_out),
+            query_weight=Lazy(query_weight),
+            kv_weight=Lazy(kv_weight),
             query_gain=query_gain.reshape(HEAD, 1),
             key_gain=key_gain.reshape(HEAD, 1),
-            two=two,
+            two=Lazy(two),
             norm_attn=norm_attn.reshape(1, -1),
-            cosine=tables[0],
-            sine=tables[1],
+            cosine=Lazy(tables[0]),
+            sine=Lazy(tables[1]),
             **where,
         ),
         dict(
-            grad_three_t=((width, rows), BF16),
-            grad_query=((rows, columns), BF16),
-            grad_kv=((rows, 2 * kv_columns), BF16),
-            grad_two_b=((rows, width), BF16),
-            grad_two_t=((width, rows), BF16),
-            grad_two=((quarter, width), F32),
+            grad_three_t=Lazy((width, rows), BF16),
+            grad_query=Lazy((rows, columns), BF16),
+            grad_kv=Lazy((rows, 2 * kv_columns), BF16),
+            grad_two_b=Lazy((rows, width), BF16),
+            grad_two_t=Lazy((width, rows), BF16),
+            grad_two=Lazy((quarter, width), F32),
             grad_norm_mlp=((1, width), F32),
             grad_norm_attn=((1, width), F32),
             grad_query_gain=((HEAD, 1), F32),
             grad_key_gain=((HEAD, 1), F32),
-            sum_down=((block, units), F32),
-            sum_gate=((block, units), F32),
-            sum_up=((block, units), F32),
-            output=((rows, width), BF16),
+            sum_down=Lazy((block, units), F32),
+            sum_gate_up=Lazy((block, 2, units), F32),
+            output=Lazy((rows, width), BF16),
         ),
         dict(
             partial=pltpu.VMEM((rows, width), BF16),
@@ -801,6 +851,225 @@
         3 + 2,
         61,
         2 * rows * width * units * 10,
+    )
+
+
+TILE = 256
+
+
+def unit_tiles(units):
+    return [(at, min(TILE, units - at)) for at in range(0, units, TILE)]
+
+
+def hidden_fetch(r, number, wide):
+    slot = lax.rem(number, 2)
+    rows = pl.ds(number * TILE, wide)
+    pairs = [
+        (r.gate_up_t.at[:, rows, :], r.gate_up_tile.at[slot, :, 0:wide, :]),
+        (r.down.at[rows, :], r.down_tile.at[slot, 0:wide, :]),
+    ]
+    return [pltpu.make_async_copy(a, b, r.h_sem.at[slot, k]) for k, (a, b) in enumerate(pairs)]
+
+
+def hidden_tiles(r, units, tile):
+    count = pl.cdiv(units, TILE)
+    rest = units - (count - 1) * TILE
+
+    def run(number, wide):
+        for copy in hidden_fetch(r, number, wide):
+            copy.wait()
+        slot = lax.rem(number, 2)
+        tile(
+            number, wide,
+            r.gate_up_tile[slot, 0, 0:wide, :],
+            r.gate_up_tile[slot, 1, 0:wide, :],
+            r.down_tile[slot, 0:wide, :],
+        )
+
+    @pl.loop(0, count - 1)
+    def _(number):
+        @pl.when(number + 1 < count - 1)
+        def _():
+            for copy in hidden_fetch(r, number + 1, TILE):
+                copy.start()
+
+        @pl.when(number + 1 == count - 1)
+        def _():
+            for copy in hidden_fetch(r, number + 1, rest):
+                copy.start()
+
+        run(number, TILE)
+
+    run(count - 1, rest)
+
+
+def tile_lanes(number, wide):
+    start = number * TILE
+    return pl.ds(start if isinstance(start, int) else pl.multiple_of(start, TILE), wide)
+
+
+def hidden_scratch(width):
+    return dict(
+        gate_up_tile=pltpu.VMEM((2, 2, TILE, width), BF16),
+        down_tile=pltpu.VMEM((2, TILE, width), BF16),
+        h_sem=pltpu.SemaphoreType.DMA((2, 2)),
+    )
+
+
+def first_forward(
+    tokens, cotangent, norm_conv, conv_in_t, kernel, conv_out, norm_mlp, gate_up_t, down, norm_attn, where
+):
+    rows, width = tokens.shape
+    channels = conv_out.shape[0]
+    units = down.shape[0]
+    quarter = rows // 4
+    count = len(unit_tiles(units))
+
+    def body(r):
+        me = lax.axis_index("dp")
+        index = lax.axis_index("tensor")
+        place = lax.rem(me, SPAN)
+        greet(tensor_peers() + span_peers())
+        for copy in hidden_fetch(r, 0, TILE):
+            copy.start()
+        r.need(r.tokens)
+        for at in range(4):
+            part = slice(at * quarter, (at + 1) * quarter)
+            values = r.tokens[part, :].astype(F32)
+            r.normed[part, :] = normalize(values, r.norm_conv[...])[0].astype(BF16)
+        r.need(r.conv_in_t)
+        for at in range(3):
+            made = jnp.dot(r.normed[...], r.conv_in_t[at], preferred_element_type=F32)
+            r.projected[:, at * channels : (at + 1) * channels] = made
+        r.flush(r.projected)
+        pad = 8
+        r.mixed[0:pad, :] = jnp.zeros((pad, channels), F32)
+        r.mixed[pad:, :] = r.projected[:, :channels] * r.projected[:, 2 * channels :]
+        r.rim_out[...] = r.mixed[rows : rows + pad, :]
+        rim_copy = remote(r.rim_out, r.rim_in, r.m_sem.at[0], r.m_sem.at[1], dict(dp=me + 1))
+
+        @pl.when(place < SPAN - 1)
+        def _():
+            rim_copy.start()
+
+        start = pl.multiple_of(index * quarter, quarter)
+        r.inputs_own[...] = r.tokens[pl.ds(start, quarter), :].astype(F32)
+        r.flush(r.inputs_own)
+
+        @pl.when(place > 0)
+        def _():
+            rim_copy.wait_recv()
+            r.mixed[0:pad, :] = r.rim_in[...]
+
+        r.rim[...] = r.mixed[0:pad, :]
+        r.flush(r.rim)
+        taps = r.kernel[...].astype(F32)
+        convolved = None
+        for k in range(KW):
+            term = taps[k : k + 1, :] * r.mixed[pad - KW + 1 + k : pad - KW + 1 + k + rows, :]
+            convolved = term if convolved is None else convolved + term
+        r.gated_true[...] = (r.projected[:, channels : 2 * channels] * convolved).astype(BF16)
+        for at, owner in enumerate(block_owners(index)):
+            start = pl.multiple_of(owner * quarter, quarter)
+            r.gated[at * quarter : (at + 1) * quarter, :] = r.gated_true[pl.ds(start, quarter), :]
+        r.need(r.conv_out)
+        r.partial[...] = jnp.dot(r.gated[...], r.conv_out[...], preferred_element_type=F32).astype(BF16)
+        r.flush(r.gated)
+        waits = sum_and_gather(
+            r, r.partial, r.gathered_one, r.norm_one_t,
+            lambda total, at, first: norm_rows(total, at, r.inputs_own, r.norm_mlp, r.one),
+        )
+        next(waits)
+        r.need(r.cotangent)
+        for at, owner in enumerate(block_owners(index)):
+            part = slice(at * quarter, (at + 1) * quarter)
+            start = pl.multiple_of(owner * quarter, quarter)
+            live = r.column_positions[part, :] < r.length[0]
+            values = jnp.where(live, r.cotangent[pl.ds(start, quarter), :].astype(F32), 0.0)
+            if at == 0:
+                r.incoming[...] = values
+            r.grad_b[part, :] = values.astype(BF16)
+        next(waits)
+        r.normed_t[...] = r.normed[...].T
+        r.grad_b_t[...] = r.grad_b[...].T
+        r.flush(r.normed_t, r.grad_b, r.grad_b_t, r.incoming)
+        exhaust(waits)
+        r.flush(r.one, r.norm_one_t)
+        r.total[...] = jnp.zeros_like(r.total)
+
+        def tile(number, wide, gate_w, up_w, down_w):
+            a = cross(r.gathered_one[...], gate_w)
+            z = cross(r.gathered_one[...], up_w)
+            r.gate[number, :, 0:wide] = a
+            r.upward[number, :, 0:wide] = z
+            s = (a * jax.nn.sigmoid(a) * z).astype(BF16)
+            r.active[:, tile_lanes(number, wide)] = s
+            r.total[...] += jnp.dot(s, down_w, preferred_element_type=F32)
+
+        hidden_tiles(r, units, tile)
+        r.partial[...] = r.total[...].astype(BF16)
+        r.flush(r.active, r.gate, r.upward)
+        exhaust(
+            sum_and_gather(
+                r, r.partial, r.gathered, r.normed_attn_t,
+                lambda total, at, first: norm_rows(total, at, r.one, r.norm_attn, r.two),
+            )
+        )
+        r.flush(r.gathered, r.normed_attn_t, r.two)
+
+        @pl.when(place < SPAN - 1)
+        def _():
+            rim_copy.wait_send()
+
+    return run_kernel(
+        body,
+        dict(
+            tokens=Lazy(tokens),
+            cotangent=Lazy(cotangent),
+            norm_conv=norm_conv.reshape(1, -1),
+            conv_in_t=Lazy(conv_in_t),
+            kernel=kernel,
+            conv_out=Lazy(conv_out),
+            norm_mlp=norm_mlp.reshape(1, -1),
+            gate_up_t=(gate_up_t, pl.ANY),
+            down=(down, pl.ANY),
+            norm_attn=norm_attn.reshape(1, -1),
+            **where,
+        ),
+        dict(
+            gathered=Lazy((rows, width), BF16),
+            normed_attn_t=Lazy((width, rows), BF16),
+            two=Lazy((quarter, width), F32),
+            one=Lazy((quarter, width), F32),
+            inputs_own=Lazy((quarter, width), F32),
+            norm_one_t=Lazy((width, rows), BF16),
+            normed_t=Lazy((width, rows), BF16),
+            active=Lazy((rows, units), BF16),
+            gate=Lazy((count, rows, TILE), F32),
+            upward=Lazy((count, rows, TILE), F32),
+            gated=Lazy((rows, channels), BF16),
+            projected=Lazy((rows, 3 * channels), F32),
+            rim=Lazy((8, channels), F32),
+            grad_b=Lazy((rows, width), BF16),
+            grad_b_t=Lazy((width, rows), BF16),
+            incoming=Lazy((quarter, width), F32),
+        ),
+        dict(
+            normed=pltpu.VMEM((rows, width), BF16),
+            partial=pltpu.VMEM((rows, width), BF16),
+            gathered_one=pltpu.VMEM((rows, width), BF16),
+            total=pltpu.VMEM((rows, width), F32),
+            gated_true=pltpu.VMEM((rows, channels), BF16),
+            mixed=pltpu.VMEM((rows + 8, channels), F32),
+            rim_out=pltpu.VMEM((8, channels), F32),
+            rim_in=pltpu.VMEM((8, channels), F32),
+            m_sem=pltpu.SemaphoreType.DMA((2,)),
+            **hidden_scratch(width),
+            **exchange_scratch(rows, width),
+        ),
+        1,
+        60,
+        6 * rows * width * units,
     )
 
 
@@ -852,17 +1121,29 @@
         index = lax.axis_index("tensor")
         place = lax.rem(me, SPAN)
 
+        done = []
+
         def store(seg, column, value):
             if seg == 0:
                 at = (0, channels, channels + columns).index(column)
-                (r.sum_attn_out, r.sum_query, r.sum_kv)[at][...] = value
+                ref = (r.sum_attn_out, r.sum_query, r.sum_kv)[at]
+                ref[...] = value
+                r.flush(ref)
+            elif seg == 1:
+                r.sum_down[...] = value
+                r.flush(r.sum_down)
             elif seg < 4:
-                (r.sum_down, r.sum_gate, r.sum_up)[seg - 1][...] = value
+                r.sum_gate_up[:, seg - 2, :] = value
+                done.append(seg)
+                if len(done) == 2:
+                    r.flush(r.sum_gate_up)
             elif column == 0:
                 r.sum_conv_out[...] = value
+                r.flush(r.sum_conv_out)
             else:
                 for at in range(3):
                     r.sum_conv_in[at] = value[:, at * channels : (at + 1) * channels]
+                r.flush(r.sum_conv_in)
 
         rings = Rings(
             devices, sides,
@@ -928,6 +1209,7 @@
                 r.grad_up[:, at : at + wide] = (grad * gates * sigma).astype(BF16)
                 if number % 3 == 2:
                     yield 1
+            r.need(r.norm_one_t, r.one, r.grad_two)
             pump.ready += [2, 3]
             yield 2
             yield from stream_product(r, [r.grad_gate, r.grad_up], r.gate_up_t, r.partial)
@@ -940,6 +1222,7 @@
             r.small_out[...] = r.small[...]
             r.small_out[1:2, :] = r.gain_term[...]
 
+            r.need(r.conv_out, r.projected, r.rim, r.gated, r.normed_conv_t, r.inputs)
             made = cross(r.gathered[...], r.conv_out[...])
             for at, owner in enumerate(block_owners(index)):
                 start = pl.multiple_of(owner * quarter, quarter)
@@ -949,7 +1232,7 @@
             taps = r.kernel[...].astype(F32)
             pad = 8
             r.mixed[pad:, :] = before * signal
-            r.mixed[pad - KW + 1 : pad, :] = r.rim[...]
+            r.mixed[0:pad, :] = r.rim[...]
             grad_gated = r.grad_gated[...]
             r.grad_conv[0:rows, :] = grad_gated * r.projected[:, channels : 2 * channels]
             r.grad_conv[rows:, :] = jnp.zeros_like(r.grad_conv[rows:, :])
@@ -1016,6 +1299,7 @@
                     total, at, first, r.inputs, r.norm_conv, r.grad_one, None, r.gain_term
                 ),
             )
+            r.flush_blocks(r.input_grad, block_owners(index))
             r.small_out[0:1, :] = r.gain_term[...]
             row = lax.broadcasted_iota(jnp.int32, small.shape, 0)
             for stage in range(stages):
@@ -1030,8 +1314,12 @@
                     r.small_out[...] += jnp.where(row < 5, r.slots[stage], 0.0)
                 else:
                     r.small_out[...] += r.slots[stage]
-
-        pump.run(2)
+            r.flush(r.small_out)
+
+        r.need(r.grad_three_t, r.attended, r.normed_attn_t, r.grad_query, r.grad_kv)
+        pump.run(1)
+        r.need(r.grad_two_t, r.active)
+        pump.run(1)
         for number in main():
             pump.run(number)
         pump.rest()
@@ -1039,44 +1327,43 @@
     return run_kernel(
         body,
         dict(
-            grad_three_t=grad_three_t,
-            normed_attn_t=normed_attn_t,
-            grad_two_t=grad_two_t,
-            norm_one_t=norm_one_t,
-            normed_conv_t=normed_conv_t,
-            attended=attended,
-            grad_query=grad_query,
-            grad_kv=grad_kv,
-            active=active,
-            gated=gated,
+            grad_three_t=Lazy(grad_three_t),
+            attended=Lazy(attended),
+            normed_attn_t=Lazy(normed_attn_t),
+            grad_query=Lazy(grad_query),
+            grad_kv=Lazy(grad_kv),
+            grad_two_t=Lazy(grad_two_t),
+            active=Lazy(active),
+            norm_one_t=Lazy(norm_one_t),
+            one=Lazy(one),
+            grad_two=Lazy(grad_two),
+            conv_out=Lazy(conv_out),
+            projected=Lazy(projected),
+            rim=Lazy(rim),
+            gated=Lazy(gated),
+            normed_conv_t=Lazy(normed_conv_t),
+            inputs=Lazy(inputs),
             grad_two_b=(grad_two_b, pl.ANY),
             down=(down, pl.ANY),
             gate_up_t=(gate_up_t, pl.ANY),
             gate=(gate, pl.ANY),
             upward=(upward, pl.ANY),
-            one=one,
             norm_mlp=norm_mlp.reshape(1, -1),
-            grad_two=grad_two,
-            conv_out=conv_out,
             conv_in_t=(conv_in_t, pl.ANY),
-            projected=projected,
-            rim=rim,
             kernel=kernel,
-            inputs=inputs,
             norm_conv=norm_conv.reshape(1, -1),
             small=small,
         ),
         dict(
-            input_grad=((rows, width), BF16),
-            small_out=(small.shape, F32),
-            sum_attn_out=((block, channels), F32),
-            sum_query=((block, columns), F32),
-            sum_kv=((block, kv_columns), F32),
-            sum_down=((block, units), F32),
-            sum_gate=((block, units), F32),
-            sum_up=((block, units), F32),
-            sum_conv_out=((block, channels), F32),
-            sum_conv_in=((3, block, channels), F32),
+            input_grad=Lazy((rows, width), BF16),
+            small_out=Lazy(small.shape, F32),
+            sum_attn_out=Lazy((block, channels), F32),
+            sum_query=Lazy((block, columns), F32),
+            sum_kv=Lazy((block, kv_columns), F32),
+            sum_down=Lazy((block, units), F32),
+            sum_gate_up=Lazy((block, 2, units), F32),
+            sum_conv_out=Lazy((block, channels), F32),
+            sum_conv_in=Lazy((3, block, channels), F32),
         ),
         dict(
             gathered=pltpu.VMEM((rows, width), BF16),
@@ -1113,92 +1400,6 @@
     )
 
 
-TILE = 256
-
-
-def hidden_forward(normed_b, gate_up_t, down):
-    rows, width = normed_b.shape
-    units = down.shape[0]
-    tiles = pl.cdiv(units, TILE)
-    rest = units - (tiles - 1) * TILE
-
-    def body(normed, weight, down_ref, partial, active, gate, upward, total):
-        at = pl.program_id(0)
-        a = cross(normed[...], weight[0])
-        z = cross(normed[...], weight[1])
-        gate[0] = a
-        upward[0] = z
-        s = (a * jax.nn.sigmoid(a) * z).astype(BF16)
-        active[...] = s
-
-        @pl.when(at == 0)
-        def _():
-            total[...] = jnp.dot(s, down_ref[...], preferred_element_type=F32)
-
-        @pl.when((at > 0) & (at < tiles - 1))
-        def _():
-            total[...] += jnp.dot(s, down_ref[...], preferred_element_type=F32)
-
-        @pl.when(at == tiles - 1)
-        def _():
-            last = jnp.dot(s[:, :rest], down_ref[0:rest, :], preferred_element_type=F32)
-            partial[...] = (total[...] + last).astype(BF16)
-
-    return pl.pallas_call(
-        body,
-        grid=(tiles,),
-        in_specs=[
-            pl.BlockSpec((rows, width), lambda i: (0, 0)),
-            pl.BlockSpec((2, TILE, width), lambda i: (0, i, 0)),
-            pl.BlockSpec((TILE, width), lambda i: (i, 0)),
-        ],
-        out_specs=[
-            pl.BlockSpec((rows, width), lambda i: (0, 0)),
-            pl.BlockSpec((rows, TILE), lambda i: (0, i)),
-            pl.BlockSpec((1, rows, TILE), lambda i: (i, 0, 0)),
-            pl.BlockSpec((1, rows, TILE), lambda i: (i, 0, 0)),
-        ],
-        out_shape=[
-            jax.ShapeDtypeStruct((rows, width), BF16),
-            jax.ShapeDtypeStruct((rows, units), BF16),
-            jax.ShapeDtypeStruct((tiles, rows, TILE), F32),
-            jax.ShapeDtypeStruct((tiles, rows, TILE), F32),
-        ],
-        scratch_shapes=[pltpu.VMEM((rows, width), F32)],
-        compiler_params=pltpu.CompilerParams(vmem_limit_bytes=40 * 2**20),
-    )(normed_b, gate_up_t, down)
-
-
-def hidden_both(normed_b, gate_up_t, down, grad_b):
-    rows, width = normed_b.shape
-    units = down.shape[0]
-
-    def body(normed, weight, down_ref, grad_ref, active, grad_gate, grad_up):
-        a = cross(normed[...], weight[0])
-        z = cross(normed[...], weight[1])
-        grad = cross(grad_ref[...], down_ref[...])
-        sigma = jax.nn.sigmoid(a)
-        active[...] = (a * sigma * z).astype(BF16)
-        grad_gate[...] = (grad * z * sigma * (1.0 + a * (1.0 - sigma))).astype(BF16)
-        grad_up[...] = (grad * a * sigma).astype(BF16)
-
-    whole = pl.BlockSpec((rows, width), lambda i: (0, 0))
-    tile = pl.BlockSpec((rows, TILE), lambda i: (0, i))
-    return pl.pallas_call(
-        body,
-        grid=(pl.cdiv(units, TILE),),
-        in_specs=[
-            whole,
-            pl.BlockSpec((2, TILE, width), lambda i: (0, i, 0)),
-            pl.BlockSpec((TILE, width), lambda i: (i, 0)),
-            whole,
-        ],
-        out_specs=[tile] * 3,
-        out_shape=[jax.ShapeDtypeStruct((rows, units), BF16)] * 3,
-        compiler_params=pltpu.CompilerParams(vmem_limit_bytes=40 * 2**20),
-    )(normed_b, gate_up_t, down, grad_b)
-
-
 def local(
     tokens,
     lengths,
@@ -1223,8 +1424,6 @@
     row_count = tokens.shape[0]
     width = tokens.shape[1]
     quarter = row_count // 4
-    channels = conv_out.shape[0]
-    local_heads = query_weight.shape[1] // HEAD
     local_kv = kv_weight.shape[2] // HEAD
     device = lax.axis_index("dp")
     devices = lax.axis_size("dp")
@@ -1236,46 +1435,49 @@
         [o * quarter + jnp.arange(quarter, dtype=jnp.int32) for o in block_owners(index)]
     )
     positions = place_index * row_count + offsets
-    is_valid = positions < length
     frequency = THETA ** (-2.0 * jnp.arange(HEAD // 2, dtype=jnp.float32) / HEAD)
     angles = frequency[:, None] * positions.astype(jnp.float32)[None, :]
     tables = (jnp.cos(angles), jnp.sin(angles))
     where = position_inputs(positions, length)
-    kernel = conv_kernel.astype(jnp.float32)
-    rim_rows = KW - 1
     gate_up_one_t = jnp.transpose(gate_up_one, (1, 2, 0))
     gate_up_two_t = jnp.transpose(gate_up_two, (1, 2, 0))
-    forward_route = [(i, i + 1) for i in range(devices - 1) if (i + 1) % SPAN]
-    backward_route = [(b, a) for a, b in forward_route]
-
-    inputs = tokens.astype(F32)
-    normed_conv, inverse_conv = normalize(inputs, norm_conv)
-    normed_conv_b = normed_conv.astype(BF16)
-    weight_in = conv_in.reshape(width, 3 * channels)
-    projected = matmul(normed_conv_b, weight_in)
-    before = projected[:, :channels]
-    after = projected[:, channels : 2 * channels]
-    signal = projected[:, 2 * channels :]
-    mixed = before * signal
-    rim_in = lax.ppermute(mixed[row_count - rim_rows :], "dp", forward_route)
-    padded = jnp.concatenate([rim_in, mixed], axis=0)
-    convolved = kernel[0] * padded[0:row_count]
-    for offset in range(1, KW):
-        convolved = convolved + kernel[offset] * padded[offset : offset + row_count]
-    gated_b = to_local((after * convolved).astype(BF16), index)
-    inputs_own = lax.dynamic_slice_in_dim(tokens, index * quarter, quarter).astype(F32)
-
-    norm_one_b, norm_one_t, one_own = norm_spread(
-        matmul(gated_b, conv_out).astype(BF16), inputs_own, norm_mlp_one
-    )
-    partial_b, active_one, gate_a, up_a = hidden_forward(norm_one_b, gate_up_one_t, down_one)
-
-    normed_attn_b, normed_attn_t, two_own = norm_spread(
-        partial_b, one_own, norm_attn
-    )
+    conv_in_t = jnp.transpose(conv_in, (1, 0, 2))
     kv_flat = kv_weight.reshape(width, 2 * local_kv * HEAD)
+
     (
-        norm_two_b,
+        normed_attn_b,
+        normed_attn_t,
+        two_own,
+        one_own,
+        inputs_own,
+        norm_one_t,
+        normed_conv_t,
+        active_one,
+        gate_one,
+        up_one,
+        gated_b,
+        projected,
+        rim,
+        grad_b,
+        grad_b_t,
+        incoming,
+    ) = first_forward(
+        tokens,
+        cotangent,
+        norm_conv,
+        conv_in_t,
+        conv_kernel,
+        conv_out,
+        norm_mlp_one,
+        gate_up_one_t,
+        down_one,
+        norm_attn,
+        where,
+    )
+    (
+        active_two,
+        grad_gate_two,
+        grad_up_two,
         norm_two_t,
         three_own,
         *kept,
@@ -1293,14 +1495,11 @@
         norm_mlp_two,
         tables,
         where,
+        gate_up_two_t,
+        down_two,
+        grad_b,
     )
     kept = (*kept, attended_t, log_total)
-
-    grad_result = to_local(cotangent, index).astype(F32) * is_valid[:, None].astype(F32)
-    grad_result_b = grad_result.astype(BF16)
-    active_two, grad_gate_two, grad_up_two = hidden_both(
-        norm_two_b, gate_up_two_t, down_two, grad_result_b
-    )
     (
         grad_three_t,
         grad_query,
@@ -1313,11 +1512,10 @@
         part_query_gain,
         part_key_gain,
         sum_down_two,
-        sum_gate_two,
-        sum_up_two,
+        sum_gate_up_two,
         output,
     ) = attention_backward(
-        grad_result_b.T,
+        grad_b_t,
         norm_two_t,
         active_two,
         grad_gate_two,
@@ -1326,7 +1524,7 @@
         down_two,
         three_own,
         norm_mlp_two,
-        grad_result[:quarter],
+        incoming,
         kept,
         attn_out,
         query_weight,
@@ -1359,33 +1557,31 @@
         sum_query,
         sum_kv,
         sum_down_one,
-        sum_gate_one,
-        sum_up_one,
+        sum_gate_up_one,
         sum_conv_out,
         sum_conv_in,
     ) = first_backward(
-        [grad_three_t, normed_attn_t, grad_two_t, norm_one_t, normed_conv_b.T],
+        [grad_three_t, normed_attn_t, grad_two_t, norm_one_t, normed_conv_t],
         [attended_b, grad_query, grad_kv, active_one, gated_b],
         grad_two_b,
         down_one,
         gate_up_one_t,
-        gate_a,
-        up_a,
+        gate_one,
+        up_one,
         one_own,
         norm_mlp_one,
         grad_two,
         conv_out,
-        jnp.transpose(conv_in, (1, 0, 2)),
+        conv_in_t,
         projected,
-        rim_in,
+        rim,
         conv_kernel,
         inputs_own,
         norm_conv,
         small,
         devices,
     )
-    grad_inputs = to_true(grad_inputs, index).astype(F32)
-    output = to_true(output, index)
+    grad_inputs = grad_inputs.astype(F32)
 
     out_rows = width // devices
     return (
@@ -1393,10 +1589,10 @@
         grad_inputs,
         small[0],
         jnp.transpose(sum_conv_in, (1, 0, 2)),
-        small[5:, :channels],
+        small[5:, : conv_out.shape[0]],
         sum_conv_out.T,
         small[1],
-        jnp.stack([sum_gate_one, sum_up_one], axis=1),
+        sum_gate_up_one,
         sum_down_one.T,
         small[2],
         sum_query,
@@ -1405,7 +1601,7 @@
         small[4, HEAD : 2 * HEAD],
         sum_attn_out.T,
         small[3],
-        jnp.stack([sum_gate_two, sum_up_two], axis=1),
+        sum_gate_up_two,
         sum_down_two.T,
     )
 

time: 643 us -> 586 us (0.911)
  local copies, waits for them, and re-layouts: 55 us -> 23.9 us
  other arithmetic: 16.7 us -> 7.75 us
    unnamed x121 -> x40, local copies, waits for them, and re-layouts: 38 us -> 12.6 us
    pallas_call x7 -> x4, Pallas kernels: 554 us -> 550 us  [run_kernel(): pl.pallas_call(whole, in_specs=specs, out_specs=out_specs, out_shape=shap...]
  transfers between devices with their start and end apart: 1 -> 0, of which waited for: 0 -> 0; matrix products, arithmetic and copies ran while one was open for 3% -> 0% of each run, Pallas kernels for 0% -> 0%
where the time goes in v4:
time: 586 us; the launch traced here: 583 us
  Pallas kernels  550 us (94%)
  local copies, waits for them, and re-layouts  23.9 us (4%)
  other arithmetic  7.75 us (1%)
    pallas_call x4, Pallas kernels, run_kernel(): pl.pallas_call(whole, in_specs=specs, out_specs=out_specs, out_shape=shap...  550 us
    unnamed x40, local copies, waits for them, and re-layouts  12.6 us

profile of v4, /device:TPU:0, one launch (start us, length us, event | category | flops | bytes accessed | tf_op | source)
XLA Modules:
  0.0 582.6 jit_solution(5530611764738109545)
XLA Ops:
  0.7 1.2 dynamic_slice.3.refs_10_.refs_13_.refs_26_
  2.1 0.7 broadcast_add_fusion.refs_12_.refs_15_.refs_28_
  3.4 1.3 reshape.182.refs_2_.refs_24_
  4.7 1.3 reshape.183.refs_6_.refs_21_
  6.0 1.3 reshape.184.refs_9_.refs_23_
  7.3 66.7 %shard_map.322 = (bf16[512,1536]{1,0:T(8,128)(2,1)}, bf16[1536,512]{1,0:T(8,128)(2,1)}, f32[128,1536]{1,0:T(8,128)}, f32[128,1536]{1,0:T(8,128)}, f32[128,1536]{...) custom-call(bf16[512,1536]{1,0:T(8,128)(2,1)} %refs_0_.1, ...), custom_call_target="tpu_custom_call" | custom-call | flops 8153726976 | bytes 23814404 | tf_op jit(solution)/shard_map/pallas_call | solution.py:130
  74.1 1.0 multiply_sine_fusion
  75.1 1.0 copy.60
  78.1 48.5 %shard_map.323 = (bf16[512,1728]{1,0:T(8,128)(2,1)}, bf16[512,1728]{1,0:T(8,128)(2,1)}, bf16[512,1728]{1,0:T(8,128)(2,1)}, bf16[1536,512]{1,0:T(8,128)(2,1)}, f3...) custom-call(bf16[512,1536]{1,0:T(8,128)(2,1)} %get-tuple-element.70., ...), custom_call_target="tpu_custom_call" | custom-call | flops 6442450944 | bytes 23144964 | tf_op jit(solution)/shard_map/pallas_call | solution.py:130
  126.5 194.1 %shard_map.324 = (bf16[1536,512]{1,0:T(8,128)(2,1)}, bf16[512,384]{1,0:T(8,128)(2,1)}, bf16[512,256]{1,0:T(8,128)(2,1)}, bf16[512,1536]{1,0:T(8,128)(2,1)}, bf16...) custom-call(bf16[1536,512]{1,0:T(8,128)(2,1)} %get-tuple-element.69., ...), custom_call_target="tpu_custom_call" | custom-call | flops 27179089920 | bytes 33321476 | tf_op jit(solution)/shard_map/pallas_call | solution.py:130
  320.7 0.9 reduce
  321.5 0.9 reduce.1
  322.5 1.4 concatenate.58.refs_25_
  323.9 240.5 %shard_map.325 = (bf16[512,1536]{1,0:T(8,128)(2,1)}, f32[8,1536]{1,0:T(8,128)}, f32[192,384]{1,0:T(8,128)}, f32[192,384]{1,0:T(8,128)}, f32[192,256]{1,0:T(8,128...) custom-call(bf16[1536,512]{1,0:T(8,128)(2,1)} %get-tuple-element.87.refs_0_, ...), custom_call_target="tpu_custom_call" | custom-call | flops 36540776448 | bytes 45426944 | tf_op jit(solution)/shard_map/pallas_call | solution.py:130
  564.4 3.6 convert_element_type.13
  568.0 0.8 reshape.191
  570.7 1.1 copy.70
  571.8 0.9 copy.71
  574.1 1.5 copy.73
  575.6 0.8 copy-done.4
  576.4 1.1 copy.74
  578.9 1.5 copy.77
  580.4 0.8 copy-done.3
  581.2 1.1 copy.78
  (52 shorter events, 7.5 us)
Async XLA Ops:
  7.3 67.8 %copy-start.6 = (bf16[1536,2,128]{2,1,0:T(2,128)(2,1)S(1)}, bf16[1536,2,128]{2,1,0:T(2,128)(2,1)}, u32[]{:S(2)}) copy-start(bf16[1536,2,128]{2,1,0:T(2,128)(2,1)} %param.30) | copy-start | bytes 2359300
  74.0 2.0 copy-start.13
  74.0 2.7 copy-start.14
  74.0 3.4 copy-start.12
  564.4 3.6 copy-start.10
  564.4 4.4 copy-start.11
  564.4 6.2 %copy-start.2 = (bf16[512,1536]{1,0:T(8,128)(2,1)S(1)}, bf16[512,1536]{1,0:T(8,128)(2,1)}, u32[]{:S(2)}) copy-start(bf16[512,1536]{1,0:T(8,128)(2,1)} %get-tuple-element.158) | copy-start | bytes 4718596
  568.8 3.0 copy-start.5
  570.7 3.4 copy-start.1
  571.8 1.5 copy-start.9
  574.1 2.3 copy-start.4
  574.1 3.4 copy-start.8
  576.4 1.8 copy-start.7
  576.4 2.5 copy-start
  578.9 2.3 copy-start.3

commit v5 on v4

--- a/solution.py
+++ b/solution.py
@@ -113,7 +113,7 @@
             scratch[name] = pltpu.VMEM(shape, dtype)
             names.append(None)
         else:
-            (shape, dtype), space = value, pltpu.VMEM
+            shape, dtype, space = value if len(value) == 3 else (*value, pltpu.VMEM)
             names.append(name)
         shapes.append(jax.ShapeDtypeStruct(shape, dtype))
         out_specs.append(pl.BlockSpec(memory_space=space))
@@ -246,13 +246,13 @@
 def norm_rows(total, rows, residual, gain, hidden):
     values = residual[rows, :] + total
     hidden[rows, :] = values
-    return normalize(values, gain[...])[0].astype(BF16)
+    return normalize(values, gain)[0].astype(BF16)
 
 
 def back_rows(total, rows, first, hidden, gain, incoming, own, grad_gain):
     values = hidden[rows, :]
     inverse = lax.rsqrt(jnp.mean(values * values, axis=-1, keepdims=True) + EPSILON)
-    made, term = normalize_back(values, inverse, gain[...], total)
+    made, term = normalize_back(values, inverse, gain, total)
     made = made + incoming[rows, :]
     if own is not None:
         own[rows, :] = made
@@ -402,27 +402,35 @@
     return inverse * (weighted - values * inverse * inverse * inner), grad * values * inverse
 
 
+def block_positions(block, quarter, shape, axis):
+    place = lax.rem(lax.axis_index("dp"), SPAN)
+    owner = block_owners(lax.axis_index("tensor"))[block]
+    start = (place * 4 + owner) * quarter
+    return start + lax.broadcasted_iota(jnp.int32, shape, axis)
+
+
+def own_length(r):
+    return r.lengths[lax.axis_index("dp") // SPAN]
+
+
 def fill_bias(r):
-    keys = r.column_positions[...]
-    allowed = (keys <= r.row_positions[...]) & (keys < r.length[0])
-    r.bias[...] = jnp.where(allowed, 0.0, -1e30)
+    quarter = r.bias.shape[0] // 4
+    shape = (quarter, quarter)
+    for row in range(4):
+        keys = block_positions(row, quarter, shape, 0)
+        live = keys < own_length(r)
+        for column in range(4):
+            allowed = live & (keys <= block_positions(column, quarter, shape, 1))
+            at = slice(row * quarter, (row + 1) * quarter)
+            r.bias[at, column * quarter : (column + 1) * quarter] = jnp.where(allowed, 0.0, -1e30)
 
 
 def head_rows(head):
     return slice(head * HEAD, (head + 1) * HEAD)
 
 
-def position_inputs(positions, length):
-    rows = positions.shape[0]
-    return dict(
-        length=(length.reshape(1), pltpu.SMEM),
-        row_positions=positions.reshape(1, rows),
-        column_positions=positions.reshape(rows, 1),
-    )
-
-
 def attention_forward(
-    normed_b, query_weight, kv_weight, query_gain, key_gain, attn_out, residual, gain, tables, where,
+    normed_b, query_weight, kv_weight, head_gains, attn_out, residual, tables, gains, lengths,
     gate_up_t, down, grad_b,
 ):
     rows, width = normed_b.shape
@@ -450,7 +458,7 @@
         r.key_raw[...] = made[:, :kv_columns].T
         r.own[:, kv_columns:] = made[:, kv_columns:].astype(BF16)
         for group in range(kv_heads):
-            keys = head_norm_t(r.key_raw[head_rows(group), :], r.key_gain[...])
+            keys = head_norm_t(r.key_raw[head_rows(group), :], r.head_gains[:, 1:2])
             r.keys_t[head_rows(group), :] = turn_t(keys, cosine, sine, False).astype(BF16)
         r.own[:, :kv_columns] = r.keys_t[...].T
         for distance in range(1, SPAN):
@@ -463,7 +471,7 @@
         made = jnp.dot(r.normed[...], r.query_weight[...], preferred_element_type=F32)
         r.query_raw[...] = made.T
         for head in range(heads):
-            query = head_norm_t(r.query_raw[head_rows(head), :], r.query_gain[...])
+            query = head_norm_t(r.query_raw[head_rows(head), :], r.head_gains[:, 0:1])
             query = turn_t(query, cosine, sine, False).astype(BF16)
             r.query[head_rows(head), :] = query * jnp.asarray(HEAD ** (-0.5), BF16)
         fill_bias(r)
@@ -508,7 +516,7 @@
         exhaust(
             sum_and_gather(
                 r, r.partial, r.gathered, r.gathered_t,
-                lambda total, at, first: norm_rows(total, at, r.residual, r.gain, r.hidden),
+                lambda total, at, first: norm_rows(total, at, r.residual, r.gains[3:4, :], r.hidden),
             )
         )
         r.flush(r.gathered_t, r.hidden)
@@ -525,11 +533,12 @@
             grad = cross(r.grad_b[...], down_w)
             sigma = jax.nn.sigmoid(a)
             r.active[:, lanes] = (a * sigma * z).astype(BF16)
-            r.grad_gate[:, lanes] = (grad * z * sigma * (1.0 + a * (1.0 - sigma))).astype(BF16)
-            r.grad_up[:, lanes] = (grad * a * sigma).astype(BF16)
+            grad_gate = (grad * z * sigma * (1.0 + a * (1.0 - sigma))).astype(BF16)
+            grad_up = (grad * a * sigma).astype(BF16)
+            put_joined(r.joined, number, TILE, (grad_gate, grad_up), units)
 
         hidden_tiles(r, units, tile)
-        r.flush(r.active, r.grad_gate, r.grad_up)
+        r.flush(r.active, r.joined)
 
     return run_kernel(
         body,
@@ -537,22 +546,20 @@
             normed=Lazy(normed_b),
             query_weight=Lazy(query_weight),
             kv_weight=Lazy(kv_weight),
-            query_gain=query_gain.reshape(HEAD, 1),
-            key_gain=key_gain.reshape(HEAD, 1),
+            head_gains=head_gains,
             attn_out=Lazy(attn_out),
             residual=Lazy(residual),
-            gain=gain.reshape(1, -1),
             cosine=Lazy(tables[0]),
             sine=Lazy(tables[1]),
             gate_up_t=(gate_up_t, pl.ANY),
             down=(down, pl.ANY),
             grad_b=Lazy(grad_b),
-            **where,
+            lengths=(lengths, pltpu.SMEM),
+            gains=gains,
         ),
         dict(
             active=Lazy((rows, units), BF16),
-            grad_gate=Lazy((rows, units), BF16),
-            grad_up=Lazy((rows, units), BF16),
+            joined=Lazy((rows, 2 * units), BF16),
             gathered_t=Lazy((width, rows), BF16),
             hidden=Lazy(residual.shape, F32),
             query_raw=Lazy((columns, rows), F32),
@@ -581,17 +588,20 @@
     )
 
 
-def stream_product(r, lefts, weights, out):
+def stream_product(r, left, weights, parts, out):
     width = weights.shape[2]
-    size = r.tile.shape[3]
+    size = r.tile.shape[2]
     tiles = width // size
+    depth = sum(part[3] for part in parts)
 
     def fetch(j):
         return [
             pltpu.make_async_copy(
-                weights.at[k, :, pl.ds(j * size, size)], r.tile.at[j % 2, k], r.tile_sem.at[j % 2, k]
+                weights.at[which, pl.ds(there, count), pl.ds(j * size, size)],
+                r.tile.at[j % 2, pl.ds(here, count), :],
+                r.tile_sem.at[j % 2, k],
             )
-            for k in range(len(lefts))
+            for k, (which, there, here, count) in enumerate(parts)
         ]
 
     for copy in fetch(0):
@@ -602,25 +612,22 @@
                 copy.start()
         for copy in fetch(j):
             copy.wait()
-        made = None
-        for k, left in enumerate(lefts):
-            term = jnp.dot(left[...], r.tile[j % 2, k], preferred_element_type=F32)
-            made = term if made is None else made + term
+        made = jnp.dot(left[...], r.tile[j % 2, 0:depth, :], preferred_element_type=F32)
         out[:, j * size : (j + 1) * size] = made.astype(BF16)
         if j % 2:
             yield 1
 
 
-def stream_scratch(count, depth, size):
+def stream_scratch(depth, size):
     return dict(
-        tile=pltpu.VMEM((2, count, depth, size), BF16),
-        tile_sem=pltpu.SemaphoreType.DMA((2, count)),
+        tile=pltpu.VMEM((2, depth, size), BF16),
+        tile_sem=pltpu.SemaphoreType.DMA((2, 4)),
     )
 
 
 def attention_backward(
-    grad_b_t, norm_two_t, active, grad_gate, grad_up, gate_up_t, down, three, norm_mlp, incoming,
-    kept, attn_out, query_weight, kv_weight, query_gain, key_gain, two, norm_attn, tables, where, devices,
+    grad_b_t, norm_two_t, active, joined, gate_up_t, down, three, incoming,
+    kept, attn_out, query_weight, kv_weight, head_gains, two, tables, gains, lengths, devices,
 ):
     units, tokens_width = gate_up_t.shape[1:]
     query_raw, key_raw, query, own, near, attended_t, log_total = kept
@@ -630,7 +637,7 @@
     heads, kv_heads = columns // HEAD, kv_columns // HEAD
     sides = piece_sides(width, devices)
     block = width // devices
-    segment_widths = [units] * 3
+    segment_widths = [units] + joined_widths(units)
 
     def body(r):
         me = lax.axis_index("dp")
@@ -641,13 +648,13 @@
                 r.sum_down[...] = value
                 r.flush(r.sum_down)
             else:
-                r.sum_gate_up[:, seg - 1, :] = value
+                store_joined(r.sum_gate_up, seg - 1, value, units)
                 if seg == 2:
                     r.flush(r.sum_gate_up)
 
         rings = Rings(
             devices, sides,
-            [[(r.grad_b_t, r.active)], [(r.norm_two_t, r.grad_gate)], [(r.norm_two_t, r.grad_up)]],
+            [[(r.grad_b_t, r.active)]] + joined_segments(r.norm_two_t, r.joined, units),
             [r.held0, r.held1, r.held2], r.r_send, r.r_recv, r.r_credit, store,
         )
         greet(rings.peers() + tensor_peers() + span_peers())
@@ -688,16 +695,18 @@
                 write(value_at, grad_v)
 
         def main():
-            yield from stream_product(r, [r.grad_gate, r.grad_up], r.gate_up_t, r.partial)
+            yield from stream_product(r, r.joined, r.gate_up_t, joined_parts(units), r.partial)
             fill_bias(r)
             r.need(r.three, r.incoming)
             yield from sum_and_gather(
                 r, r.partial, r.gathered, r.grad_three_t,
                 lambda total, at, first: back_rows(
-                    total, at, first, r.three, r.norm_mlp, r.incoming, r.grad_three, r.grad_norm_mlp
+                    total, at, first, r.three, r.gains[3:4, :], r.incoming, r.grad_three, r.gain_term
                 ),
             )
             r.flush(r.grad_three_t)
+            r.small[...] = jnp.zeros_like(r.small)
+            r.small[3:4, :] = r.gain_term[...]
             r.need(r.attn_out, r.attended_t, r.own, r.near, r.query, r.log_total)
             r.grads[...] = cross(r.gathered[...], r.attn_out[...]).astype(BF16)
             for head in range(heads):
@@ -729,10 +738,10 @@
             for head in range(heads):
                 at = head_rows(head)
                 grad = turn_t(r.grad_q_t[at, :] * HEAD ** (-0.5), cosine, sine, True)
-                made, term = head_back_t(r.query_raw[at, :], r.query_gain[...], grad)
+                made, term = head_back_t(r.query_raw[at, :], r.head_gains[:, 0:1], grad)
                 terms = term if terms is None else terms + term
                 r.grad_query[:, at] = made.T.astype(BF16)
-            r.grad_query_gain[...] = jnp.sum(terms, axis=1, keepdims=True)
+            r.small[4:5, 0:HEAD] = jnp.sum(terms.T, axis=0, keepdims=True)
             yield 1
             for distance in range(1, SPAN):
 
@@ -745,10 +754,10 @@
             for group in range(kv_heads):
                 at = head_rows(group)
                 grad = turn_t(r.grad_own[:, at].T, cosine, sine, True)
-                made, term = head_back_t(r.key_raw[at, :], r.key_gain[...], grad)
+                made, term = head_back_t(r.key_raw[at, :], r.head_gains[:, 1:2], grad)
                 terms = term if terms is None else terms + term
                 r.grad_kv[:, at] = made.T.astype(BF16)
-            r.grad_key_gain[...] = jnp.sum(terms, axis=1, keepdims=True)
+            r.small[4:5, HEAD : 2 * HEAD] = jnp.sum(terms.T, axis=0, keepdims=True)
             r.grad_kv[:, kv_columns:] = r.grad_own[:, kv_columns:].astype(BF16)
             r.flush(r.grad_query, r.grad_kv)
             r.partial[...] = (
@@ -758,17 +767,18 @@
             yield from sum_and_gather(
                 r, r.partial, r.grad_two_b, r.grad_two_t,
                 lambda total, at, first: back_rows(
-                    total, at, first, r.two, r.norm_attn, r.grad_three, r.grad_two, r.grad_norm_attn
+                    total, at, first, r.two, r.gains[2:3, :], r.grad_three, r.grad_two, r.gain_term
                 ),
             )
-            r.flush(r.grad_two_b, r.grad_two_t, r.grad_two)
+            r.small[2:3, :] = r.gain_term[...]
+            r.flush(r.grad_two_b, r.grad_two_t, r.grad_two, r.small)
             for distance in range(1, SPAN):
 
                 @pl.when(place >= distance)
                 def _():
                     pass_back(distance).wait_send()
 
-            yield from stream_product(r, [r.active], r.down, r.partial)
+            yield from stream_product(r, r.active, r.down, [(0, 0, 0, units)], r.partial)
             yield from sum_and_gather(
                 r, r.partial, r.output, None,
                 lambda total, at, first: (r.three[at, :] + total).astype(BF16),
@@ -776,7 +786,7 @@
             r.flush_blocks(r.output, block_owners(lax.axis_index("tensor")))
 
         def first(seg):
-            r.need(*((r.grad_b_t, r.active), (r.norm_two_t, r.grad_gate), (r.grad_up,))[seg])
+            r.need(*((r.grad_b_t, r.active), (r.norm_two_t, r.joined), ())[seg])
             rings.unit(seg, 0)
 
         order = [(seg, step) for step in range(1, devices) for seg in range(3)]
@@ -791,12 +801,10 @@
             grad_b_t=Lazy(grad_b_t),
             active=Lazy(active),
             norm_two_t=Lazy(norm_two_t),
-            grad_gate=Lazy(grad_gate),
-            grad_up=Lazy(grad_up),
+            joined=Lazy(joined),
             gate_up_t=(gate_up_t, pl.ANY),
             down=(down.reshape((1,) + down.shape), pl.ANY),
             three=Lazy(three),
-            norm_mlp=norm_mlp.reshape(1, -1),
             incoming=Lazy(incoming),
             query_raw=Lazy(query_raw),
             key_raw=Lazy(key_raw),
@@ -808,13 +816,12 @@
             attn_out=Lazy(attn_out),
             query_weight=Lazy(query_weight),
             kv_weight=Lazy(kv_weight),
-            query_gain=query_gain.reshape(HEAD, 1),
-            key_gain=key_gain.reshape(HEAD, 1),
+            head_gains=head_gains,
             two=Lazy(two),
-            norm_attn=norm_attn.reshape(1, -1),
             cosine=Lazy(tables[0]),
             sine=Lazy(tables[1]),
-            **where,
+            lengths=(lengths, pltpu.SMEM),
+            gains=gains,
         ),
         dict(
             grad_three_t=Lazy((width, rows), BF16),
@@ -823,10 +830,7 @@
             grad_two_b=Lazy((rows, width), BF16),
             grad_two_t=Lazy((width, rows), BF16),
             grad_two=Lazy((quarter, width), F32),
-            grad_norm_mlp=((1, width), F32),
-            grad_norm_attn=((1, width), F32),
-            grad_query_gain=((HEAD, 1), F32),
-            grad_key_gain=((HEAD, 1), F32),
+            small=Lazy((8, width), F32),
             sum_down=Lazy((block, units), F32),
             sum_gate_up=Lazy((block, 2, units), F32),
             output=Lazy((rows, width), BF16),
@@ -836,6 +840,7 @@
             gathered=pltpu.VMEM((rows, width), BF16),
             grad_three=pltpu.VMEM((quarter, width), F32),
             grads=pltpu.VMEM((rows, columns), BF16),
+            gain_term=pltpu.VMEM((1, width), F32),
             delta=pltpu.VMEM((heads, rows), F32),
             bias=pltpu.VMEM((rows, rows), F32),
             grad_q_t=pltpu.VMEM((columns, rows), F32),
@@ -844,7 +849,7 @@
             arrived=pltpu.VMEM((SPAN - 1, rows, 2 * kv_columns), BF16),
             p_send=pltpu.SemaphoreType.DMA((SPAN - 1,)),
             p_recv=pltpu.SemaphoreType.DMA((SPAN - 1,)),
-            **stream_scratch(2, units, 256),
+            **stream_scratch(2 * units, 256),
             **exchange_scratch(rows, width),
             **ring_scratch(devices, sides, block, segment_widths),
         ),
@@ -854,7 +859,7 @@
     )
 
 
-TILE = 256
+TILE = 512
 
 
 def unit_tiles(units):
@@ -903,6 +908,57 @@
     run(count - 1, rest)
 
 
+def joined_parts(units):
+    main = units // 128 * 128
+    rest = units - main
+    return [
+        (0, 0, 0, main),
+        (1, 0, main, main),
+        (0, main, 2 * main, rest),
+        (1, main, 2 * main + rest, rest),
+    ]
+
+
+def put_joined(ref, number, size, values, units):
+    main = units // 128 * 128
+    rest = units - main
+    wide = values[0].shape[1]
+    for which, value in enumerate(values):
+        if isinstance(number, int):
+            at = number * size
+            cut = min(wide, main - at)
+            ref[:, which * main + at : which * main + at + cut] = value[:, :cut]
+            if cut < wide:
+                at = 2 * main + which * rest
+                ref[:, at : at + rest] = value[:, cut:]
+        else:
+            ref[:, pl.ds(pl.multiple_of(which * main + number * size, 128), wide)] = value
+
+
+def joined_segments(left, joined, units):
+    main = units // 128 * 128
+    return [
+        [(left, joined.at[:, pl.ds(0, main)])],
+        [(left, joined.at[:, pl.ds(main, 2 * units - main)])],
+    ]
+
+
+def joined_widths(units):
+    main = units // 128 * 128
+    return [main, 2 * units - main]
+
+
+def store_joined(ref, part, value, units):
+    main = units // 128 * 128
+    rest = units - main
+    if part == 0:
+        ref[:, 0, 0:main] = value
+    else:
+        ref[:, 1, 0:main] = value[:, :main]
+        ref[:, 0, main:units] = value[:, main : main + rest]
+        ref[:, 1, main:units] = value[:, main + rest :]
+
+
 def tile_lanes(number, wide):
     start = number * TILE
     return pl.ds(start if isinstance(start, int) else pl.multiple_of(start, TILE), wide)
@@ -917,7 +973,7 @@
 
 
 def first_forward(
-    tokens, cotangent, norm_conv, conv_in_t, kernel, conv_out, norm_mlp, gate_up_t, down, norm_attn, where
+    tokens, cotangent, conv_in_t, kernel, conv_out, gate_up_t, down, gains, lengths
 ):
     rows, width = tokens.shape
     channels = conv_out.shape[0]
@@ -936,7 +992,7 @@
         for at in range(4):
             part = slice(at * quarter, (at + 1) * quarter)
             values = r.tokens[part, :].astype(F32)
-            r.normed[part, :] = normalize(values, r.norm_conv[...])[0].astype(BF16)
+            r.normed[part, :] = normalize(values, r.gains[0:1, :])[0].astype(BF16)
         r.need(r.conv_in_t)
         for at in range(3):
             made = jnp.dot(r.normed[...], r.conv_in_t[at], preferred_element_type=F32)
@@ -977,14 +1033,14 @@
         r.flush(r.gated)
         waits = sum_and_gather(
             r, r.partial, r.gathered_one, r.norm_one_t,
-            lambda total, at, first: norm_rows(total, at, r.inputs_own, r.norm_mlp, r.one),
+            lambda total, at, first: norm_rows(total, at, r.inputs_own, r.gains[1:2, :], r.one),
         )
         next(waits)
         r.need(r.cotangent)
         for at, owner in enumerate(block_owners(index)):
             part = slice(at * quarter, (at + 1) * quarter)
             start = pl.multiple_of(owner * quarter, quarter)
-            live = r.column_positions[part, :] < r.length[0]
+            live = block_positions(at, quarter, (quarter, width), 0) < own_length(r)
             values = jnp.where(live, r.cotangent[pl.ds(start, quarter), :].astype(F32), 0.0)
             if at == 0:
                 r.incoming[...] = values
@@ -1012,7 +1068,7 @@
         exhaust(
             sum_and_gather(
                 r, r.partial, r.gathered, r.normed_attn_t,
-                lambda total, at, first: norm_rows(total, at, r.one, r.norm_attn, r.two),
+                lambda total, at, first: norm_rows(total, at, r.one, r.gains[2:3, :], r.two),
             )
         )
         r.flush(r.gathered, r.normed_attn_t, r.two)
@@ -1026,15 +1082,13 @@
         dict(
             tokens=Lazy(tokens),
             cotangent=Lazy(cotangent),
-            norm_conv=norm_conv.reshape(1, -1),
             conv_in_t=Lazy(conv_in_t),
             kernel=kernel,
             conv_out=Lazy(conv_out),
-            norm_mlp=norm_mlp.reshape(1, -1),
             gate_up_t=(gate_up_t, pl.ANY),
             down=(down, pl.ANY),
-            norm_attn=norm_attn.reshape(1, -1),
-            **where,
+            lengths=(lengths, pltpu.SMEM),
+            gains=gains,
         ),
         dict(
             gathered=Lazy((rows, width), BF16),
@@ -1094,8 +1148,8 @@
 
 
 def first_backward(
-    lefts, rights, grad_two_b, down, gate_up_t, gate, upward, one, norm_mlp, grad_two, conv_out,
-    conv_in_t, projected, rim, kernel, inputs, norm_conv, small, devices,
+    lefts, rights, grad_two_b, down, gate_up_t, gate, upward, one, grad_two, conv_out,
+    conv_in_t, projected, rim, kernel, inputs, gains, small, devices,
 ):
     rows, width = grad_two_b.shape
     units = down.shape[0]
@@ -1106,14 +1160,14 @@
     grad_three_t, normed_attn_t, grad_two_t, norm_one_t, normed_conv_t = lefts
     attended, grad_query, grad_kv, active, gated = rights
     columns, kv_columns = grad_query.shape[1], grad_kv.shape[1]
-    widths = [channels + columns + kv_columns, units, units, units, 4 * channels]
+    widths = [channels + columns + kv_columns, units, *joined_widths(units), 4 * channels]
     bits = []
     bit = 1
     while bit < devices:
         bits.append(bit)
         bit *= 2
     stages = 2 + len(bits)
-    size = TILE
+    size = TILE // 2
     tiles = [(at, min(size, units - at)) for at in range(0, units, size)]
 
     def body(r):
@@ -1126,14 +1180,17 @@
         def store(seg, column, value):
             if seg == 0:
                 at = (0, channels, channels + columns).index(column)
-                ref = (r.sum_attn_out, r.sum_query, r.sum_kv)[at]
-                ref[...] = value
-                r.flush(ref)
+                if at == 2:
+                    r.sum_kv[:, 0, :] = value[:, : kv_columns // 2]
+                    r.sum_kv[:, 1, :] = value[:, kv_columns // 2 :]
+                else:
+                    (r.sum_attn_out, r.sum_query)[at][...] = value
+                r.flush((r.sum_attn_out, r.sum_query, r.sum_kv)[at])
             elif seg == 1:
                 r.sum_down[...] = value
                 r.flush(r.sum_down)
             elif seg < 4:
-                r.sum_gate_up[:, seg - 2, :] = value
+                store_joined(r.sum_gate_up, seg - 2, value, units)
                 done.append(seg)
                 if len(done) == 2:
                     r.flush(r.sum_gate_up)
@@ -1154,10 +1211,9 @@
                     (r.normed_attn_t, r.grad_kv),
                 ],
                 [(r.grad_two_t, r.active)],
-                [(r.norm_one_t, r.grad_gate)],
-                [(r.norm_one_t, r.grad_up)],
-                [(r.grad_one_t, r.gated), (r.normed_conv_t, r.grad_projected)],
-            ],
+            ]
+            + joined_segments(r.norm_one_t, r.joined, units)
+            + [[(r.grad_one_t, r.gated), (r.normed_conv_t, r.grad_projected)]],
             [r.held0, r.held1, r.held2, r.held3, r.held4], r.r_send, r.r_recv, r.r_credit, store,
         )
         pump = Pump(rings, [0, 1])
@@ -1169,8 +1225,8 @@
             slot = number % 2
             pairs = [
                 (r.down.at[at : at + wide, :], r.down_tile.at[slot, 0:wide, :]),
-                (r.gate.at[number], r.gate_tile.at[slot]),
-                (r.upward.at[number], r.up_tile.at[slot]),
+                (r.gate.at[at // TILE, :, pl.ds(at % TILE, size)], r.gate_tile.at[slot]),
+                (r.upward.at[at // TILE, :, pl.ds(at % TILE, size)], r.up_tile.at[slot]),
             ]
             return [
                 pltpu.make_async_copy(a, b, r.h_sem.at[slot, k]) for k, (a, b) in enumerate(pairs)
@@ -1203,20 +1259,19 @@
                 grad = cross(r.gathered[...], r.down_tile[slot, 0:wide, :])
                 gates, ups = r.gate_tile[slot, :, 0:wide], r.up_tile[slot, :, 0:wide]
                 sigma = jax.nn.sigmoid(gates)
-                r.grad_gate[:, at : at + wide] = (
-                    grad * ups * sigma * (1.0 + gates * (1.0 - sigma))
-                ).astype(BF16)
-                r.grad_up[:, at : at + wide] = (grad * gates * sigma).astype(BF16)
+                grad_gate = (grad * ups * sigma * (1.0 + gates * (1.0 - sigma))).astype(BF16)
+                grad_up = (grad * gates * sigma).astype(BF16)
+                put_joined(r.joined, number, size, (grad_gate, grad_up), units)
                 if number % 3 == 2:
                     yield 1
             r.need(r.norm_one_t, r.one, r.grad_two)
             pump.ready += [2, 3]
             yield 2
-            yield from stream_product(r, [r.grad_gate, r.grad_up], r.gate_up_t, r.partial)
+            yield from stream_product(r, r.joined, r.gate_up_t, joined_parts(units), r.partial)
             yield from sum_and_gather(
                 r, r.partial, r.gathered, r.grad_one_t,
                 lambda total, at, first: back_rows(
-                    total, at, first, r.one, r.norm_mlp, r.grad_two, r.grad_one, r.gain_term
+                    total, at, first, r.one, r.gains[1:2, :], r.grad_two, r.grad_one, r.gain_term
                 ),
             )
             r.small_out[...] = r.small[...]
@@ -1296,10 +1351,24 @@
             yield from sum_and_gather(
                 r, r.partial, r.input_grad, None,
                 lambda total, at, first: back_rows(
-                    total, at, first, r.inputs, r.norm_conv, r.grad_one, None, r.gain_term
+                    total, at, first, r.inputs, r.gains[0:1, :], r.grad_one, None, r.gain_term
                 ),
             )
-            r.flush_blocks(r.input_grad, block_owners(index))
+            out_copies = []
+            small_rows = quarter // 2
+            for at in range(8):
+                start = pl.multiple_of(block_owners(index)[at // 2] * quarter + at % 2 * small_rows, 8)
+                if at >= 2:
+                    out_copies[at - 2].wait()
+                r.final[at % 2] = r.input_grad[at * small_rows : (at + 1) * small_rows, :].astype(F32)
+                out_copies.append(
+                    pltpu.make_async_copy(
+                        r.final.at[at % 2], r.result.at[pl.ds(start, small_rows), :], r.g_sem.at[at]
+                    )
+                )
+                out_copies[-1].start()
+            for copy in out_copies[-2:]:
+                copy.wait()
             r.small_out[0:1, :] = r.gain_term[...]
             row = lax.broadcasted_iota(jnp.int32, small.shape, 0)
             for stage in range(stages):
@@ -1348,18 +1417,17 @@
             gate_up_t=(gate_up_t, pl.ANY),
             gate=(gate, pl.ANY),
             upward=(upward, pl.ANY),
-            norm_mlp=norm_mlp.reshape(1, -1),
             conv_in_t=(conv_in_t, pl.ANY),
             kernel=kernel,
-            norm_conv=norm_conv.reshape(1, -1),
+            gains=gains,
             small=small,
         ),
         dict(
-            input_grad=Lazy((rows, width), BF16),
+            result=((rows, width), F32, pl.ANY),
             small_out=Lazy(small.shape, F32),
             sum_attn_out=Lazy((block, channels), F32),
             sum_query=Lazy((block, columns), F32),
-            sum_kv=Lazy((block, kv_columns), F32),
+            sum_kv=Lazy((block, 2, kv_columns // 2), F32),
             sum_down=Lazy((block, units), F32),
             sum_gate_up=Lazy((block, 2, units), F32),
             sum_conv_out=Lazy((block, channels), F32),
@@ -1370,8 +1438,10 @@
             partial=pltpu.VMEM((rows, width), BF16),
             grad_one_t=pltpu.VMEM((width, rows), BF16),
             grad_one=pltpu.VMEM((quarter, width), F32),
-            grad_gate=pltpu.VMEM((rows, units), BF16),
-            grad_up=pltpu.VMEM((rows, units), BF16),
+            joined=pltpu.VMEM((rows, 2 * units), BF16),
+            input_grad=pltpu.VMEM((rows, width), BF16),
+            final=pltpu.VMEM((2, quarter // 2, width), F32),
+            g_sem=pltpu.SemaphoreType.DMA((8,)),
             grad_projected=pltpu.VMEM((rows, 3 * channels), BF16),
             grad_gated=pltpu.VMEM((rows, channels), F32),
             mixed=pltpu.VMEM((rows + 8, channels), F32),
@@ -1390,7 +1460,7 @@
             slots=pltpu.VMEM((stages,) + small.shape, F32),
             s_send=pltpu.SemaphoreType.DMA((stages,)),
             s_recv=pltpu.SemaphoreType.DMA((stages,)),
-            **stream_scratch(2, units, 128),
+            **stream_scratch(2 * units, 128),
             **exchange_scratch(rows, width),
             **ring_scratch(devices, sides, block, widths),
         ),
@@ -1428,17 +1498,16 @@
     device = lax.axis_index("dp")
     devices = lax.axis_size("dp")
     index = lax.axis_index("tensor")
-    sequence = device // SPAN
     place_index = device % SPAN
-    length = lengths[sequence]
     offsets = jnp.concatenate(
         [o * quarter + jnp.arange(quarter, dtype=jnp.int32) for o in block_owners(index)]
     )
     positions = place_index * row_count + offsets
+    gains = jnp.stack([norm_conv, norm_mlp_one, norm_attn, norm_mlp_two])
+    head_gains = jnp.stack([query_gain, key_gain], axis=1)
     frequency = THETA ** (-2.0 * jnp.arange(HEAD // 2, dtype=jnp.float32) / HEAD)
     angles = frequency[:, None] * positions.astype(jnp.float32)[None, :]
     tables = (jnp.cos(angles), jnp.sin(angles))
-    where = position_inputs(positions, length)
     gate_up_one_t = jnp.transpose(gate_up_one, (1, 2, 0))
     gate_up_two_t = jnp.transpose(gate_up_two, (1, 2, 0))
     conv_in_t = jnp.transpose(conv_in, (1, 0, 2))
@@ -1462,22 +1531,11 @@
         grad_b_t,
         incoming,
     ) = first_forward(
-        tokens,
-        cotangent,
-        norm_conv,
-        conv_in_t,
-        conv_kernel,
-        conv_out,
-        norm_mlp_one,
-        gate_up_one_t,
-        down_one,
-        norm_attn,
-        where,
+        tokens, cotangent, conv_in_t, conv_kernel, conv_out, gate_up_one_t, down_one, gains, lengths
     )
     (
         active_two,
-        grad_gate_two,
-        grad_up_two,
+        joined_two,
         norm_two_t,
         three_own,
         *kept,
@@ -1488,13 +1546,12 @@
         normed_attn_b,
         query_weight,
         kv_flat,
-        query_gain,
-        key_gain,
+        head_gains,
         attn_out,
         two_own,
-        norm_mlp_two,
         tables,
-        where,
+        gains,
+        lengths,
         gate_up_two_t,
         down_two,
         grad_b,
@@ -1507,10 +1564,7 @@
         grad_two_b,
         grad_two_t,
         grad_two,
-        grad_norm_mlp_two,
-        grad_norm_attn,
-        part_query_gain,
-        part_key_gain,
+        small,
         sum_down_two,
         sum_gate_up_two,
         output,
@@ -1518,38 +1572,23 @@
         grad_b_t,
         norm_two_t,
         active_two,
-        grad_gate_two,
-        grad_up_two,
+        joined_two,
         gate_up_two_t,
         down_two,
         three_own,
-        norm_mlp_two,
         incoming,
         kept,
         attn_out,
         query_weight,
         kv_flat,
-        query_gain,
-        key_gain,
+        head_gains,
         two_own,
-        norm_attn,
         tables,
-        where,
+        gains,
+        lengths,
         devices,
     )
 
-    small = jnp.concatenate(
-        [
-            jnp.zeros((2, width), F32),
-            grad_norm_attn,
-            grad_norm_mlp_two,
-            jnp.pad(
-                jnp.concatenate([part_query_gain[:, 0], part_key_gain[:, 0]]), (0, width - 2 * HEAD)
-            ).reshape(1, width),
-            jnp.zeros((KW, width), F32),
-        ],
-        axis=0,
-    )
     (
         grad_inputs,
         small,
@@ -1569,7 +1608,6 @@
         gate_one,
         up_one,
         one_own,
-        norm_mlp_one,
         grad_two,
         conv_out,
         conv_in_t,
@@ -1577,12 +1615,10 @@
         rim,
         conv_kernel,
         inputs_own,
-        norm_conv,
+        gains,
         small,
         devices,
     )
-    grad_inputs = grad_inputs.astype(F32)
-
     out_rows = width // devices
     return (
         output,
@@ -1596,7 +1632,7 @@
         sum_down_one.T,
         small[2],
         sum_query,
-        sum_kv.reshape(out_rows, 2, local_kv * HEAD),
+        sum_kv,
         small[4, :HEAD],
         small[4, HEAD : 2 * HEAD],
         sum_attn_out.T,

time: 586 us -> 570 us (0.973)
  Pallas kernels: 550 us -> 537 us
    pallas_call x4, Pallas kernels: 550 us -> 537 us  [run_kernel(): pl.pallas_call(whole, in_specs=specs, out_specs=out_specs, out_shape=shap...]
    reshape x8 -> x0, local copies, waits for them, and re-layouts: 6.68 us -> none  [the longest x1 1.29 us: first_forward(): norm_conv.reshape(1, -1)]
    unnamed x40 -> x34, local copies, waits for them, and re-layouts: 12.6 us -> 17.7 us
where the time goes in v5:
time: 570 us; the launch traced here: 566 us
  Pallas kernels  537 us (94%)
  local copies, waits for them, and re-layouts  25.5 us (4%)
    pallas_call x4, Pallas kernels, run_kernel(): pl.pallas_call(whole, in_specs=specs, out_specs=out_specs, out_shape=shap...  537 us
    unnamed x34, local copies, waits for them, and re-layouts  17.7 us

profile of v5, /device:TPU:0, one launch (start us, length us, event | category | flops | bytes accessed | tf_op | source)
XLA Modules:
  0.0 566.2 jit_solution(823847247723297861)
XLA Ops:
  4.9 0.7 copy.39.refs_3_.refs_18_
  5.6 1.0 multiply_sine_fusion
  6.5 2.1 copy.43
  8.6 64.4 %shard_map.322 = (bf16[512,1536]{1,0:T(8,128)(2,1)}, bf16[1536,512]{1,0:T(8,128)(2,1)}, f32[128,1536]{1,0:T(8,128)}, f32[128,1536]{1,0:T(8,128)}, f32[128,1536]{...) custom-call(bf16[512,1536]{1,0:T(8,128)(2,1)} %refs_0_.1, ...), custom_call_target="tpu_custom_call" | custom-call | flops 8153726976 | bytes 23816456 | tf_op jit(solution)/shard_map/pallas_call | solution.py:130
  73.1 46.6 %shard_map.323 = (bf16[512,1728]{1,0:T(8,128)(2,1)}, bf16[512,3456]{1,0:T(8,128)(2,1)}, bf16[1536,512]{1,0:T(8,128)(2,1)}, f32[128,1536]{1,0:T(8,128)}, f32[384,...) custom-call(bf16[512,1536]{1,0:T(8,128)(2,1)} %get-tuple-element.66., ...), custom_call_target="tpu_custom_call" | custom-call | flops 6442450944 | bytes 23159304 | tf_op jit(solution)/shard_map/pallas_call | solution.py:130
  119.7 189.2 %shard_map.324 = (bf16[1536,512]{1,0:T(8,128)(2,1)}, bf16[512,384]{1,0:T(8,128)(2,1)}, bf16[512,256]{1,0:T(8,128)(2,1)}, bf16[512,1536]{1,0:T(8,128)(2,1)}, bf16...) custom-call(bf16[1536,512]{1,0:T(8,128)(2,1)} %get-tuple-element.65., ...), custom_call_target="tpu_custom_call" | custom-call | flops 27179089920 | bytes 33329672 | tf_op jit(solution)/shard_map/pallas_call | solution.py:130
  309.0 237.1 %shard_map.325 = (f32[512,1536]{1,0:T(8,128)}, f32[8,1536]{1,0:T(8,128)}, f32[192,384]{1,0:T(8,128)}, f32[192,384]{1,0:T(8,128)}, f32[192,2,128]{2,1,0:T(2,128)}...) custom-call(bf16[1536,512]{1,0:T(8,128)(2,1)} %get-tuple-element.82.refs_0_, ...), custom_call_target="tpu_custom_call" | custom-call | flops 36540776448 | bytes 46487808 | tf_op jit(solution)/shard_map/pallas_call | solution.py:130
  546.1 1.3 slice_bitcast_fusion
  547.4 1.3 slice.22
  548.7 1.6 slice_reduce_fusion
  550.3 1.1 copy.55
  551.5 1.3 copy-done
  552.8 1.7 copy.56
  554.6 0.9 copy.57
  555.5 0.8 copy-done.9
  556.3 0.7 copy.58
  557.0 1.5 copy.59
  558.6 0.8 copy-done.5
  559.3 1.1 copy.60
  560.4 0.7 copy.61
  561.8 0.7 copy.63
  562.5 1.5 copy.64
  564.1 0.8 copy-done.4
  564.9 1.1 copy.65
  (29 shorter events, 5.0 us)
Async XLA Ops:
  308.9 241.4 %copy-start.3 = (bf16[512,1536]{1,0:T(8,128)(2,1)S(1)}, bf16[512,1536]{1,0:T(8,128)(2,1)}, u32[]{:S(2)}) copy-start(bf16[512,1536]{1,0:T(8,128)(2,1)} %get-tuple-element.142) | copy-start | bytes 4718596
  550.3 2.5 copy-start
  552.8 1.8 copy-start.6
  552.8 4.2 copy-start.2
  554.6 1.7 copy-start.9
  557.0 2.3 copy-start.5
  557.0 3.4 copy-start.8
  559.3 1.8 copy-start.10
  559.3 2.5 copy-start.7
  559.3 3.2 copy-start.1
  562.5 2.3 copy-start.4

commit v6 on v5

--- a/solution.py
+++ b/solution.py
@@ -1470,6 +1470,36 @@
     )
 
 
+def assemble(arrays):
+    count = len(arrays)
+
+    def body(*refs):
+        held, arrive, leave = refs[2 * count : 3 * count], refs[-2], refs[-1]
+        first = [
+            pltpu.make_async_copy(refs[at], held[at], arrive.at[at]) for at in range(count)
+        ]
+        second = [
+            pltpu.make_async_copy(held[at], refs[count + at], leave.at[at]) for at in range(count)
+        ]
+        for copy in first:
+            copy.start()
+        for one, two in zip(first, second):
+            one.wait()
+            two.start()
+        for copy in second:
+            copy.wait()
+
+    return pl.pallas_call(
+        body,
+        in_specs=[pl.BlockSpec(memory_space=pl.ANY)] * count,
+        out_specs=[pl.BlockSpec(memory_space=pl.ANY)] * count,
+        out_shape=[jax.ShapeDtypeStruct(a.shape, a.dtype) for a in arrays],
+        scratch_shapes=[pltpu.VMEM(a.shape, a.dtype) for a in arrays]
+        + [pltpu.SemaphoreType.DMA((count,))] * 2,
+        compiler_params=pltpu.CompilerParams(vmem_limit_bytes=60 * 2**20),
+    )(*arrays)
+
+
 def local(
     tokens,
     lengths,
@@ -1503,7 +1533,7 @@
         [o * quarter + jnp.arange(quarter, dtype=jnp.int32) for o in block_owners(index)]
     )
     positions = place_index * row_count + offsets
-    gains = jnp.stack([norm_conv, norm_mlp_one, norm_attn, norm_mlp_two])
+    gains = jnp.concatenate([norm_conv, norm_mlp_one, norm_attn, norm_mlp_two]).reshape(4, width)
     head_gains = jnp.stack([query_gain, key_gain], axis=1)
     frequency = THETA ** (-2.0 * jnp.arange(HEAD // 2, dtype=jnp.float32) / HEAD)
     angles = frequency[:, None] * positions.astype(jnp.float32)[None, :]
@@ -1620,6 +1650,16 @@
         devices,
     )
     out_rows = width // devices
+    (
+        output, grad_inputs, sum_conv_in, sum_conv_out, sum_gate_up_one, sum_down_one, sum_query, sum_kv,
+        sum_attn_out, sum_gate_up_two, sum_down_two,
+    ) = assemble(
+        [
+            output, grad_inputs, jnp.reshape(sum_conv_in, (-1, sum_conv_in.shape[2])), sum_conv_out,
+            sum_gate_up_one, sum_down_one, sum_query, sum_kv, sum_attn_out, sum_gate_up_two, sum_down_two,
+        ]
+    )
+    sum_conv_in = sum_conv_in.reshape(3, -1, sum_conv_in.shape[1])
     return (
         output,
         grad_inputs,

time: 570 us -> 560 us (0.982)
  local copies, waits for them, and re-layouts: 25.5 us -> 5.29 us
  Pallas kernels: 537 us -> 548 us
    unnamed x34 -> x3, local copies, waits for them, and re-layouts: 17.7 us -> 2.12 us
    pallas_call x0 -> x1, Pallas kernels: none -> 10.6 us  [assemble(): pl.pallas_call(body, in_specs=[pl.BlockSpec(memory_space=pl.ANY)] * count...]
where the time goes in v6:
time: 560 us; the launch traced here: 557 us
  Pallas kernels  548 us (98%)
    pallas_call x4, Pallas kernels, run_kernel(): pl.pallas_call(whole, in_specs=specs, out_specs=out_specs, out_shape=shap...  537 us

profile of v6, /device:TPU:0, one launch (start us, length us, event | category | flops | bytes accessed | tf_op | source)
XLA Modules:
  0.0 556.6 jit_solution(11550212723907209562)
XLA Ops:
  0.7 0.7 pad_maximum_fusion.1
  1.4 0.8 pad_maximum_fusion
  2.2 0.6 reshape.82.refs_8_.refs_12_.refs_23_
  2.8 0.7 copy.39.refs_3_.refs_18_
  3.5 1.0 multiply_sine_fusion
  4.5 2.1 copy.43
  6.6 64.4 %shard_map.322 = (bf16[512,1536]{1,0:T(8,128)(2,1)}, bf16[1536,512]{1,0:T(8,128)(2,1)}, f32[128,1536]{1,0:T(8,128)}, f32[128,1536]{1,0:T(8,128)}, f32[128,1536]{...) custom-call(bf16[512,1536]{1,0:T(8,128)(2,1)} %refs_0_.1, ...), custom_call_target="tpu_custom_call" | custom-call | flops 8153726976 | bytes 23816456 | tf_op jit(solution)/shard_map/pallas_call | solution.py:130
  71.0 46.6 %shard_map.323 = (bf16[512,1728]{1,0:T(8,128)(2,1)}, bf16[512,3456]{1,0:T(8,128)(2,1)}, bf16[1536,512]{1,0:T(8,128)(2,1)}, f32[128,1536]{1,0:T(8,128)}, f32[384,...) custom-call(bf16[512,1536]{1,0:T(8,128)(2,1)} %get-tuple-element.77., ...), custom_call_target="tpu_custom_call" | custom-call | flops 6442450944 | bytes 23159304 | tf_op jit(solution)/shard_map/pallas_call | solution.py:130
  117.6 189.3 %shard_map.324 = (bf16[1536,512]{1,0:T(8,128)(2,1)}, bf16[512,384]{1,0:T(8,128)(2,1)}, bf16[512,256]{1,0:T(8,128)(2,1)}, bf16[512,1536]{1,0:T(8,128)(2,1)}, bf16...) custom-call(bf16[1536,512]{1,0:T(8,128)(2,1)} %get-tuple-element.76., ...), custom_call_target="tpu_custom_call" | custom-call | flops 27179089920 | bytes 33329672 | tf_op jit(solution)/shard_map/pallas_call | solution.py:130
  306.9 237.0 %shard_map.325 = (f32[512,1536]{1,0:T(8,128)}, f32[8,1536]{1,0:T(8,128)}, f32[192,384]{1,0:T(8,128)}, f32[192,384]{1,0:T(8,128)}, f32[192,2,128]{2,1,0:T(2,128)}...) custom-call(bf16[1536,512]{1,0:T(8,128)(2,1)} %get-tuple-element.93.refs_0_, ...), custom_call_target="tpu_custom_call" | custom-call | flops 36540776448 | bytes 46487808 | tf_op jit(solution)/shard_map/pallas_call | solution.py:130
  543.9 0.0 copy-start
  543.9 10.6 %shard_map.326 = (bf16[512,1536]{1,0:T(8,128)(2,1)}, f32[512,1536]{1,0:T(8,128)}, f32[576,384]{1,0:T(8,128)}, f32[192,384]{1,0:T(8,128)}, f32[192,2,1728]{2,1,0:...) custom-call(bf16[512,1536]{1,0:T(8,128)(2,1)} %get-tuple-element.92., ...), custom_call_target="tpu_custom_call" | custom-call | tf_op jit(solution)/shard_map/pallas_call | solution.py:1492
  554.5 0.0 copy-done
  554.5 0.6 slice_bitcast_fusion
  555.1 0.6 slice.22
  555.7 0.7 slice_reduce_fusion
  (4 shorter events, 0.0 us)
Async XLA Ops:
  543.9 10.6 %copy-start = (f32[8,1536]{1,0:T(8,128)S(1)}, f32[8,1536]{1,0:T(8,128)}, u32[]{:S(2)}) copy-start(f32[8,1536]{1,0:T(8,128)} %get-tuple-element.124) | copy-start | bytes 147460

commit v7 on v6

--- a/solution.py
+++ b/solution.py
@@ -721,7 +721,6 @@
                 r.grad_own[:, at] = value
 
             part(r.own[...], write_own, True)
-            yield 1
 
             @pl.loop(1, place + 1)
             def _(distance):
@@ -731,7 +730,7 @@
                 part(r.near[distance - 1], write_far, False)
                 pass_back(distance).start()
 
-            yield 2
+            yield 1
             r.need(r.cosine, r.sine, r.query_raw, r.key_raw, r.query_weight, r.kv_weight, r.two)
             cosine, sine = r.cosine[...], r.sine[...]
             terms = None

time: 560 us -> 560 us (level)
  no operation moved by 1% of the time
where the time goes in v7:
time: 560 us; the launch traced here: 556 us
  Pallas kernels  548 us (98%)
    pallas_call x4, Pallas kernels, run_kernel(): pl.pallas_call(whole, in_specs=specs, out_specs=out_specs, out_shape=shap...  537 us

profile of v7, /device:TPU:0, one launch (start us, length us, event | category | flops | bytes accessed | tf_op | source)
XLA Modules:
  0.0 556.5 jit_solution(6347899071854282493)
XLA Ops:
  0.7 0.7 pad_maximum_fusion.1
  1.4 0.8 pad_maximum_fusion
  2.2 0.6 reshape.82.refs_8_.refs_12_.refs_23_
  2.8 0.7 copy.39.refs_3_.refs_18_
  3.5 1.0 multiply_sine_fusion
  4.5 2.1 copy.43
  6.6 64.4 %shard_map.322 = (bf16[512,1536]{1,0:T(8,128)(2,1)}, bf16[1536,512]{1,0:T(8,128)(2,1)}, f32[128,1536]{1,0:T(8,128)}, f32[128,1536]{1,0:T(8,128)}, f32[128,1536]{...) custom-call(bf16[512,1536]{1,0:T(8,128)(2,1)} %refs_0_.1, ...), custom_call_target="tpu_custom_call" | custom-call | flops 8153726976 | bytes 23816456 | tf_op jit(solution)/shard_map/pallas_call | solution.py:130
  71.0 46.6 %shard_map.323 = (bf16[512,1728]{1,0:T(8,128)(2,1)}, bf16[512,3456]{1,0:T(8,128)(2,1)}, bf16[1536,512]{1,0:T(8,128)(2,1)}, f32[128,1536]{1,0:T(8,128)}, f32[384,...) custom-call(bf16[512,1536]{1,0:T(8,128)(2,1)} %get-tuple-element.77., ...), custom_call_target="tpu_custom_call" | custom-call | flops 6442450944 | bytes 23159304 | tf_op jit(solution)/shard_map/pallas_call | solution.py:130
  117.6 189.2 %shard_map.324 = (bf16[1536,512]{1,0:T(8,128)(2,1)}, bf16[512,384]{1,0:T(8,128)(2,1)}, bf16[512,256]{1,0:T(8,128)(2,1)}, bf16[512,1536]{1,0:T(8,128)(2,1)}, bf16...) custom-call(bf16[1536,512]{1,0:T(8,128)(2,1)} %get-tuple-element.76., ...), custom_call_target="tpu_custom_call" | custom-call | flops 27179089920 | bytes 33329672 | tf_op jit(solution)/shard_map/pallas_call | solution.py:130
  306.9 236.9 %shard_map.325 = (f32[512,1536]{1,0:T(8,128)}, f32[8,1536]{1,0:T(8,128)}, f32[192,384]{1,0:T(8,128)}, f32[192,384]{1,0:T(8,128)}, f32[192,2,128]{2,1,0:T(2,128)}...) custom-call(bf16[1536,512]{1,0:T(8,128)(2,1)} %get-tuple-element.93.refs_0_, ...), custom_call_target="tpu_custom_call" | custom-call | flops 36540776448 | bytes 46487808 | tf_op jit(solution)/shard_map/pallas_call | solution.py:130
  543.8 0.0 copy-start
  543.8 10.6 %shard_map.326 = (bf16[512,1536]{1,0:T(8,128)(2,1)}, f32[512,1536]{1,0:T(8,128)}, f32[576,384]{1,0:T(8,128)}, f32[192,384]{1,0:T(8,128)}, f32[192,2,1728]{2,1,0:...) custom-call(bf16[512,1536]{1,0:T(8,128)(2,1)} %get-tuple-element.92., ...), custom_call_target="tpu_custom_call" | custom-call | tf_op jit(solution)/shard_map/pallas_call | solution.py:1491
  554.3 0.0 copy-done
  554.4 0.6 slice_bitcast_fusion
  554.9 0.6 slice.22
  555.5 0.7 slice_reduce_fusion
  (4 shorter events, 0.0 us)
Async XLA Ops:
  543.8 10.6 %copy-start = (f32[8,1536]{1,0:T(8,128)S(1)}, f32[8,1536]{1,0:T(8,128)}, u32[]{:S(2)}) copy-start(f32[8,1536]{1,0:T(8,128)} %get-tuple-element.124) | copy-start | bytes 147460
